TPU v7x, 32 devices: a whole 2x2x4 slice. The times are simulated.
32 devices in a mesh: dp: 2 (over core), mem: 16 (over z, y, x).
Axes of the slice: x: 2, y: 2, z: 4, core: 2. Of those that a mesh axis runs over, the one named last changes fastest.
Arguments:
- tokens: bfloat16 [4096, 1024], P(('dp', 'mem')), may hold values from -6 to 6
- attn_gain: float32 [1024], replicated, may hold values from 0.5 to 1.5
- qkv_weight: bfloat16 [1024, 3072], replicated, may hold values from -0.1875 to 0.1875
- out_weight: bfloat16 [1024, 1024], replicated, may hold values from -0.75 to 0.75
- bias_table: float32 [8, 32], replicated, may hold values from -4 to 4
- gate_logit: float32 [8], replicated, may hold values from -1.5 to 1.5
- ffn_gain: float32 [1024], replicated, may hold values from 0.5 to 1.5
- up_weight: bfloat16 [1024, 4096], replicated, may hold values from -0.1875 to 0.1875
- down_weight: bfloat16 [1024, 4096], replicated, may hold values from -0.09375 to 0.09375
- memory_keys: bfloat16 [65536, 1024], P('mem'), may hold values from -6 to 6
- memory_values: bfloat16 [65536, 1024], P('mem'), may hold values from -6 to 6
- book_lengths: int32 [2, 3], P('dp'), may hold values from 1 to 2046, as said below
- slot_shard: int32 [4096, 8, 32, 1], P(('dp', 'mem')), may hold values from 0 to 15; in each aligned block of 32768 rows (0 to 32767, 32768 to 65535, ..., all dimensions but the last counted through in order) at most 3072 rows name the same one
- slot_index: int32 [4096, 8, 32], P(('dp', 'mem')), may hold values from 0 to 4095
- slot_live: int32 [4096, 8, 32], P(('dp', 'mem')), may hold values from 0 to 1, as said below
- cotangent: bfloat16 [4096, 1024], P(('dp', 'mem')), may hold values from -6 to 6
Outputs:
- block_out: bfloat16 [4096, 1024], P(('dp', 'mem'))
- tokens_grad: float32 [4096, 1024], P(('dp', 'mem'))
- qkv_grad: float32 [1024, 3072], P('mem')
- out_grad: float32 [1024, 1024], P('mem')
- up_grad: float32 [1024, 4096], P('mem')
- down_grad: float32 [1024, 4096], P('mem')
- attn_gain_grad: float32 [1024], replicated
- ffn_gain_grad: float32 [1024], replicated
- bias_grad: float32 [8, 32], replicated
- gate_grad: float32 [8], replicated
Inputs may be any that keep to these rules, and one draw needn't show every extreme that they name: `book_lengths`: the 3 books of a group fill its 2048 tokens; the middle one begins in the first 128 tokens and ends in the last 128; in some group the first and last books are one token long. `slot_shard`: among the 32768 entries of one device's tokens no device of mem is named more than 3072 times, and some device is named exactly 3072 times. `slot_live`: some token heads have no live entry.
All inputs are finite; a program needn't handle non-finite values.
Results may differ from a plain program's by a relative error of at most 0.014.
Values may be sent and summed in bfloat16 or wider, within the bound.
A program may use at most 256 MiB of HBM per device.

v0:
```python
import math

import jax
import jax.numpy as jnp
from jax import lax
from jax.sharding import PartitionSpec as P

W = 512


eps_norm = 1e-06
bucket_edges = tuple((math.ceil(16 * 8 ** (edge_step / 16)) for edge_step in range(1, 16)))
masked_score = -1e30
dead_score = -10000.0
contract_rows = (((0,), (0,)), ((), ()))
contract_cols = (((1,), (1,)), ((), ()))


def passed_along(value, axis, by):
    size = lax.axis_size(axis)
    pairs = [(i, i + by) for i in range(size) if 0 <= i + by < size]
    return lax.ppermute(value, axis, pairs)


def bucket_of(offset):
    past_edges = sum(((offset >= edge_pos).astype(jnp.int32) for edge_pos in bucket_edges))
    return jnp.where(offset < 16, offset, 16 + past_edges)


def normed(values, gain_vec):
    return (
        values * lax.rsqrt(jnp.mean(values * values, axis=-1, keepdims=True) + eps_norm) * gain_vec
    )


def gelu_exact(values):
    return jax.nn.gelu(values, approximate=False)


def book_of(positions, lengths):
    book_ends = jnp.cumsum(lengths, dtype=jnp.int32)
    return jnp.sum((positions[..., None] >= book_ends).astype(jnp.int32), axis=-1)


def place_requests(slot_shard, slot_index, groups, capacity, heads):
    targets = slot_shard.reshape(-1)
    head_ids = jnp.broadcast_to(jnp.arange(heads, dtype=jnp.int32)[None, :, None], slot_index.shape)
    wanted = (slot_index * heads + head_ids).reshape(-1)
    total = targets.shape[0]
    block = math.gcd(total, 128)
    blocks = total // block
    owner_hot = (
        targets.reshape(blocks, block)[:, :, None]
        == jnp.arange(groups, dtype=jnp.int32)[None, None, :]
    )
    hot_low = owner_hot.astype(jnp.bfloat16)
    earlier = (
        jnp.arange(block, dtype=jnp.int32)[:, None] > jnp.arange(block, dtype=jnp.int32)[None, :]
    ).astype(jnp.bfloat16)
    inside_count = jnp.einsum("ij,bjg->big", earlier, hot_low, preferred_element_type=jnp.float32)
    block_totals = jnp.sum(owner_hot.astype(jnp.float32), axis=1)
    before_blocks = jnp.cumsum(block_totals, axis=0) - block_totals
    counts = inside_count + before_blocks[:, None, :]
    within = jnp.sum(jnp.where(owner_hot, counts, 0.0), axis=-1).reshape(-1).astype(jnp.int32)
    places = targets * capacity + within
    requests = jnp.zeros((groups * capacity,), jnp.int32).at[places].set(wanted)
    return (requests.reshape(groups, capacity), places)


def lookup(incoming, memory_keys, memory_values, heads):
    key_table = memory_keys.reshape(-1, memory_keys.shape[1] // heads)
    value_table = memory_values.reshape(-1, memory_values.shape[1] // heads)
    flat_ids = incoming.reshape(-1)
    found_rows = jnp.stack(
        [jnp.take(key_table, flat_ids, axis=0), jnp.take(value_table, flat_ids, axis=0)], axis=1
    )
    return found_rows.reshape(incoming.shape[0], incoming.shape[1], 2, key_table.shape[1])


def unpack(replies, places, entry_shape):
    flat_rows = replies.reshape(-1, 2, replies.shape[3])
    picked = jnp.take(flat_rows, places, axis=0)
    return picked.reshape(entry_shape + (2, replies.shape[3]))


def fetch_rows(requests, places, memory_keys, memory_values, heads, entry_shape):
    replies = lax.all_to_all(
        lookup(
            lax.all_to_all(requests, "mem", split_axis=0, concat_axis=0, tiled=True),
            memory_keys,
            memory_values,
            heads,
        ),
        "mem",
        split_axis=0,
        concat_axis=0,
        tiled=True,
    )
    return unpack(replies, places, entry_shape)


def memory_probs(queries, fetched_keys, live_mask, score_scale):
    raw_scores = (
        jnp.einsum("qhd,qhkd->qhk", queries, fetched_keys, preferred_element_type=jnp.float32)
        * score_scale
    )
    row_max = jnp.max(jnp.where(live_mask, raw_scores, dead_score), axis=-1, keepdims=True)
    exp_scores = jnp.exp(jnp.where(live_mask, raw_scores - row_max, dead_score))
    sums_mem = jnp.sum(exp_scores, axis=-1, keepdims=True)
    return exp_scores / jnp.where(sums_mem > 0, sums_mem, 1.0)


def on_device(
    tokens,
    attn_gain,
    qkv_weight,
    out_weight,
    bias_table,
    gate_logit,
    ffn_gain,
    up_weight,
    down_weight,
    memory_keys,
    memory_values,
    book_lengths,
    slot_shard,
    slot_index,
    slot_live,
    cotangent,
):
    rows, width = tokens.shape
    heads, buckets = bias_table.shape
    head_dim = width // heads
    top_count = slot_index.shape[2]
    hidden = up_weight.shape[1]
    groups = lax.axis_size("mem")
    capacity = max(2, 3 * rows * heads * top_count // (2 * groups))
    score_scale = 1.0 / math.sqrt(head_dim)
    sent_rows = min(W, rows)
    repeats = W // sent_rows
    first_pos = lax.axis_index("mem") * rows
    query_pos = first_pos + jnp.arange(rows, dtype=jnp.int32)
    key_pos = first_pos - W + jnp.arange(W + rows, dtype=jnp.int32)
    lengths = book_lengths[0]
    query_book = book_of(query_pos, lengths)
    key_book = jnp.where(key_pos >= 0, book_of(key_pos, lengths), -1)
    offset = (
        jnp.arange(rows, dtype=jnp.int32)[:, None]
        + W
        - jnp.arange(W + rows, dtype=jnp.int32)[None, :]
    )
    allowed = (offset >= 0) & (offset < W) & (query_book[:, None] == key_book[None, :])
    bucket = bucket_of(jnp.maximum(offset, 0))
    one_hot_f = (bucket[:, :, None] == jnp.arange(buckets, dtype=jnp.int32)).astype(jnp.float32)
    score_bias = jnp.einsum("qkb,hb->hqk", one_hot_f, bias_table, precision=lax.Precision.HIGHEST)
    tokens_f = tokens.astype(jnp.float32)
    normed_f, norm_in_back = jax.vjp(normed, tokens_f, attn_gain)
    normed_in = normed_f.astype(jnp.bfloat16)
    projected = jnp.dot(normed_in, qkv_weight, preferred_element_type=jnp.float32).astype(
        jnp.bfloat16
    )
    queries = projected[:, :width].reshape(rows, heads, head_dim)
    keys_own = projected[:, width : 2 * width].reshape(rows, heads, head_dim)
    values_own = projected[:, 2 * width :].reshape(rows, heads, head_dim)
    tail_rows = jnp.stack([keys_own, values_own])
    received = []
    for distance in range(repeats, 0, -1):
        received.append(passed_along(tail_rows, "mem", distance))
    halo_rows = jnp.concatenate(received, axis=1)
    keys_all = jnp.concatenate([halo_rows[0], keys_own], axis=0)
    values_all = jnp.concatenate([halo_rows[1], values_own], axis=0)

    def local_scores():
        raw_scores = (
            jnp.einsum("qhd,khd->hqk", queries, keys_all, preferred_element_type=jnp.float32)
            * score_scale
            + score_bias
        )
        return jnp.where(allowed[None], raw_scores, masked_score)

    scores = local_scores()
    row_max = jnp.max(scores, axis=-1, keepdims=True)
    exp_scores = jnp.exp(scores - row_max)
    sums_local = jnp.sum(exp_scores, axis=-1, keepdims=True)
    local_probs = exp_scores / sums_local
    log_total = row_max + jnp.log(sums_local)
    local_out = jnp.einsum(
        "hqk,khd->qhd",
        local_probs.astype(jnp.bfloat16),
        values_all,
        preferred_element_type=jnp.float32,
    )
    requests, places = place_requests(slot_shard, slot_index, groups, capacity, heads)
    entry_shape = (rows, heads, top_count)
    fetched = fetch_rows(requests, places, memory_keys, memory_values, heads, entry_shape)
    live_mask = slot_live > 0
    mem_probs = memory_probs(queries, fetched[..., 0, :], live_mask, score_scale)
    memory_out = jnp.einsum(
        "qhk,qhkd->qhd",
        mem_probs.astype(jnp.bfloat16),
        fetched[..., 1, :],
        preferred_element_type=jnp.float32,
    )
    gate_share = jax.nn.sigmoid(gate_logit)[:, None]
    mixed_heads = (
        (gate_share * memory_out + (1.0 - gate_share) * local_out)
        .reshape(rows, width)
        .astype(jnp.bfloat16)
    )
    residual = tokens_f + jnp.dot(mixed_heads, out_weight, preferred_element_type=jnp.float32)
    normed_mid_f, norm_mid_back = jax.vjp(normed, residual, ffn_gain)
    normed_mid = normed_mid_f.astype(jnp.bfloat16)
    up_proj = jnp.dot(normed_mid, up_weight, preferred_element_type=jnp.float32)
    activated_f, gelu_back = jax.vjp(gelu_exact, up_proj)
    activated = activated_f.astype(jnp.bfloat16)
    ffn_branch = lax.dot_general(
        activated, down_weight, contract_cols, preferred_element_type=jnp.float32
    )
    block_out = (residual + ffn_branch).astype(jnp.bfloat16)
    d_act = jnp.dot(cotangent, down_weight, preferred_element_type=jnp.float32)
    d_up = gelu_back(d_act)[0].astype(jnp.bfloat16)
    d_mid = lax.dot_general(d_up, up_weight, contract_cols, preferred_element_type=jnp.float32)
    d_resid_part, ffn_gain_part = norm_mid_back(d_mid)
    d_residual = cotangent.astype(jnp.float32) + d_resid_part
    d_branch = d_residual.astype(jnp.bfloat16)
    d_mixed = lax.dot_general(
        d_branch, out_weight, contract_cols, preferred_element_type=jnp.float32
    ).reshape(rows, heads, head_dim)
    gate_part = (
        jnp.sum(d_mixed * (memory_out - local_out), axis=(0, 2))
        * (gate_share * (1.0 - gate_share))[:, 0]
    )
    d_memory = (gate_share * d_mixed).astype(jnp.bfloat16)
    d_local_out = ((1.0 - gate_share) * d_mixed).astype(jnp.bfloat16)
    probs_again = jnp.exp(local_scores() - log_total)
    d_lw = jnp.einsum("qhd,khd->hqk", d_local_out, values_all, preferred_element_type=jnp.float32)
    d_local = (probs_again * (d_lw - jnp.sum(probs_again * d_lw, axis=-1, keepdims=True))).astype(
        jnp.bfloat16
    )
    d_values_all = jnp.einsum(
        "hqk,qhd->khd",
        probs_again.astype(jnp.bfloat16),
        d_local_out,
        preferred_element_type=jnp.float32,
    )
    d_keys_all = (
        jnp.einsum("hqk,qhd->khd", d_local, queries, preferred_element_type=jnp.float32)
        * score_scale
    )
    d_queries = (
        jnp.einsum("hqk,khd->qhd", d_local, keys_all, preferred_element_type=jnp.float32)
        * score_scale
    )
    bias_part = jnp.einsum(
        "hqk,qkb->hb", d_local, one_hot_f.astype(jnp.bfloat16), preferred_element_type=jnp.float32
    )
    d_mw = jnp.einsum(
        "qhd,qhkd->qhk", d_memory, fetched[..., 1, :], preferred_element_type=jnp.float32
    )
    d_mem = (mem_probs * (d_mw - jnp.sum(mem_probs * d_mw, axis=-1, keepdims=True))).astype(
        jnp.bfloat16
    )
    d_queries = (
        d_queries
        + jnp.einsum("qhk,qhkd->qhd", d_mem, fetched[..., 0, :], preferred_element_type=jnp.float32)
        * score_scale
    )
    halo_grads = jnp.stack([d_keys_all[:W], d_values_all[:W]])
    d_tails = jnp.zeros((2, sent_rows, heads, head_dim), jnp.float32)
    for distance in range(repeats, 0, -1):
        first_row = (repeats - distance) * sent_rows
        d_tails = d_tails + passed_along(
            halo_grads[:, first_row : first_row + sent_rows].astype(jnp.bfloat16), "mem", -distance
        ).astype(jnp.float32)
    d_keys = d_keys_all[W:] + d_tails[0]
    d_values = d_values_all[W:] + d_tails[1]
    d_projected = jnp.concatenate(
        [
            d_queries.reshape(rows, width),
            d_keys.reshape(rows, width),
            d_values.reshape(rows, width),
        ],
        axis=1,
    ).astype(jnp.bfloat16)
    d_in = lax.dot_general(
        d_projected, qkv_weight, contract_cols, preferred_element_type=jnp.float32
    )
    d_tokens_part, attn_gain_part = norm_in_back(d_in)
    tokens_grad = d_residual + d_tokens_part
    summed = lax.psum_scatter(
        jnp.concatenate(
            [
                lax.dot_general(
                    normed_in, d_projected, contract_rows, preferred_element_type=jnp.float32
                ),
                lax.dot_general(
                    mixed_heads, d_branch, contract_rows, preferred_element_type=jnp.float32
                ),
                lax.dot_general(
                    normed_mid, d_up, contract_rows, preferred_element_type=jnp.float32
                ),
                lax.dot_general(
                    cotangent, activated, contract_rows, preferred_element_type=jnp.float32
                ),
            ],
            axis=1,
        ),
        "mem",
        scatter_dimension=0,
        tiled=True,
    )
    summed = lax.psum(summed.astype(jnp.bfloat16), "dp").astype(jnp.float32)
    small_sums = lax.psum((attn_gain_part, ffn_gain_part, bias_part, gate_part), ("dp", "mem"))
    return (
        block_out,
        tokens_grad,
        summed[:, : 3 * width],
        summed[:, 3 * width : 4 * width],
        summed[:, 4 * width : 4 * width + hidden],
        summed[:, 4 * width + hidden :],
        small_sums[0],
        small_sums[1],
        small_sums[2],
        small_sums[3],
    )


def solution(mesh):
    in_specs = (
        P(("dp", "mem"), None),
        P(),
        P(),
        P(),
        P(),
        P(),
        P(),
        P(),
        P(),
        P("mem", None),
        P("mem", None),
        P("dp", None),
        P(("dp", "mem"), None, None, None),
        P(("dp", "mem"), None, None),
        P(("dp", "mem"), None, None),
        P(("dp", "mem"), None),
    )
    out_specs = (
        P(("dp", "mem"), None),
        P(("dp", "mem"), None),
        P("mem", None),
        P("mem", None),
        P("mem", None),
        P("mem", None),
        P(),
        P(),
        P(),
        P(),
    )
    return jax.shard_map(
        on_device, mesh=mesh, in_specs=in_specs, out_specs=out_specs, check_vma=False
    )
```

profile of v0, /device:TPU:9, one launch (start us, length us, event | category | flops | bytes accessed | tf_op | source)
XLA Modules:
  0.0 2371.2 jit_solution(17137563238203328121)
XLA Ops:
  13.1 121.0 %scatter_custom_fusion = s32[49152]{0:T(1024)} fusion(s32[32768]{0:T(1024)S(1)} %bitcast.203, s32[32768]{0:T(1024)} %reshape.412, s32[]{:T(128)} %constant.74.clone.1), kind=kCustom, calls=%fused_computation.179 | custom fusion | bytes 197120 | tf_op jit(solution)/shard_map/scatter | solution.py:66
  134.2 6.7 all-to-all-start
  140.9 13.3 reshape.371
  154.1 13.3 reshape.374
  167.6 169.2 %gather_fusion.1 = bf16[49152,128]{1,0:T(8,128)(2,1)} fusion(bf16[32768,128]{1,0:T(8,128)(2,1)} %reshape.371, s32[49152]{0:T(1024)S(1)} %fusion.85), kind=kCustom, calls=%fused_computation.clone | custom fusion | bytes 25362432 | tf_op jit(solution)/shard_map/jit(_take)/gather | solution.py:75
  336.8 169.2 %gather_fusion.2 = bf16[49152,128]{1,0:T(8,128)(2,1)} fusion(bf16[32768,128]{1,0:T(8,128)(2,1)} %reshape.374, s32[49152]{0:T(1024)S(1)} %fusion.85), kind=kCustom, calls=%fused_computation.1.clone | custom fusion | bytes 25362432 | tf_op jit(solution)/shard_map/jit(_take)/gather | solution.py:75
  506.0 26.4 %broadcast_select_fusion.1 = (bf16[49152,128]{1,0:T(8,128)(2,1)S(1)}, bf16[49152,128]{1,0:T(8,128)(2,1)S(1)}) fusion(bf16[49152,128]{1,0:T(8,128)(2,1)} %gather_fusion.1, pred[49152]{0:T(1024)(128)(4,1)S(1)} %compare_and_fusion.1, bf16[49152,128]{1,0:T(8,128)(2,1)} %gather_fusion.2), kind=kLoop, calls=%fused_computation.10 | loop fusion | flops 12582912 | bytes 50380800 | tf_op jit(solution)/shard_map/jit(_take)/select_n | solution.py:75
  532.4 10.1 pad_maximum_fusion.1
  542.4 6.4 all-to-all-start.1
  562.9 4.0 collective-permute-start.1
  566.9 14.6 collective-permute-start
  589.2 4.8 fusion.2
  602.2 497.0 %collective-permute-done = bf16[2,128,8,128]{3,1,2,0:T(8,128)(2,1)} collective-permute-done((bf16[2,128,8,128]{3,1,2,0:T(8,128)(2,1)}, bf16[2,128,8,128]{3,1,2,0:T(8,128)(2,1)}, u32[]{:S(2)}, u32[]{:S(2)}) %collective-permute-start) | collective-permute-done | bytes 524320 | tf_op jit(solution)/shard_map/ppermute | solution.py:22
  1109.6 48.9 %copy.123 = bf16[16,3072,2,128]{3,2,1,0:T(2,128)(2,1)} copy(bf16[16,3072,2,128]{3,1,2,0:T(8,128)(2,1)} %all-to-all-done.1) | data formatting | bytes 50331648 | tf_op jit(solution)/shard_map/all_to_all | solution.py:87
  1158.5 221.5 %gather_fusion = bf16[32768,2,128]{2,1,0:T(2,128)(2,1)} fusion(bf16[49152,2,128]{2,1,0:T(2,128)(2,1)} %bitcast.180, s32[32768]{0:T(1024)} %broadcast_clamp_fusion), kind=kCustom, calls=%fused_computation.2 | custom fusion | bytes 33685504 | tf_op jit(solution)/shard_map/jit(_take)/gather | solution.py:82
  1380.0 7.4 copy_select_fusion
  1387.4 6.7 fusion.4
  1409.1 6.8 add_convert_fusion
  1428.8 8.2 fusion.108
  1440.6 8.0 fusion.5
  1448.6 5.6 fusion.35
  1454.2 6.5 fusion.3
  1478.4 8.2 convolution_bitcast_fusion
  1486.6 29.3 %collective-permute-done.4 = bf16[2,128,8,128]{1,3,2,0:T(8,128)(2,1)S(1)} collective-permute-done((bf16[2,128,8,128]{1,3,2,0:T(8,128)(2,1)S(1)}, bf16[2,128,8,128]{1,3,2,0:T(8,128)(2,1)S(1)}, u32[]{:S(2)}, u32[]{:S(2)}) %collective-permute-start.4) | collective-permute-done | bytes 524320 | tf_op jit(solution)/shard_map/ppermute | solution.py:22
  1515.9 14.4 collective-permute-done.7
  1533.7 10.0 collective-permute-done.5
  1545.0 6.4 fusion.80
  1551.4 33.2 %pad_maximum_fusion = f32[1024,12288]{1,0:T(8,128)} fusion(f32[1024,4096]{1,0:T(8,128)} %convolution_bitcast_fusion, f32[1024,4096]{1,0:T(8,128)} %fusion.108, f32[1024,1024]{1,0:T(8,128)} %fusion.86, f32[1024,3072]{1,0:T(8,128)} %fusion.80), kind=kLoop, calls=%fused_computation.6 | loop fusion | flops 37748736 | bytes 100663296 | tf_op jit(solution)/shard_map/concatenate | solution.py:291
  1591.7 708.2 %reduce-scatter.2.cloned.1.call-done = f32[64,12288]{1,0:T(8,128)} async-done(((f32[1024,12288]{1,0:T(8,128)}), f32[64,12288]{1,0:T(8,128)}) %reduce-scatter.2.cloned.1.call-update) | async-done | bytes 3145744 | tf_op jit(solution)/shard_map/reduce_scatter | solution.py:290
  2303.1 7.4 fusion.32
  2310.5 6.1 fusion.43
  2316.6 40.3 %all-reduce = (f32[1024]{0:T(1024)}, f32[1024]{0:T(1024)}, f32[8,32]{1,0:T(8,128)}, f32[8]{0:T(128)}) all-reduce(f32[1024]{0:T(1024)S(1)} %get-tuple-element.13, f32[1024]{0:T(1024)S(1)} %get-tuple-element.11, f32[8,32]{1,0:T(8,128)S(1)} %fusion.36, f32[8]{0:T(128)S(1)} %multiply_multiply_fusion.5), channel_id=1, replica_groups=mesh['dp'=2,'mem'=16] {'dp','mem'}, use_global_device_ids=true, to_apply=%region_21.23 | all-reduce | flops 2312 | bytes 18496 | tf_op jit(solution)/shard_map/psum | solution.py:313
  (222 shorter events, 117.3 us)
Async XLA Ops:
  7.2 1398.5 %copy-start = (bf16[1024,1024]{1,0:T(8,128)(2,1)S(1)}, bf16[1024,1024]{1,0:T(8,128)(2,1)}, u32[]{:S(2)}) copy-start(bf16[1024,1024]{1,0:T(8,128)(2,1)} %param.21) | copy-start | bytes 6291460
  13.1 141.0 %copy-start.32 = (s32[32768,1]{0,1:T(1,128)}, s32[32768,1]{0,1:T(1,128)S(1)}, u32[]{:S(2)}) copy-start(s32[32768,1]{0,1:T(1,128)S(1)} %compare_select_fusion.2) | copy-start | bytes 393220
  134.2 33.3 %all-to-all-start = ((s32[16,1,3072]{2,1,0:T(1,128)}), s32[16,1,3072]{2,1,0:T(1,128)S(1)}, u32[]{:S(2)}, u32[]{:S(2)}) async-start(s32[16,1,3072]{2,1,0:T(1,128)} %bitcast.7), calls=%async_computation | async-start | bytes 393216 | tf_op jit(solution)/shard_map/all_to_all | solution.py:89
  542.4 7.7 copy-start.36
  542.4 567.1 %all-to-all-start.1 = ((bf16[16,3072,2,128]{3,1,2,0:T(8,128)(2,1)}), bf16[16,3072,2,128]{3,1,2,0:T(8,128)(2,1)}, u32[]{:S(2)}, u32[]{:S(2)}) async-start(bf16[16,3072,2,128]{3,1,2,0:T(8,128)(2,1)} %pad_maximum_fusion.1), calls=%async_computation.1 | async-start | bytes 50331648 | tf_op jit(solution)/shard_map/all_to_all | solution.py:87
  548.9 1751.0 %reduce-scatter.2.cloned.1.call-start = ((), (), s32[]{:S(2)}) async-start(), calls=%async_computation.3 | async-start | bytes 53477376 | tf_op jit(solution)/shard_map/reduce_scatter | solution.py:290
  554.0 28.4 %copy-start.49 = (s32[1,3]{1,0:T(1,128)S(1)}, s32[1,3]{1,0:T(1,128)}, u32[]{:S(2)}) copy-start(s32[1,3]{1,0:T(1,128)} %param.29) | copy-start | bytes 40
  555.9 33.2 %copy-start.44 = (f32[8,32]{1,0:T(8,128)S(1)}, f32[8,32]{1,0:T(8,128)}, u32[]{:S(2)}) copy-start(f32[8,32]{1,0:T(8,128)} %param.22) | copy-start | bytes 3076
  556.7 545.9 %collective-permute-start.3 = (bf16[2,128,8,128]{3,1,2,0:T(8,128)(2,1)}, bf16[2,128,8,128]{3,1,2,0:T(8,128)(2,1)}, u32[]{:S(2)}, u32[]{:S(2)}) collective-permute-start(bf16[2,128,8,128]{3,1,2,0:T(8,128)(2,1)} %copy_dynamic-update-slice_fusion), channel_id=1, source_target_pairs={{0,1},{1,2},{2,3},{3,4},{4,5},{5,6},{6,7},{7,8},{8,9},{9,10},{10,1... | collective-permute-start | bytes 1572872 | tf_op jit(solution)/shard_map/ppermute | solution.py:22
  559.8 541.7 %collective-permute-start.2 = (bf16[2,128,8,128]{3,1,2,0:T(8,128)(2,1)}, bf16[2,128,8,128]{3,1,2,0:T(8,128)(2,1)}, u32[]{:S(2)}, u32[]{:S(2)}) collective-permute-start(bf16[2,128,8,128]{3,1,2,0:T(8,128)(2,1)} %copy_dynamic-update-slice_fusion), channel_id=1, source_target_pairs={{0,2},{1,3},{2,4},{3,5},{4,6},{5,7},{6,8},{7,9},{8,10},{9,11},{10,... | collective-permute-start | bytes 1572872 | tf_op jit(solution)/shard_map/ppermute | solution.py:22
  562.9 537.4 %collective-permute-start.1 = (bf16[2,128,8,128]{3,1,2,0:T(8,128)(2,1)}, bf16[2,128,8,128]{3,1,2,0:T(8,128)(2,1)}, u32[]{:S(2)}, u32[]{:S(2)}) collective-permute-start(bf16[2,128,8,128]{3,1,2,0:T(8,128)(2,1)} %copy_dynamic-update-slice_fusion), channel_id=1, source_target_pairs={{0,3},{1,4},{2,5},{3,6},{4,7},{5,8},{6,9},{7,10},{8,11},{9,12},{10... | collective-permute-start | bytes 1572872 | tf_op jit(solution)/shard_map/ppermute | solution.py:22
  566.9 532.3 %collective-permute-start = (bf16[2,128,8,128]{3,1,2,0:T(8,128)(2,1)}, bf16[2,128,8,128]{3,1,2,0:T(8,128)(2,1)}, u32[]{:S(2)}, u32[]{:S(2)}) collective-permute-start(bf16[2,128,8,128]{3,1,2,0:T(8,128)(2,1)} %copy_dynamic-update-slice_fusion), channel_id=1, source_target_pairs={{0,4},{1,5},{2,6},{3,7},{4,8},{5,9},{6,10},{7,11},{8,12},{9,13},{1... | collective-permute-start | bytes 1572872 | tf_op jit(solution)/shard_map/ppermute | solution.py:22
  589.2 8.1 copy-start.40
  1103.9 297.9 %copy-start.14 = (bf16[512,8,128]{2,0,1:T(8,128)(2,1)}, bf16[512,8,128]{2,0,1:T(8,128)(2,1)S(1)}, u32[]{:S(2)}) copy-start(bf16[512,8,128]{2,0,1:T(8,128)(2,1)S(1)} %get-tuple-element.27) | copy-start | bytes 3145732
  1387.4 9.3 copy-start.3
  1387.4 6.7 copy-start.18
  1401.8 6.7 slice-start.2
  1419.1 7.1 copy-start.8
  1440.6 8.0 copy-start.20
  1469.4 74.8 %copy-start.38 = (bf16[128,8,128]{0,2,1:T(8,128)(2,1)}, bf16[128,8,128]{0,2,1:T(8,128)(2,1)S(1)}, u32[]{:S(2)}) copy-start(bf16[128,8,128]{0,2,1:T(8,128)(2,1)S(1)} %fusion.33) | copy-start | bytes 786436
  1469.9 8.5 copy-start.6
  1469.9 8.5 copy-start.24
  1470.5 45.4 %collective-permute-start.4 = (bf16[2,128,8,128]{1,3,2,0:T(8,128)(2,1)S(1)}, bf16[2,128,8,128]{1,3,2,0:T(8,128)(2,1)S(1)}, u32[]{:S(2)}, u32[]{:S(2)}) collective-permute-start(bf16[2,128,8,128]{1,3,2,0:T(8,128)(2,1)S(1)} %get-tuple-element.23), channel_id=1, source_target_pairs={{4,0},{5,1},{6,2},{7,3},{8,4},{9,5},{10,6},{11,7},{12,8},{13,9},{1... | collective-permute-start | bytes 1572872 | tf_op jit(solution)/shard_map/ppermute | solution.py:22
  1472.4 57.8 %collective-permute-start.7 = (bf16[2,128,8,128]{1,3,2,0:T(8,128)(2,1)S(1)}, bf16[2,128,8,128]{1,3,2,0:T(8,128)(2,1)S(1)}, u32[]{:S(2)}, u32[]{:S(2)}) collective-permute-start(bf16[2,128,8,128]{1,3,2,0:T(8,128)(2,1)S(1)} %get-tuple-element.24), channel_id=1, source_target_pairs={{1,0},{2,1},{3,2},{4,3},{5,4},{6,5},{7,6},{8,7},{9,8},{10,9},{11,1... | collective-permute-start | bytes 1572872 | tf_op jit(solution)/shard_map/ppermute | solution.py:22
  1474.3 59.3 %collective-permute-start.6 = (bf16[2,128,8,128]{1,3,2,0:T(8,128)(2,1)S(1)}, bf16[2,128,8,128]{1,3,2,0:T(8,128)(2,1)S(1)}, u32[]{:S(2)}, u32[]{:S(2)}) collective-permute-start(bf16[2,128,8,128]{1,3,2,0:T(8,128)(2,1)S(1)} %get-tuple-element.25), channel_id=1, source_target_pairs={{2,0},{3,1},{4,2},{5,3},{6,4},{7,5},{8,6},{9,7},{10,8},{11,9},{12,... | collective-permute-start | bytes 1572872 | tf_op jit(solution)/shard_map/ppermute | solution.py:22
  1476.3 67.4 %collective-permute-start.5 = (bf16[2,128,8,128]{1,3,2,0:T(8,128)(2,1)S(1)}, bf16[2,128,8,128]{1,3,2,0:T(8,128)(2,1)S(1)}, u32[]{:S(2)}, u32[]{:S(2)}) collective-permute-start(bf16[2,128,8,128]{1,3,2,0:T(8,128)(2,1)S(1)} %get-tuple-element.26), channel_id=1, source_target_pairs={{3,0},{4,1},{5,2},{6,3},{7,4},{8,5},{9,6},{10,7},{11,8},{12,9},{13... | collective-permute-start | bytes 1572872 | tf_op jit(solution)/shard_map/ppermute | solution.py:22
  1584.6 774.4 %all-reduce.3.cloned.1.call-start = ((), (), s32[]{:S(2)}) async-start(), calls=%async_computation.4 | async-start | bytes 3145728 | tf_op jit(solution)/shard_map/psum | solution.py:312
  2303.1 7.4 copy-start.26
  2303.1 7.4 copy-start.28
  2303.1 7.4 copy-start.39
  2310.5 46.4 %copy-start.47 = (f32[128]{0:T(128)S(1)}, f32[128]{0:T(128)}, u32[]{:S(2)}) copy-start(f32[128]{0:T(128)} %copy-done.46) | copy-start | bytes 1540
  2310.5 46.4 %copy-start.9 = (f32[128,1024]{1,0:T(8,128)S(1)}, f32[128,1024]{1,0:T(8,128)}, u32[]{:S(2)}) copy-start(f32[128,1024]{1,0:T(8,128)} %copy-done.8) | copy-start | bytes 1572868
  (35 other events, 90.6 us)
Sparse Core Ops, SparseCore 0:
  1584.7 715.1 reduce-scatter.1
  2303.2 21.5 all-reduce.2
where the time goes:
time: 2380 us; the launch traced here: 2370 us
  waiting for transfers between devices  1260 us (53%)
  local copies, waits for them, and re-layouts  804 us (34%)
  other arithmetic  105 us (4%)
  matrix products  98.4 us (4%)
  starting transfers between devices  45.8 us (2%)
  blocking collectives  40.3 us (2%)
    reduce_scatter x1, waiting for transfers between devices, on_device(): lax.psum_scatter(jnp.concatenate([lax.dot_general(normed_in, d_projected,...  708 us
    ppermute x8, waiting for transfers between devices, passed_along(): return lax.ppermute(value, axis, pairs)  554 us
    gather x1, local copies, waits for them, and re-layouts, unpack(): picked = jnp.take(flat_rows, places, axis=0)  221 us
    gather x1, local copies, waits for them, and re-layouts, lookup(): jnp.take(key_table, flat_ids, axis=0)  169 us
    gather x1, local copies, waits for them, and re-layouts, lookup(): jnp.take(value_table, flat_ids, axis=0)  169 us
    scatter x1, local copies, waits for them, and re-layouts, place_requests(): requests = jnp.zeros((groups * capacity,), jnp.int32).at[places].set(wanted)  121 us
    all_to_all x1, local copies, waits for them, and re-layouts, fetch_rows(): lax.all_to_all(lookup(lax.all_to_all(requests, 'mem', split_axis=0, conca...  48.9 us
  transfers between devices with their start and end apart: 12, of which 6 were waited for; matrix products, arithmetic and copies ran while one was open for 4% of the time, Pallas kernels for 0%

commit v1 on v0

--- a/solution.py
+++ b/solution.py
@@ -20,6 +20,10 @@
     size = lax.axis_size(axis)
     pairs = [(i, i + by) for i in range(size) if 0 <= i + by < size]
     return lax.ppermute(value, axis, pairs)
+
+
+def swapped(value):
+    return lax.ppermute(value, "dp", [(0, 1), (1, 0)])
 
 
 def bucket_of(offset):
@@ -287,37 +291,46 @@
     )
     d_tokens_part, attn_gain_part = norm_in_back(d_in)
     tokens_grad = d_residual + d_tokens_part
+    core = lax.axis_index("dp")
+    lefts, rights = [], []
+    for left, right in (
+        (normed_in, d_projected),
+        (mixed_heads, d_branch),
+        (normed_mid, d_up),
+        (cotangent, activated),
+    ):
+        half = right.shape[1] // 2
+        kept = lax.dynamic_slice_in_dim(right, core * half, half, 1)
+        sent = lax.dynamic_slice_in_dim(right, (1 - core) * half, half, 1)
+        lefts.append(left)
+        rights.append((kept, sent))
+    other_left = swapped(jnp.concatenate(lefts, axis=1))
+    other_right = swapped(jnp.concatenate([sent for _, sent in rights], axis=1))
+    partials, at = [], 0
+    for i, (left, (kept, _)) in enumerate(zip(lefts, rights)):
+        half = kept.shape[1]
+        left_both = jnp.concatenate([left, other_left[:, i * width : (i + 1) * width]], axis=0)
+        right_both = jnp.concatenate([kept, other_right[:, at : at + half]], axis=0)
+        at += half
+        partials.append(
+            lax.dot_general(
+                left_both, right_both, contract_rows, preferred_element_type=jnp.float32
+            ).astype(jnp.bfloat16)
+        )
     summed = lax.psum_scatter(
-        jnp.concatenate(
-            [
-                lax.dot_general(
-                    normed_in, d_projected, contract_rows, preferred_element_type=jnp.float32
-                ),
-                lax.dot_general(
-                    mixed_heads, d_branch, contract_rows, preferred_element_type=jnp.float32
-                ),
-                lax.dot_general(
-                    normed_mid, d_up, contract_rows, preferred_element_type=jnp.float32
-                ),
-                lax.dot_general(
-                    cotangent, activated, contract_rows, preferred_element_type=jnp.float32
-                ),
-            ],
-            axis=1,
-        ),
-        "mem",
-        scatter_dimension=0,
-        tiled=True,
-    )
-    summed = lax.psum(summed.astype(jnp.bfloat16), "dp").astype(jnp.float32)
+        jnp.concatenate(partials, axis=1), "mem", scatter_dimension=0, tiled=True
+    )
+    halves = lax.all_gather(summed, "dp", axis=0).astype(jnp.float32)
+    grads, at = [], 0
+    for kept, _ in rights:
+        half = kept.shape[1]
+        grads.append(jnp.concatenate([halves[0, :, at : at + half], halves[1, :, at : at + half]], 1))
+        at += half
     small_sums = lax.psum((attn_gain_part, ffn_gain_part, bias_part, gate_part), ("dp", "mem"))
     return (
         block_out,
         tokens_grad,
-        summed[:, : 3 * width],
-        summed[:, 3 * width : 4 * width],
-        summed[:, 4 * width : 4 * width + hidden],
-        summed[:, 4 * width + hidden :],
+        *grads,
         small_sums[0],
         small_sums[1],
         small_sums[2],

time: 2380 us -> 1900 us (0.80)
  waiting for transfers between devices: 1260 us -> 787 us
    reduce_scatter x1, waiting for transfers between devices: 708 us -> 215 us  [on_device(): lax.psum_scatter(jnp.concatenate(partials, axis=1), 'mem', scatter_dimens...]
  transfers between devices with their start and end apart: 12 -> 14, of which waited for: 6 -> 5; matrix products, arithmetic and copies ran while one was open for 4% -> 5% of each run, Pallas kernels for 0% -> 0%
where the time goes in v1:
time: 1900 us; the launch traced here: 1890 us
  local copies, waits for them, and re-layouts  815 us (43%)
  waiting for transfers between devices  787 us (41%)
  other arithmetic  110 us (6%)
  matrix products  86 us (5%)
  blocking collectives  39.3 us (2%)
  starting transfers between devices  38.1 us (2%)
    ppermute x8, waiting for transfers between devices, passed_along(): return lax.ppermute(value, axis, pairs)  568 us
    gather x1, local copies, waits for them, and re-layouts, unpack(): picked = jnp.take(flat_rows, places, axis=0)  221 us
    reduce_scatter x1, waiting for transfers between devices, on_device(): lax.psum_scatter(jnp.concatenate(partials, axis=1), 'mem', scatter_dimens...  215 us
    gather x1, local copies, waits for them, and re-layouts, lookup(): jnp.take(key_table, flat_ids, axis=0)  169 us
    gather x1, local copies, waits for them, and re-layouts, lookup(): jnp.take(value_table, flat_ids, axis=0)  169 us
    scatter x1, local copies, waits for them, and re-layouts, place_requests(): requests = jnp.zeros((groups * capacity,), jnp.int32).at[places].set(wanted)  121 us
    all_to_all x1, local copies, waits for them, and re-layouts, fetch_rows(): lax.all_to_all(lookup(lax.all_to_all(requests, 'mem', split_axis=0, conca...  48.9 us
    psum x1, blocking collectives, on_device(): lax.psum((attn_gain_part, ffn_gain_part, bias_part, gate_part), ('dp', 'm...  39.3 us
  transfers between devices with their start and end apart: 14, of which 5 were waited for; matrix products, arithmetic and copies ran while one was open for 5% of the time, Pallas kernels for 0%

profile of v1, /device:TPU:9, one launch (start us, length us, event | category | flops | bytes accessed | tf_op | source)
XLA Modules:
  0.0 1891.6 jit_solution(16065531854447946650)
XLA Ops:
  12.6 120.8 %scatter_custom_fusion = s32[49152]{0:T(1024)} fusion(s32[32768]{0:T(1024)S(1)} %bitcast.216, s32[32768]{0:T(1024)S(1)} %reshape.412, s32[]{:T(128)} %constant.81.clone.1), kind=kCustom, calls=%fused_computation.214 | custom fusion | bytes 196612 | tf_op jit(solution)/shard_map/scatter | solution.py:70
  133.3 6.7 all-to-all-start
  140.0 13.3 reshape.374
  153.3 13.3 reshape.371
  166.7 169.3 %gather_fusion.2 = bf16[49152,128]{1,0:T(8,128)(2,1)} fusion(bf16[32768,128]{1,0:T(8,128)(2,1)} %reshape.374, s32[49152]{0:T(1024)S(1)} %fusion.107), kind=kCustom, calls=%fused_computation.1.clone | custom fusion | bytes 25362432 | tf_op jit(solution)/shard_map/jit(_take)/gather | solution.py:79
  336.0 169.3 %gather_fusion.1 = bf16[49152,128]{1,0:T(8,128)(2,1)} fusion(bf16[32768,128]{1,0:T(8,128)(2,1)} %reshape.371, s32[49152]{0:T(1024)S(1)} %fusion.107), kind=kCustom, calls=%fused_computation.clone | custom fusion | bytes 25362432 | tf_op jit(solution)/shard_map/jit(_take)/gather | solution.py:79
  505.3 26.4 %broadcast_select_fusion.1 = (bf16[49152,128]{1,0:T(8,128)(2,1)S(1)}, bf16[49152,128]{1,0:T(8,128)(2,1)S(1)}) fusion(bf16[49152,128]{1,0:T(8,128)(2,1)} %gather_fusion.1, pred[49152]{0:T(1024)(128)(4,1)S(1)} %compare_and_fusion.1, bf16[49152,128]{1,0:T(8,128)(2,1)} %gather_fusion.2), kind=kLoop, calls=%fused_computation.10 | loop fusion | flops 12582912 | bytes 50380800 | tf_op jit(solution)/shard_map/jit(_take)/select_n | solution.py:79
  531.7 9.9 pad_maximum_fusion
  541.6 6.5 all-to-all-start.1
  548.8 3.9 convolution_convert_fusion.3
  558.5 4.0 collective-permute-start.1
  574.8 4.7 fusion.2
  586.5 511.9 %collective-permute-done = bf16[2,128,8,128]{3,1,2,0:T(8,128)(2,1)} collective-permute-done((bf16[2,128,8,128]{3,1,2,0:T(8,128)(2,1)}, bf16[2,128,8,128]{3,1,2,0:T(8,128)(2,1)}, u32[]{:S(2)}, u32[]{:S(2)}) %collective-permute-start) | collective-permute-done | bytes 524320 | tf_op jit(solution)/shard_map/ppermute | solution.py:22
  1108.5 48.9 %copy.139 = bf16[16,3072,2,128]{3,2,1,0:T(2,128)(2,1)} copy(bf16[16,3072,2,128]{3,1,2,0:T(8,128)(2,1)} %all-to-all-done.1) | data formatting | bytes 50331648 | tf_op jit(solution)/shard_map/all_to_all | solution.py:91
  1157.4 221.4 %gather_fusion = bf16[32768,2,128]{2,1,0:T(2,128)(2,1)} fusion(bf16[49152,2,128]{2,1,0:T(2,128)(2,1)} %bitcast.194, s32[32768]{0:T(1024)S(1)} %broadcast_clamp_fusion), kind=kCustom, calls=%fused_computation.2 | custom fusion | bytes 33685504 | tf_op jit(solution)/shard_map/jit(_take)/gather | solution.py:86
  1378.9 7.5 copy_select_fusion
  1386.4 4.5 fusion.4
  1390.9 21.2 %fusion.132 = (f32[128,8]{1,0:T(8,128)S(1)}, f32[128,8,32]{2,1,0:T(8,128)S(1)}) fusion(f32[128,8,32]{2,1,0:T(8,128)S(1)} %bitcast.215, s32[128,8,32]{2,1,0:T(8,128)S(1)} %copy.131), kind=kOutput, calls=%fused_computation.268 | output fusion | flops 262175 | bytes 397312 | tf_op jit(solution)/shard_map/sub | solution.py:112
  1417.7 4.1 fusion.74
  1425.3 14.4 add_convert_fusion
  1453.1 8.0 fusion.5
  1461.2 5.6 fusion.35
  1466.7 6.5 fusion.3
  1502.6 42.2 %collective-permute-done.4 = bf16[2,128,8,128]{1,3,2,0:T(8,128)(2,1)} collective-permute-done((bf16[2,128,8,128]{1,3,2,0:T(8,128)(2,1)}, bf16[2,128,8,128]{1,3,2,0:T(8,128)(2,1)}, u32[]{:S(2)}, u32[]{:S(2)}) %collective-permute-start.4) | collective-permute-done | bytes 524320 | tf_op jit(solution)/shard_map/ppermute | solution.py:22
  1544.7 14.1 collective-permute-done.7
  1568.7 4.2 collective-permute-start.9
  1573.2 4.2 collective-permute-done.8
  1590.3 10.4 pad_maximum_fusion.1
  1608.0 215.1 %reduce-scatter.2.cloned.1.call-done = bf16[64,6144]{1,0:T(8,128)(2,1)} async-done(((bf16[1024,6144]{1,0:T(8,128)(2,1)}), bf16[64,6144]{1,0:T(8,128)(2,1)}) %reduce-scatter.2.cloned.1.call-update) | async-done | bytes 786448 | tf_op jit(solution)/shard_map/reduce_scatter | solution.py:320
  1823.2 7.4 fusion.32
  1830.7 6.3 fusion.52
  1837.0 39.3 %all-reduce = (f32[1024]{0:T(1024)}, f32[1024]{0:T(1024)}, f32[8,32]{1,0:T(8,128)}, f32[8]{0:T(128)}) all-reduce(f32[1024]{0:T(1024)S(1)} %get-tuple-element.13, f32[1024]{0:T(1024)S(1)} %get-tuple-element.11, f32[8,32]{1,0:T(8,128)S(1)} %fusion.36, f32[8]{0:T(128)S(1)} %multiply_multiply_fusion.5), channel_id=1, replica_groups=mesh['dp'=2,'mem'=16] {'dp','mem'}, use_global_device_ids=true, to_apply=%region_20.22 | all-reduce | flops 2312 | bytes 18496 | tf_op jit(solution)/shard_map/psum | solution.py:329
  (298 shorter events, 130.8 us)
Async XLA Ops:
  7.2 1414.6 %copy-start = (bf16[1024,1024]{1,0:T(8,128)(2,1)S(1)}, bf16[1024,1024]{1,0:T(8,128)(2,1)}, u32[]{:S(2)}) copy-start(bf16[1024,1024]{1,0:T(8,128)(2,1)} %param.21) | copy-start | bytes 6291460
  12.6 120.8 %copy-start.52 = (s32[32768,1]{0,1:T(1,128)}, s32[32768,1]{0,1:T(1,128)S(1)}, u32[]{:S(2)}) copy-start(s32[32768,1]{0,1:T(1,128)S(1)} %compare_select_fusion.2) | copy-start | bytes 393220
  133.3 33.3 %all-to-all-start = ((s32[16,1,3072]{2,1,0:T(1,128)}), s32[16,1,3072]{2,1,0:T(1,128)S(1)}, u32[]{:S(2)}, u32[]{:S(2)}) async-start(s32[16,1,3072]{2,1,0:T(1,128)} %bitcast.7), calls=%async_computation | async-start | bytes 393216 | tf_op jit(solution)/shard_map/all_to_all | solution.py:93
  541.6 566.9 %all-to-all-start.1 = ((bf16[16,3072,2,128]{3,1,2,0:T(8,128)(2,1)}), bf16[16,3072,2,128]{3,1,2,0:T(8,128)(2,1)}, u32[]{:S(2)}, u32[]{:S(2)}) async-start(bf16[16,3072,2,128]{3,1,2,0:T(8,128)(2,1)} %pad_maximum_fusion), calls=%async_computation.1 | async-start | bytes 50331648 | tf_op jit(solution)/shard_map/all_to_all | solution.py:91
  548.1 1275.0 %reduce-scatter.2.cloned.1.call-start = ((), (), s32[]{:S(2)}) async-start(), calls=%async_computation.3 | async-start | bytes 13369344 | tf_op jit(solution)/shard_map/reduce_scatter | solution.py:320
  552.7 16.3 copy-start.74
  554.7 20.1 %copy-start.63 = (f32[8,32]{1,0:T(8,128)S(1)}, f32[8,32]{1,0:T(8,128)}, u32[]{:S(2)}) copy-start(f32[8,32]{1,0:T(8,128)} %param.22) | copy-start | bytes 3076
  555.4 543.0 %collective-permute-start = (bf16[2,128,8,128]{3,1,2,0:T(8,128)(2,1)}, bf16[2,128,8,128]{3,1,2,0:T(8,128)(2,1)}, u32[]{:S(2)}, u32[]{:S(2)}) collective-permute-start(bf16[2,128,8,128]{3,1,2,0:T(8,128)(2,1)} %copy_dynamic-update-slice_fusion), channel_id=1, source_target_pairs={{0,4},{1,5},{2,6},{3,7},{4,8},{5,9},{6,10},{7,11},{8,12},{9,13},{1... | collective-permute-start | bytes 1572872 | tf_op jit(solution)/shard_map/ppermute | solution.py:22
  558.5 541.0 %collective-permute-start.1 = (bf16[2,128,8,128]{3,1,2,0:T(8,128)(2,1)}, bf16[2,128,8,128]{3,1,2,0:T(8,128)(2,1)}, u32[]{:S(2)}, u32[]{:S(2)}) collective-permute-start(bf16[2,128,8,128]{3,1,2,0:T(8,128)(2,1)} %copy_dynamic-update-slice_fusion), channel_id=1, source_target_pairs={{0,3},{1,4},{2,5},{3,6},{4,7},{5,8},{6,9},{7,10},{8,11},{9,12},{10... | collective-permute-start | bytes 1572872 | tf_op jit(solution)/shard_map/ppermute | solution.py:22
  562.5 538.1 %collective-permute-start.2 = (bf16[2,128,8,128]{3,1,2,0:T(8,128)(2,1)}, bf16[2,128,8,128]{3,1,2,0:T(8,128)(2,1)}, u32[]{:S(2)}, u32[]{:S(2)}) collective-permute-start(bf16[2,128,8,128]{3,1,2,0:T(8,128)(2,1)} %copy_dynamic-update-slice_fusion), channel_id=1, source_target_pairs={{0,2},{1,3},{2,4},{3,5},{4,6},{5,7},{6,8},{7,9},{8,10},{9,11},{10,... | collective-permute-start | bytes 1572872 | tf_op jit(solution)/shard_map/ppermute | solution.py:22
  565.6 536.1 %collective-permute-start.3 = (bf16[2,128,8,128]{3,1,2,0:T(8,128)(2,1)}, bf16[2,128,8,128]{3,1,2,0:T(8,128)(2,1)}, u32[]{:S(2)}, u32[]{:S(2)}) collective-permute-start(bf16[2,128,8,128]{3,1,2,0:T(8,128)(2,1)} %copy_dynamic-update-slice_fusion), channel_id=1, source_target_pairs={{0,1},{1,2},{2,3},{3,4},{4,5},{5,6},{6,7},{7,8},{8,9},{9,10},{10,1... | collective-permute-start | bytes 1572872 | tf_op jit(solution)/shard_map/ppermute | solution.py:22
  582.1 521.9 %copy-start.24 = (bf16[128,1024]{0,1:T(8,128)(2,1)}, bf16[128,1024]{0,1:T(8,128)(2,1)S(1)}, u32[]{:S(2)}) copy-start(bf16[128,1024]{0,1:T(8,128)(2,1)S(1)} %copy.173) | copy-start | bytes 786436
  1157.4 221.4 %copy-start.51 = (pred[128,8,32]{2,1,0:T(8,128)(4,1)S(1)}, pred[128,8,32]{2,1,0:T(8,128)(4,1)}, u32[]{:S(2)}) copy-start(pred[128,8,32]{2,1,0:T(8,128)(4,1)} %compare_and_fusion) | copy-start | bytes 98308
  1378.9 7.5 copy-start.54
  1386.3 26.9 %copy-start.3 = (bf16[128,8,32,2,128]{4,2,1,0,3:T(8,128)(2,1)}, bf16[128,8,32,2,128]{4,2,1,0,3:T(8,128)(2,1)S(1)}, u32[]{:S(2)}) copy-start(bf16[128,8,32,2,128]{4,2,1,0,3:T(8,128)(2,1)S(1)} %copy_select_fusion) | copy-start | bytes 50331652
  1422.4 20.3 %copy-start.61 = (f32[128]{0:T(128)}, f32[128]{0:T(128)S(1)}, u32[]{:S(2)}) copy-start(f32[128]{0:T(128)S(1)} %fusion.115) | copy-start | bytes 1540
  1425.3 14.4 copy-start.7
  1453.1 8.0 copy-start.29
  1484.0 9.5 copy-start.8
  1484.1 9.5 copy-start.30
  1485.7 59.0 %collective-permute-start.4 = (bf16[2,128,8,128]{1,3,2,0:T(8,128)(2,1)}, bf16[2,128,8,128]{1,3,2,0:T(8,128)(2,1)}, u32[]{:S(2)}, u32[]{:S(2)}) collective-permute-start(bf16[2,128,8,128]{1,3,2,0:T(8,128)(2,1)} %get-tuple-element.31), channel_id=1, source_target_pairs={{4,0},{5,1},{6,2},{7,3},{8,4},{9,5},{10,6},{11,7},{12,8},{13,9},{1... | collective-permute-start | bytes 1572872 | tf_op jit(solution)/shard_map/ppermute | solution.py:22
  1487.8 56.9 %collective-permute-start.5 = (bf16[2,128,8,128]{1,3,2,0:T(8,128)(2,1)}, bf16[2,128,8,128]{1,3,2,0:T(8,128)(2,1)}, u32[]{:S(2)}, u32[]{:S(2)}) collective-permute-start(bf16[2,128,8,128]{1,3,2,0:T(8,128)(2,1)} %get-tuple-element.34), channel_id=1, source_target_pairs={{3,0},{4,1},{5,2},{6,3},{7,4},{8,5},{9,6},{10,7},{11,8},{12,9},{13... | collective-permute-start | bytes 1572872 | tf_op jit(solution)/shard_map/ppermute | solution.py:22
  1489.7 55.0 %collective-permute-start.6 = (bf16[2,128,8,128]{1,3,2,0:T(8,128)(2,1)}, bf16[2,128,8,128]{1,3,2,0:T(8,128)(2,1)}, u32[]{:S(2)}, u32[]{:S(2)}) collective-permute-start(bf16[2,128,8,128]{1,3,2,0:T(8,128)(2,1)} %get-tuple-element.33), channel_id=1, source_target_pairs={{2,0},{3,1},{4,2},{5,3},{6,4},{7,5},{8,6},{9,7},{10,8},{11,9},{12,... | collective-permute-start | bytes 1572872 | tf_op jit(solution)/shard_map/ppermute | solution.py:22
  1491.6 67.2 %collective-permute-start.7 = (bf16[2,128,8,128]{1,3,2,0:T(8,128)(2,1)}, bf16[2,128,8,128]{1,3,2,0:T(8,128)(2,1)}, u32[]{:S(2)}, u32[]{:S(2)}) collective-permute-start(bf16[2,128,8,128]{1,3,2,0:T(8,128)(2,1)} %get-tuple-element.32), channel_id=1, source_target_pairs={{1,0},{2,1},{3,2},{4,3},{5,4},{6,5},{7,6},{8,7},{9,8},{10,9},{11,1... | collective-permute-start | bytes 1572872 | tf_op jit(solution)/shard_map/ppermute | solution.py:22
  1568.7 10.8 copy-start.58
  1568.7 9.6 collective-permute-start.9
  1572.9 4.5 collective-permute-start.8
  1600.7 277.8 %all-gather.3.cloned.1.call-start = ((), (), s32[]{:S(2)}) async-start(), calls=%async_computation.4 | async-start | bytes 2359296 | tf_op jit(solution)/shard_map/all_gather | solution.py:323
  1830.6 45.7 %copy-start.70 = (f32[128]{0:T(128)S(1)}, f32[128]{0:T(128)}, u32[]{:S(2)}) copy-start(f32[128]{0:T(128)} %copy-done.69) | copy-start | bytes 1540
  1830.6 45.7 %copy-start.11 = (f32[128,1024]{1,0:T(8,128)S(1)}, f32[128,1024]{1,0:T(8,128)}, u32[]{:S(2)}) copy-start(f32[128,1024]{1,0:T(8,128)} %copy-done.10) | copy-start | bytes 1572868
  1830.6 45.7 %copy-start.62 = (f32[128]{0:T(128)S(1)}, f32[128]{0:T(128)}, u32[]{:S(2)}) copy-start(f32[128]{0:T(128)} %copy-done.61) | copy-start | bytes 1540
  1830.6 45.7 %copy-start.67 = (f32[128]{0:T(128)S(1)}, f32[128]{0:T(128)}, u32[]{:S(2)}) copy-start(f32[128]{0:T(128)} %copy-done.66) | copy-start | bytes 1540
  (62 other events, 209.1 us)
Sparse Core Ops, SparseCore 0:
  1600.8 222.2 reduce-scatter.1
  1824.7 10.2 all-gather.2

commit v2 on v1

--- a/solution.py
+++ b/solution.py
@@ -3,9 +3,12 @@
 import jax
 import jax.numpy as jnp
 from jax import lax
+from jax.experimental import pallas as pl
+from jax.experimental.pallas import tpu as pltpu
 from jax.sharding import PartitionSpec as P
 
 W = 512
+VMEM_LIMIT = 56 * 1024 * 1024
 
 
 eps_norm = 1e-06
@@ -46,72 +49,336 @@
     return jnp.sum((positions[..., None] >= book_ends).astype(jnp.int32), axis=-1)
 
 
-def place_requests(slot_shard, slot_index, groups, capacity, heads):
-    targets = slot_shard.reshape(-1)
-    head_ids = jnp.broadcast_to(jnp.arange(heads, dtype=jnp.int32)[None, :, None], slot_index.shape)
-    wanted = (slot_index * heads + head_ids).reshape(-1)
-    total = targets.shape[0]
-    block = math.gcd(total, 128)
-    blocks = total // block
-    owner_hot = (
-        targets.reshape(blocks, block)[:, :, None]
-        == jnp.arange(groups, dtype=jnp.int32)[None, None, :]
-    )
-    hot_low = owner_hot.astype(jnp.bfloat16)
-    earlier = (
-        jnp.arange(block, dtype=jnp.int32)[:, None] > jnp.arange(block, dtype=jnp.int32)[None, :]
-    ).astype(jnp.bfloat16)
-    inside_count = jnp.einsum("ij,bjg->big", earlier, hot_low, preferred_element_type=jnp.float32)
-    block_totals = jnp.sum(owner_hot.astype(jnp.float32), axis=1)
-    before_blocks = jnp.cumsum(block_totals, axis=0) - block_totals
-    counts = inside_count + before_blocks[:, None, :]
-    within = jnp.sum(jnp.where(owner_hot, counts, 0.0), axis=-1).reshape(-1).astype(jnp.int32)
-    places = targets * capacity + within
-    requests = jnp.zeros((groups * capacity,), jnp.int32).at[places].set(wanted)
-    return (requests.reshape(groups, capacity), places)
-
-
-def lookup(incoming, memory_keys, memory_values, heads):
-    key_table = memory_keys.reshape(-1, memory_keys.shape[1] // heads)
-    value_table = memory_values.reshape(-1, memory_values.shape[1] // heads)
-    flat_ids = incoming.reshape(-1)
-    found_rows = jnp.stack(
-        [jnp.take(key_table, flat_ids, axis=0), jnp.take(value_table, flat_ids, axis=0)], axis=1
-    )
-    return found_rows.reshape(incoming.shape[0], incoming.shape[1], 2, key_table.shape[1])
-
-
-def unpack(replies, places, entry_shape):
-    flat_rows = replies.reshape(-1, 2, replies.shape[3])
-    picked = jnp.take(flat_rows, places, axis=0)
-    return picked.reshape(entry_shape + (2, replies.shape[3]))
-
-
-def fetch_rows(requests, places, memory_keys, memory_values, heads, entry_shape):
-    replies = lax.all_to_all(
-        lookup(
-            lax.all_to_all(requests, "mem", split_axis=0, concat_axis=0, tiled=True),
-            memory_keys,
-            memory_values,
-            heads,
+def place_requests(slot_shard, slot_index, slot_live, owners, capacity, slots):
+    rows, heads, top_count = slot_index.shape
+    entries = rows * heads * top_count
+    row_of = (
+        jnp.arange(heads, dtype=jnp.int32)[None, :] * rows
+        + jnp.arange(rows, dtype=jnp.int32)[:, None]
+    )
+    place = row_of[:, :, None] * top_count + jnp.arange(top_count, dtype=jnp.int32)
+    owner = jnp.where(slot_live > 0, slot_shard[..., 0], owners)
+    keys, picked = lax.sort(
+        ((owner * entries + place).reshape(-1), slot_index.reshape(-1)), num_keys=1
+    )
+    ends = jnp.sum(
+        (keys[None, :] < (jnp.arange(owners, dtype=jnp.int32) + 1)[:, None] * entries).astype(jnp.int32),
+        axis=1,
+    )
+    starts = jnp.concatenate([jnp.zeros((1,), jnp.int32), ends[:-1]])
+    codes = jnp.concatenate(
+        [(keys % entries) // top_count * slots + picked, jnp.zeros((capacity,), jnp.int32)]
+    )
+    lists = jnp.stack(
+        [lax.dynamic_slice_in_dim(codes, starts[i], capacity) for i in range(owners)]
+    )
+    used = jnp.arange(capacity, dtype=jnp.int32)[None, :] < (ends - starts)[:, None]
+    return jnp.where(used, lists, heads * rows * slots)
+
+
+def split3(stat):
+    high = lax.reduce_precision(stat, 8, 7)
+    middle = lax.reduce_precision(stat - high, 8, 7)
+    return jnp.concatenate([high, middle, stat - high - middle], axis=1).astype(jnp.bfloat16)
+
+
+def gather_rows(index, counts, memory_keys, memory_values, heads, sources, capacity):
+    slots, width = memory_keys.shape
+    head_dim = width // heads
+    step = 16
+
+    def kernel(index_ref, counts_ref, keys, values, out_keys, out_values, key_table, value_table, key_rows, value_rows):
+        i = pl.program_id(0)
+
+        @pl.when(i == 0)
+        def _():
+            key_rows[...] = jnp.zeros_like(key_rows)
+            value_rows[...] = jnp.zeros_like(value_rows)
+
+        @pl.when(i < heads)
+        def _():
+            place = pl.ds(pl.multiple_of(i * slots, slots), slots)
+            key_table[place, :] = keys[...].astype(jnp.float32)
+            value_table[place, :] = values[...].astype(jnp.float32)
+
+        @pl.when(i >= heads)
+        def _():
+            source = i - heads
+
+            @pl.loop(0, (counts_ref[source] + step - 1) // step)
+            def _(group):
+                first = pl.multiple_of(group * step, step)
+                for u in range(step):
+                    row = index_ref[source * capacity + first + u]
+                    key_rows[pl.ds(first + u, 1), :] = key_table[pl.ds(row, 1), :]
+                    value_rows[pl.ds(first + u, 1), :] = value_table[pl.ds(row, 1), :]
+
+            out_keys[...] = key_rows[...].astype(jnp.bfloat16)
+            out_values[...] = value_rows[...].astype(jnp.bfloat16)
+
+    table_spec = pl.BlockSpec((slots, head_dim), lambda i, *_: (0, jnp.minimum(i, heads - 1)))
+    out_spec = pl.BlockSpec((capacity, head_dim), lambda i, *_: (jnp.maximum(i - heads, 0), 0))
+    out_shape = jax.ShapeDtypeStruct((sources * capacity, head_dim), jnp.bfloat16)
+    return pl.pallas_call(
+        kernel,
+        grid_spec=pltpu.PrefetchScalarGridSpec(
+            num_scalar_prefetch=2,
+            grid=(heads + sources,),
+            in_specs=[table_spec, table_spec],
+            out_specs=[out_spec, out_spec],
+            scratch_shapes=[
+                pltpu.VMEM((heads * slots, head_dim), jnp.float32),
+                pltpu.VMEM((heads * slots, head_dim), jnp.float32),
+                pltpu.VMEM((capacity, head_dim), jnp.float32),
+                pltpu.VMEM((capacity, head_dim), jnp.float32),
+            ],
         ),
-        "mem",
-        split_axis=0,
-        concat_axis=0,
-        tiled=True,
-    )
-    return unpack(replies, places, entry_shape)
-
-
-def memory_probs(queries, fetched_keys, live_mask, score_scale):
-    raw_scores = (
-        jnp.einsum("qhd,qhkd->qhk", queries, fetched_keys, preferred_element_type=jnp.float32)
-        * score_scale
-    )
-    row_max = jnp.max(jnp.where(live_mask, raw_scores, dead_score), axis=-1, keepdims=True)
-    exp_scores = jnp.exp(jnp.where(live_mask, raw_scores - row_max, dead_score))
-    sums_mem = jnp.sum(exp_scores, axis=-1, keepdims=True)
-    return exp_scores / jnp.where(sums_mem > 0, sums_mem, 1.0)
+        out_shape=[out_shape, out_shape],
+        compiler_params=pltpu.CompilerParams(vmem_limit_bytes=VMEM_LIMIT),
+        name="gather_rows",
+    )(index, counts, memory_keys, memory_values)
+
+
+def triple(stat):
+    part = lax.broadcasted_iota(jnp.int32, stat.shape, 1) // 16
+    high = stat.astype(jnp.bfloat16).astype(jnp.float32)
+    rest = stat - high
+    middle = rest.astype(jnp.bfloat16).astype(jnp.float32)
+    low = rest - middle
+    chosen = jnp.where(part == 0, high, jnp.where(part == 1, middle, jnp.where(part == 2, low, 0.0)))
+    return chosen.astype(jnp.bfloat16)
+
+
+def window_of(bounds, source, head, heads, span, capacity):
+    first = bounds[source * (heads + 1) + head]
+    last = bounds[source * (heads + 1) + head + 1]
+    start = jnp.minimum((first // 128) * 128, capacity - span)
+    extra = jnp.maximum(last - start - span + span - 1, 0) // span
+    return start, extra
+
+
+def memory_forward(bounds, queries, key_rows, value_rows, row_ids, heads, sources, rows, score_scale):
+    capacity, head_dim = key_rows.shape[0] // sources, key_rows.shape[1]
+    width = heads * head_dim
+    span = min(512, capacity)
+
+    def kernel(bounds_ref, q_ref, k_ref, v_ref, id_ref, out_ref, sums, tops, totals):
+        source = pl.program_id(0)
+        token = lax.broadcasted_iota(jnp.int32, (rows, span), 0)
+        lane = lax.broadcasted_iota(jnp.int32, (rows, 128), 1) % 16
+
+        def scores_of(head, start, least):
+            here = pl.ds(pl.multiple_of(start, 128), span)
+            ids = id_ref[0, :, here]
+            mine = ids == token + head * rows
+            if least is not None:
+                place = lax.broadcasted_iota(jnp.int32, (1, span), 1) + start
+                mine = mine & (place >= least)
+            q = q_ref[:, head * head_dim : (head + 1) * head_dim]
+            raw = lax.dot_general(q, k_ref[here, :], contract_cols, preferred_element_type=jnp.float32)
+            return jnp.where(mine, raw * score_scale, masked_score), mine, v_ref[here, :]
+
+        windows = [window_of(bounds_ref, source, head, heads, span, capacity) for head in range(heads)]
+        top_tile = jnp.zeros((rows, 128), jnp.float32)
+        total_tile = jnp.zeros((rows, 128), jnp.float32)
+        for head in range(heads):
+            scores, mine, v = scores_of(head, windows[head][0], None)
+            top = jnp.max(scores, axis=1, keepdims=True)
+            weights = jnp.where(mine, jnp.exp(scores - top), 0.0)
+            sums[:, head * head_dim : (head + 1) * head_dim] = jnp.dot(
+                weights.astype(jnp.bfloat16), v, preferred_element_type=jnp.float32
+            )
+            top_tile = jnp.where(lane == head, top, top_tile)
+            total_tile = jnp.where(
+                lane == heads + head, jnp.sum(weights, axis=1, keepdims=True), total_tile
+            )
+        tops[...] = top_tile
+        totals[...] = total_tile
+        more = sum(extra for _, extra in windows)
+
+        @pl.when(more > 0)
+        def _():
+            for head in range(heads):
+                start, extra = windows[head]
+                columns = slice(head * head_dim, (head + 1) * head_dim)
+
+                @pl.loop(0, extra)
+                def _(turn):
+                    least = start + (turn + 1) * span
+                    scores, mine, v = scores_of(head, jnp.minimum(least, capacity - span), least)
+                    old_top = jnp.max(
+                        jnp.where(lane == head, tops[...], masked_score), axis=1, keepdims=True
+                    )
+                    top = jnp.maximum(old_top, jnp.max(scores, axis=1, keepdims=True))
+                    weights = jnp.where(mine, jnp.exp(scores - top), 0.0)
+                    faded = jnp.exp(old_top - top)
+                    sums[:, columns] = sums[:, columns] * faded + jnp.dot(
+                        weights.astype(jnp.bfloat16), v, preferred_element_type=jnp.float32
+                    )
+                    tops[...] = jnp.where(lane == head, top, tops[...])
+                    totals[...] = jnp.where(
+                        lane == heads + head,
+                        totals[...] * faded + jnp.sum(weights, axis=1, keepdims=True),
+                        totals[...],
+                    )
+
+        out_ref[:, :width] = sums[...].astype(jnp.bfloat16)
+        out_ref[:, width:] = triple(jnp.where(lane < heads, tops[...], totals[...]))
+
+    return pl.pallas_call(
+        kernel,
+        grid_spec=pltpu.PrefetchScalarGridSpec(
+            num_scalar_prefetch=1,
+            grid=(sources,),
+            in_specs=[
+                pl.BlockSpec((rows, width), lambda i, *_: (i, 0)),
+                pl.BlockSpec((capacity, head_dim), lambda i, *_: (i, 0)),
+                pl.BlockSpec((capacity, head_dim), lambda i, *_: (i, 0)),
+                pl.BlockSpec((1, 1, capacity), lambda i, *_: (i, 0, 0)),
+            ],
+            out_specs=pl.BlockSpec((rows, width + 128), lambda i, *_: (i, 0)),
+            scratch_shapes=[
+                pltpu.VMEM((rows, width), jnp.float32),
+                pltpu.VMEM((rows, 128), jnp.float32),
+                pltpu.VMEM((rows, 128), jnp.float32),
+            ],
+        ),
+        out_shape=jax.ShapeDtypeStruct((sources * rows, width + 128), jnp.bfloat16),
+        compiler_params=pltpu.CompilerParams(vmem_limit_bytes=VMEM_LIMIT),
+        name="memory_forward",
+    )(bounds, queries, key_rows, value_rows, row_ids)
+
+
+def combine_partials(partial, heads, sources, rows):
+    width = partial.shape[1] - 128
+    head_dim = width // heads
+
+    def kernel(part_ref, out_ref, log_ref, sums, tops, totals):
+        i = pl.program_id(0)
+
+        @pl.when(i == 0)
+        def _():
+            sums[...] = jnp.zeros_like(sums)
+            tops[...] = jnp.full_like(tops, masked_score)
+            totals[...] = jnp.zeros_like(totals)
+
+        stat = part_ref[:, width:].astype(jnp.float32)
+        stat = stat + pltpu.roll(stat, 128 - 16, 1) + pltpu.roll(stat, 128 - 32, 1)
+        new_total = pltpu.roll(stat, 128 - heads, 1)
+        top = jnp.maximum(tops[...], stat)
+        old_fade, new_fade = jnp.exp(tops[...] - top), jnp.exp(stat - top)
+        tops[...] = top
+        totals[...] = totals[...] * old_fade + new_total * new_fade
+        for head in range(heads):
+            columns = slice(head * head_dim, (head + 1) * head_dim)
+            sums[:, columns] = (
+                sums[:, columns] * old_fade[:, head : head + 1]
+                + part_ref[:, columns].astype(jnp.float32) * new_fade[:, head : head + 1]
+            )
+
+        @pl.when(i == sources - 1)
+        def _():
+            live = totals[...] > 0
+            total = jnp.where(live, totals[...], 1.0)
+            log_ref[...] = jnp.where(live, tops[...] + jnp.log(total), 0.0)
+            for head in range(heads):
+                columns = slice(head * head_dim, (head + 1) * head_dim)
+                out_ref[:, columns] = sums[:, columns] / total[:, head : head + 1]
+
+    return pl.pallas_call(
+        kernel,
+        grid=(sources,),
+        in_specs=[pl.BlockSpec((rows, width + 128), lambda i: (i, 0))],
+        out_specs=[
+            pl.BlockSpec((rows, width), lambda i: (0, 0)),
+            pl.BlockSpec((rows, 128), lambda i: (0, 0)),
+        ],
+        scratch_shapes=[
+            pltpu.VMEM((rows, width), jnp.float32),
+            pltpu.VMEM((rows, 128), jnp.float32),
+            pltpu.VMEM((rows, 128), jnp.float32),
+        ],
+        out_shape=[
+            jax.ShapeDtypeStruct((rows, width), jnp.float32),
+            jax.ShapeDtypeStruct((rows, 128), jnp.float32),
+        ],
+        compiler_params=pltpu.CompilerParams(vmem_limit_bytes=VMEM_LIMIT),
+        name="combine_partials",
+    )(partial)
+
+
+def memory_backward(bounds, queries, grads, key_rows, value_rows, row_ids, heads, sources, rows, score_scale):
+    capacity, head_dim = key_rows.shape[0] // sources, key_rows.shape[1]
+    width = heads * head_dim
+    span = min(512, capacity)
+
+    def kernel(bounds_ref, q_ref, g_ref, k_ref, v_ref, id_ref, out_ref, sums):
+        source = pl.program_id(0)
+        token = lax.broadcasted_iota(jnp.int32, (rows, span), 0)
+        stat = g_ref[:, width : width + 128].astype(jnp.float32)
+
+        def term(column):
+            return (
+                stat[:, column : column + 1]
+                + stat[:, column + 16 : column + 17]
+                + stat[:, column + 32 : column + 33]
+            )
+
+        def part_of(head, start, least):
+            here = pl.ds(pl.multiple_of(start, 128), span)
+            columns = slice(head * head_dim, (head + 1) * head_dim)
+            mine = id_ref[0, :, here] == token + head * rows
+            if least is not None:
+                place = lax.broadcasted_iota(jnp.int32, (1, span), 1) + start
+                mine = mine & (place >= least)
+            k, v = k_ref[here, :], v_ref[here, :]
+            raw = lax.dot_general(
+                q_ref[:, columns], k, contract_cols, preferred_element_type=jnp.float32
+            )
+            products = lax.dot_general(
+                g_ref[:, columns], v, contract_cols, preferred_element_type=jnp.float32
+            )
+            probs = jnp.exp(jnp.where(mine, raw * score_scale - term(head), dead_score))
+            slopes = (probs * (products - term(heads + head))).astype(jnp.bfloat16)
+            return jnp.dot(slopes, k, preferred_element_type=jnp.float32)
+
+        windows = [window_of(bounds_ref, source, head, heads, span, capacity) for head in range(heads)]
+        for head in range(heads):
+            sums[:, head * head_dim : (head + 1) * head_dim] = part_of(head, windows[head][0], None)
+        more = sum(extra for _, extra in windows)
+
+        @pl.when(more > 0)
+        def _():
+            for head in range(heads):
+                start, extra = windows[head]
+                columns = slice(head * head_dim, (head + 1) * head_dim)
+
+                @pl.loop(0, extra)
+                def _(turn):
+                    least = start + (turn + 1) * span
+                    sums[:, columns] += part_of(head, jnp.minimum(least, capacity - span), least)
+
+        out_ref[...] = sums[...].astype(jnp.bfloat16)
+
+    return pl.pallas_call(
+        kernel,
+        grid_spec=pltpu.PrefetchScalarGridSpec(
+            num_scalar_prefetch=1,
+            grid=(sources,),
+            in_specs=[
+                pl.BlockSpec((rows, width), lambda i, *_: (i, 0)),
+                pl.BlockSpec((rows, width + 128), lambda i, *_: (i, 0)),
+                pl.BlockSpec((capacity, head_dim), lambda i, *_: (i, 0)),
+                pl.BlockSpec((capacity, head_dim), lambda i, *_: (i, 0)),
+                pl.BlockSpec((1, 1, capacity), lambda i, *_: (i, 0, 0)),
+            ],
+            out_specs=pl.BlockSpec((rows, width), lambda i, *_: (i, 0)),
+            scratch_shapes=[pltpu.VMEM((rows, width), jnp.float32)],
+        ),
+        out_shape=jax.ShapeDtypeStruct((sources * rows, width), jnp.bfloat16),
+        compiler_params=pltpu.CompilerParams(vmem_limit_bytes=VMEM_LIMIT),
+        name="memory_backward",
+    )(bounds, queries, grads, key_rows, value_rows, row_ids)
 
 
 def on_device(
@@ -194,17 +461,36 @@
         values_all,
         preferred_element_type=jnp.float32,
     )
-    requests, places = place_requests(slot_shard, slot_index, groups, capacity, heads)
-    entry_shape = (rows, heads, top_count)
-    fetched = fetch_rows(requests, places, memory_keys, memory_values, heads, entry_shape)
-    live_mask = slot_live > 0
-    mem_probs = memory_probs(queries, fetched[..., 0, :], live_mask, score_scale)
-    memory_out = jnp.einsum(
-        "qhk,qhkd->qhd",
-        mem_probs.astype(jnp.bfloat16),
-        fetched[..., 1, :],
-        preferred_element_type=jnp.float32,
-    )
+    slots = memory_keys.shape[0]
+    requests = place_requests(slot_shard, slot_index, slot_live, groups, capacity, slots)
+    incoming = lax.all_to_all(requests, "mem", split_axis=0, concat_axis=0, tiled=True)
+    row_ids = incoming // slots
+    limits = jnp.arange(heads + 1, dtype=jnp.int32) * (rows * slots)
+    bounds = jnp.sum((incoming[:, None, :] < limits[None, :, None]).astype(jnp.int32), axis=2)
+    index = jnp.where(row_ids < heads * rows, row_ids // rows * slots + incoming % slots, 0)
+    key_rows, value_rows = gather_rows(
+        index.reshape(-1), bounds[:, heads], memory_keys, memory_values, heads, groups, capacity
+    )
+    all_queries = lax.all_gather(projected[:, :width], "mem", axis=0, tiled=True)
+    entry_rows = row_ids[:, None, :]
+    partial = memory_forward(
+        bounds.reshape(-1),
+        all_queries,
+        key_rows,
+        value_rows,
+        entry_rows,
+        heads,
+        groups,
+        rows,
+        score_scale,
+    )
+    partial = lax.all_to_all(
+        partial.reshape(groups, rows, width + 128), "mem", split_axis=0, concat_axis=0, tiled=True
+    )
+    memory_out, mem_log = combine_partials(
+        partial.reshape(groups * rows, width + 128), heads, groups, rows
+    )
+    memory_out = memory_out.reshape(rows, heads, head_dim)
     gate_share = jax.nn.sigmoid(gate_logit)[:, None]
     mixed_heads = (
         (gate_share * memory_out + (1.0 - gate_share) * local_out)
@@ -258,16 +544,34 @@
     bias_part = jnp.einsum(
         "hqk,qkb->hb", d_local, one_hot_f.astype(jnp.bfloat16), preferred_element_type=jnp.float32
     )
-    d_mw = jnp.einsum(
-        "qhd,qhkd->qhk", d_memory, fetched[..., 1, :], preferred_element_type=jnp.float32
-    )
-    d_mem = (mem_probs * (d_mw - jnp.sum(mem_probs * d_mw, axis=-1, keepdims=True))).astype(
-        jnp.bfloat16
+    mem_delta = jnp.sum(d_memory.astype(jnp.float32) * memory_out, axis=-1)
+    sent_grads = jnp.concatenate(
+        [
+            d_memory.reshape(rows, width),
+            split3(jnp.concatenate([mem_log[:, :heads], mem_delta], axis=1)),
+            jnp.zeros((rows, 80), jnp.bfloat16),
+        ],
+        axis=1,
+    )
+    all_grads = lax.all_gather(sent_grads, "mem", axis=0, tiled=True)
+    d_partial = memory_backward(
+        bounds.reshape(-1),
+        all_queries,
+        all_grads,
+        key_rows,
+        value_rows,
+        entry_rows,
+        heads,
+        groups,
+        rows,
+        score_scale,
+    )
+    d_partial = lax.all_to_all(
+        d_partial.reshape(groups, rows, width), "mem", split_axis=0, concat_axis=0, tiled=True
     )
     d_queries = (
         d_queries
-        + jnp.einsum("qhk,qhkd->qhd", d_mem, fetched[..., 0, :], preferred_element_type=jnp.float32)
-        * score_scale
+        + jnp.sum(d_partial.astype(jnp.float32), axis=0).reshape(rows, heads, head_dim) * score_scale
     )
     halo_grads = jnp.stack([d_keys_all[:W], d_values_all[:W]])
     d_tails = jnp.zeros((2, sent_rows, heads, head_dim), jnp.float32)

time: 1900 us -> 989 us (0.52)
  local copies, waits for them, and re-layouts: 815 us -> 53 us
  waiting for transfers between devices: 787 us -> 518 us
  Pallas kernels: 0 us -> 133 us
  other arithmetic: 110 us -> 58.2 us
  starting transfers between devices: 38.1 us -> 75.3 us
  matrix products: 86 us -> 54.9 us
  between operations: 15.8 us -> 44.5 us
    gather x3 -> x0, local copies, waits for them, and re-layouts: 560 us -> none  [the longest x1 221 us: unpack(): picked = jnp.take(flat_rows, places, axis=0)]
    ppermute x8, waiting for transfers between devices: 568 us -> 214 us  [passed_along(): return lax.ppermute(value, axis, pairs)]
    pallas_call x0 -> x4, Pallas kernels: none -> 133 us  [the longest x1 42.9 us: gather_rows(): pl.pallas_call(kernel, grid_spec=pltpu.PrefetchScalarGridSpec(num_scalar_...]
    scatter x1 -> x0, local copies, waits for them, and re-layouts: 121 us -> none  [place_requests(): requests = jnp.zeros((groups * capacity,), jnp.int32).at[places].set(wanted)]
    all_gather x0 -> x2, waiting for transfers between devices: none -> 92.8 us  [the longest x1 92.8 us: on_device(): all_grads = lax.all_gather(sent_grads, 'mem', axis=0, tiled=True)]
    all_to_all x1 -> x0, local copies, waits for them, and re-layouts: 48.9 us -> none  [fetch_rows(): lax.all_to_all(lookup(lax.all_to_all(requests, 'mem', split_axis=0, conca...]
    select_n x4 -> x3, other arithmetic: 34.1 us -> 3.42 us  [the longest x1 1.53 us: on_device(): row_ids = incoming // slots]
    all_to_all x2 -> x3, starting transfers between devices: 13.1 us -> 39.9 us  [the longest x1 27.7 us: on_device(): lax.all_to_all(partial.reshape(groups, rows, width + 128), 'mem', split_a...]
  transfers between devices with their start and end apart: 14 -> 17, of which waited for: 5 -> 11; matrix products, arithmetic and copies ran while one was open for 5% -> 9% of each run, Pallas kernels for 0% -> 4%
where the time goes in v2:
time: 989 us; the launch traced here: 977 us
  waiting for transfers between devices  518 us (52%)
  Pallas kernels  133 us (13%)
  starting transfers between devices  75.3 us (8%)
  other arithmetic  58.2 us (6%)
  matrix products  54.9 us (6%)
  local copies, waits for them, and re-layouts  53 us (5%)
  between operations  44.5 us (4%)
  blocking collectives  39.5 us (4%)
    ppermute x8, waiting for transfers between devices, passed_along(): return lax.ppermute(value, axis, pairs)  214 us
    reduce_scatter x1, waiting for transfers between devices, on_device(): lax.psum_scatter(jnp.concatenate(partials, axis=1), 'mem', scatter_dimens...  195 us
    all_gather x1, waiting for transfers between devices, on_device(): all_grads = lax.all_gather(sent_grads, 'mem', axis=0, tiled=True)  92.8 us
    pallas_call x1, Pallas kernels, gather_rows(): pl.pallas_call(kernel, grid_spec=pltpu.PrefetchScalarGridSpec(num_scalar_...  42.9 us
    pallas_call x1, Pallas kernels, memory_forward(): pl.pallas_call(kernel, grid_spec=pltpu.PrefetchScalarGridSpec(num_scalar_...  41.6 us
    psum x1, blocking collectives, on_device(): lax.psum((attn_gain_part, ffn_gain_part, bias_part, gate_part), ('dp', 'm...  39.5 us
    pallas_call x1, Pallas kernels, memory_backward(): pl.pallas_call(kernel, grid_spec=pltpu.PrefetchScalarGridSpec(num_scalar_...  35.7 us
    ppermute x8, starting transfers between devices, passed_along(): return lax.ppermute(value, axis, pairs)  33.5 us
  transfers between devices with their start and end apart: 17, of which 11 were waited for; matrix products, arithmetic and copies ran while one was open for 9% of the time, Pallas kernels for 4%

profile of v2, /device:TPU:9, one launch (start us, length us, event | category | flops | bytes accessed | tf_op | source)
XLA Modules:
  0.0 977.1 jit_solution(7290548334236526476)
XLA Ops:
  9.6 3.9 convolution_convert_fusion.3
  15.6 17.6 %sort.23 = (s32[32768]{0:T(1024)S(1)}, s32[32768]{0:T(1024)S(1)}, s32[32768]{0:T(1024)}) sort(s32[32768]{0:T(1024)S(1)} %reshape.605, s32[32768]{0:T(1024)S(1)} %reshape.606, s32[32768]{0:T(1024)S(1)} %iota.71), dimensions={0}, to_apply=%region_0.0 | sort | flops 491520 | bytes 786432 | tf_op jit(solution)/shard_map/sort | solution.py:61
  65.2 6.7 all-to-all-start
  71.9 12.4 %all-to-all-done = s32[16,1,3072]{2,1,0:T(1,128)S(1)} async-done(((s32[16,1,3072]{2,1,0:T(1,128)}), s32[16,1,3072]{2,1,0:T(1,128)S(1)}, u32[]{:S(2)}, u32[]{:S(2)}) %all-to-all-start) | async-done | bytes 196640 | tf_op jit(solution)/shard_map/all_to_all | solution.py:466
  86.9 42.9 %gather_rows.1 = (bf16[49152,128]{1,0:T(8,128)(2,1)}, bf16[49152,128]{1,0:T(8,128)(2,1)}) custom-call(s32[49152]{0:T(1024)} %fusion.82.index_ref, s32[16]{0:T(128)} %slice_bitcast_fusion.18.counts_ref, bf16[4096,1024]{1,0:T(8,128)(2,1)} %keys.1, bf16[4096,1024]{1,0:T(8,128)(2,1)} %values.1), custom_call_target="tpu_custom_call" | custom-call | tf_op jit(solution)/shard_map/gather_rows/pallas_call | solution.py:122
  131.4 41.6 %memory_forward.1 = bf16[2048,1152]{1,0:T(8,128)(2,1)} custom-call(s32[144]{0:T(256)} %reshape.607.bounds_ref, bf16[2048,1024]{1,0:T(8,128)(2,1)} %all-gather.5.cloned.1.call-done.q_ref, bf16[49152,128]{1,0:T(8,128)(2,1)} %get-tuple-element.20.k_ref, bf16[49152,128]{1,0:T(8,128)(2,1)} %get-tuple-element.21.v_ref, s32[16,1,3072]{2,1,0:T(1,128)} %and_select_fusion.id_ref), custom_call_target="tpu_custom_call" | custom-call | tf_op jit(solution)/shard_map/memory_forward/pallas_call | solution.py:228
  173.0 27.7 %all-to-all-start.1 = ((bf16[16,128,1152]{2,1,0:T(8,128)(2,1)}), bf16[16,128,1152]{2,1,0:T(8,128)(2,1)}, u32[]{:S(2)}, u32[]{:S(2)}) async-start(bf16[16,128,1152]{2,1,0:T(8,128)(2,1)} %bitcast.160), calls=%async_computation.1 | async-start | bytes 9437184 | tf_op jit(solution)/shard_map/all_to_all | solution.py:487
  205.4 4.0 collective-permute-start.1
  209.4 3.1 collective-permute-start.2
  212.5 13.1 %collective-permute-start.3 = (bf16[2,128,8,128]{3,1,2,0:T(8,128)(2,1)}, bf16[2,128,8,128]{3,1,2,0:T(8,128)(2,1)}, u32[]{:S(2)}, u32[]{:S(2)}) collective-permute-start(bf16[2,128,8,128]{3,1,2,0:T(8,128)(2,1)} %copy_dynamic-update-slice_fusion), channel_id=1, source_target_pairs={{0,1},{1,2},{2,3},{3,4},{4,5},{5,6},{6,7},{7,8},{8,9},{9,10},{10,1... | collective-permute-start | bytes 1572872 | tf_op jit(solution)/shard_map/ppermute | solution.py:25
  228.1 4.7 fusion
  233.8 3.5 copy.141
  238.0 80.7 %collective-permute-done = bf16[2,128,8,128]{3,1,2,0:T(8,128)(2,1)} collective-permute-done((bf16[2,128,8,128]{3,1,2,0:T(8,128)(2,1)}, bf16[2,128,8,128]{3,1,2,0:T(8,128)(2,1)}, u32[]{:S(2)}, u32[]{:S(2)}) %collective-permute-start) | collective-permute-done | bytes 524320 | tf_op jit(solution)/shard_map/ppermute | solution.py:25
  323.0 14.7 %collective-permute-done.3 = bf16[2,128,8,128]{3,1,2,0:T(8,128)(2,1)} collective-permute-done((bf16[2,128,8,128]{3,1,2,0:T(8,128)(2,1)}, bf16[2,128,8,128]{3,1,2,0:T(8,128)(2,1)}, u32[]{:S(2)}, u32[]{:S(2)}) %collective-permute-start.3) | collective-permute-done | bytes 524320 | tf_op jit(solution)/shard_map/ppermute | solution.py:25
  344.4 13.0 %combine_partials.1 = (f32[128,1024]{1,0:T(8,128)}, f32[128,128]{1,0:T(8,128)}) custom-call(bf16[2048,1152]{1,0:T(8,128)(2,1)} %bitcast.35.part_ref), custom_call_target="tpu_custom_call" | custom-call | tf_op jit(solution)/shard_map/combine_partials/pallas_call | solution.py:288
  358.7 4.1 add_convert_fusion.1
  366.5 6.9 add_convert_fusion
  382.0 92.8 %all-gather.7.cloned.1.call-done.g_ref = bf16[2048,1152]{1,0:T(8,128)(2,1)} async-done(((bf16[128,1152]{1,0:T(8,128)(2,1)}), bf16[2048,1152]{1,0:T(8,128)(2,1)}) %all-gather.7.cloned.1.call-update) | async-done | bytes 4718608 | tf_op jit(solution)/shard_map/all_gather | solution.py:556
  474.8 35.7 %memory_backward.1 = bf16[2048,1024]{1,0:T(8,128)(2,1)} custom-call(s32[144]{0:T(256)} %reshape.607.bounds_ref, bf16[2048,1024]{1,0:T(8,128)(2,1)} %all-gather.5.cloned.1.call-done.q_ref, bf16[2048,1152]{1,0:T(8,128)(2,1)} %all-gather.7.cloned.1.call-done.g_ref, bf16[49152,128]{1,0:T(8,128)(2,1)} %get-tuple-element.20.k_ref, ...), custom_call_target="tpu_custom_call" | custom-call | tf_op jit(solution)/shard_map/memory_backward/pallas_call | solution.py:363
  510.5 5.6 all-to-all-start.2
  528.0 4.1 collective-permute-start.7
  545.3 54.9 %collective-permute-done.7 = bf16[2,128,8,128]{1,3,2,0:T(8,128)(2,1)} collective-permute-done((bf16[2,128,8,128]{1,3,2,0:T(8,128)(2,1)}, bf16[2,128,8,128]{1,3,2,0:T(8,128)(2,1)}, u32[]{:S(2)}, u32[]{:S(2)}) %collective-permute-start.7) | collective-permute-done | bytes 524320 | tf_op jit(solution)/shard_map/ppermute | solution.py:25
  600.1 18.8 %collective-permute-done.6 = bf16[2,128,8,128]{1,3,2,0:T(8,128)(2,1)} collective-permute-done((bf16[2,128,8,128]{1,3,2,0:T(8,128)(2,1)}, bf16[2,128,8,128]{1,3,2,0:T(8,128)(2,1)}, u32[]{:S(2)}, u32[]{:S(2)}) %collective-permute-start.6) | collective-permute-done | bytes 524320 | tf_op jit(solution)/shard_map/ppermute | solution.py:25
  618.9 11.5 %collective-permute-done.5 = bf16[2,128,8,128]{1,3,2,0:T(8,128)(2,1)} collective-permute-done((bf16[2,128,8,128]{1,3,2,0:T(8,128)(2,1)}, bf16[2,128,8,128]{1,3,2,0:T(8,128)(2,1)}, u32[]{:S(2)}, u32[]{:S(2)}) %collective-permute-start.5) | collective-permute-done | bytes 524320 | tf_op jit(solution)/shard_map/ppermute | solution.py:25
  630.4 32.7 %collective-permute-done.4 = bf16[2,128,8,128]{1,3,2,0:T(8,128)(2,1)} collective-permute-done((bf16[2,128,8,128]{1,3,2,0:T(8,128)(2,1)}, bf16[2,128,8,128]{1,3,2,0:T(8,128)(2,1)}, u32[]{:S(2)}, u32[]{:S(2)}) %collective-permute-start.4) | collective-permute-done | bytes 524320 | tf_op jit(solution)/shard_map/ppermute | solution.py:25
  669.7 3.2 convert_reduce_fusion
  684.3 4.2 collective-permute-done.8
  699.9 10.4 %pad_maximum_fusion = bf16[1024,6144]{1,0:T(8,128)(2,1)} fusion(bf16[1024,2048]{1,0:T(8,128)(2,1)S(1)} %convolution_convert_fusion.1, bf16[1024,2048]{1,0:T(8,128)(2,1)S(1)} %convolution_convert_fusion.2, bf16[1024,512]{1,0:T(8,128)(2,1)S(1)} %copy-done.12, bf16[1024,1536]{1,0:T(8,128)(2,1)S(1)} %convolution_convert_fusion), kind=kLoop, calls=%fused_computation | loop fusion | flops 50331648 | bytes 25165824 | tf_op jit(solution)/shard_map/concatenate | solution.py:625
  716.5 194.8 %reduce-scatter.2.cloned.1.call-done = bf16[64,6144]{1,0:T(8,128)(2,1)} async-done(((bf16[1024,6144]{1,0:T(8,128)(2,1)}), bf16[64,6144]{1,0:T(8,128)(2,1)}) %reduce-scatter.2.cloned.1.call-update) | async-done | bytes 786448 | tf_op jit(solution)/shard_map/reduce_scatter | solution.py:624
  911.4 7.0 fusion.19
  918.5 5.6 fusion.35
  924.0 39.5 %all-reduce.1 = (f32[1024]{0:T(1024)}, f32[1024]{0:T(1024)}, f32[8,32]{1,0:T(8,128)}, f32[8]{0:T(128)}) all-reduce(f32[1024]{0:T(1024)S(1)} %get-tuple-element.26, f32[1024]{0:T(1024)S(1)} %get-tuple-element.24, f32[8,32]{1,0:T(8,128)S(1)} %fusion.21, f32[8]{0:T(128)S(1)} %multiply_multiply_fusion.5), channel_id=1, replica_groups=mesh['dp'=2,'mem'=16] {'dp','mem'}, use_global_device_ids=true, to_apply=%region_17.18 | all-reduce | flops 2312 | bytes 18496 | tf_op jit(solution)/shard_map/psum | solution.py:633
  (311 shorter events, 111.4 us)
Async XLA Ops:
  7.2 355.7 %copy-start = (bf16[1024,1024]{1,0:T(8,128)(2,1)S(1)}, bf16[1024,1024]{1,0:T(8,128)(2,1)}, u32[]{:S(2)}) copy-start(bf16[1024,1024]{1,0:T(8,128)(2,1)} %param.19) | copy-start | bytes 6291460
  7.2 124.2 %all-gather.5.cloned.1.call-start = ((), (), s32[]{:S(2)}) async-start(), calls=%async_computation.4 | async-start | bytes 4456448 | tf_op jit(solution)/shard_map/all_gather | solution.py:474
  65.2 19.0 %all-to-all-start = ((s32[16,1,3072]{2,1,0:T(1,128)}), s32[16,1,3072]{2,1,0:T(1,128)S(1)}, u32[]{:S(2)}, u32[]{:S(2)}) async-start(s32[16,1,3072]{2,1,0:T(1,128)} %compare_select_fusion.1), calls=%async_computation | async-start | bytes 393216 | tf_op jit(solution)/shard_map/all_to_all | solution.py:466
  173.0 171.3 %all-to-all-start.1 = ((bf16[16,128,1152]{2,1,0:T(8,128)(2,1)}), bf16[16,128,1152]{2,1,0:T(8,128)(2,1)}, u32[]{:S(2)}, u32[]{:S(2)}) async-start(bf16[16,128,1152]{2,1,0:T(8,128)(2,1)} %bitcast.160), calls=%async_computation.1 | async-start | bytes 9437184 | tf_op jit(solution)/shard_map/all_to_all | solution.py:487
  200.7 25.9 %copy-start.71 = (s32[1,3]{1,0:T(1,128)S(1)}, s32[1,3]{1,0:T(1,128)}, u32[]{:S(2)}) copy-start(s32[1,3]{1,0:T(1,128)} %param.27) | copy-start | bytes 40
  200.7 27.4 %copy-start.60 = (f32[8,32]{1,0:T(8,128)S(1)}, f32[8,32]{1,0:T(8,128)}, u32[]{:S(2)}) copy-start(f32[8,32]{1,0:T(8,128)} %param.20) | copy-start | bytes 3076
  200.7 274.1 %all-gather.7.cloned.1.call-start = ((), (), s32[]{:S(2)}) async-start(), calls=%async_computation.5 | async-start | bytes 5013504 | tf_op jit(solution)/shard_map/all_gather | solution.py:556
  202.3 116.3 %collective-permute-start = (bf16[2,128,8,128]{3,1,2,0:T(8,128)(2,1)}, bf16[2,128,8,128]{3,1,2,0:T(8,128)(2,1)}, u32[]{:S(2)}, u32[]{:S(2)}) collective-permute-start(bf16[2,128,8,128]{3,1,2,0:T(8,128)(2,1)} %copy_dynamic-update-slice_fusion), channel_id=1, source_target_pairs={{0,4},{1,5},{2,6},{3,7},{4,8},{5,9},{6,10},{7,11},{8,12},{9,13},{1... | collective-permute-start | bytes 1572872 | tf_op jit(solution)/shard_map/ppermute | solution.py:25
  205.4 114.3 %collective-permute-start.1 = (bf16[2,128,8,128]{3,1,2,0:T(8,128)(2,1)}, bf16[2,128,8,128]{3,1,2,0:T(8,128)(2,1)}, u32[]{:S(2)}, u32[]{:S(2)}) collective-permute-start(bf16[2,128,8,128]{3,1,2,0:T(8,128)(2,1)} %copy_dynamic-update-slice_fusion), channel_id=1, source_target_pairs={{0,3},{1,4},{2,5},{3,6},{4,7},{5,8},{6,9},{7,10},{8,11},{9,12},{10... | collective-permute-start | bytes 1572872 | tf_op jit(solution)/shard_map/ppermute | solution.py:25
  209.4 112.5 %collective-permute-start.2 = (bf16[2,128,8,128]{3,1,2,0:T(8,128)(2,1)}, bf16[2,128,8,128]{3,1,2,0:T(8,128)(2,1)}, u32[]{:S(2)}, u32[]{:S(2)}) collective-permute-start(bf16[2,128,8,128]{3,1,2,0:T(8,128)(2,1)} %copy_dynamic-update-slice_fusion), channel_id=1, source_target_pairs={{0,2},{1,3},{2,4},{3,5},{4,6},{5,7},{6,8},{7,9},{8,10},{9,11},{10,... | collective-permute-start | bytes 1572872 | tf_op jit(solution)/shard_map/ppermute | solution.py:25
  212.5 125.2 %collective-permute-start.3 = (bf16[2,128,8,128]{3,1,2,0:T(8,128)(2,1)}, bf16[2,128,8,128]{3,1,2,0:T(8,128)(2,1)}, u32[]{:S(2)}, u32[]{:S(2)}) collective-permute-start(bf16[2,128,8,128]{3,1,2,0:T(8,128)(2,1)} %copy_dynamic-update-slice_fusion), channel_id=1, source_target_pairs={{0,1},{1,2},{2,3},{3,4},{4,5},{5,6},{6,7},{7,8},{8,9},{9,10},{10,1... | collective-permute-start | bytes 1572872 | tf_op jit(solution)/shard_map/ppermute | solution.py:25
  226.5 7.3 copy-start.34
  228.1 111.9 %copy-start.36 = (bf16[128,8,128]{2,0,1:T(8,128)(2,1)}, bf16[128,8,128]{2,0,1:T(8,128)(2,1)S(1)}, u32[]{:S(2)}) copy-start(bf16[128,8,128]{2,0,1:T(8,128)(2,1)S(1)} %get-tuple-element.117) | copy-start | bytes 786436
  228.1 130.5 %copy-start.38 = (bf16[128,8,128]{2,0,1:T(8,128)(2,1)}, bf16[128,8,128]{2,0,1:T(8,128)(2,1)S(1)}, u32[]{:S(2)}) copy-start(bf16[128,8,128]{2,0,1:T(8,128)(2,1)S(1)} %get-tuple-element.118) | copy-start | bytes 786436
  233.8 106.2 %copy-start.23 = (bf16[128,1024]{0,1:T(8,128)(2,1)}, bf16[128,1024]{0,1:T(8,128)(2,1)S(1)}, u32[]{:S(2)}) copy-start(bf16[128,1024]{0,1:T(8,128)(2,1)S(1)} %copy.164) | copy-start | bytes 786436
  342.0 16.7 %copy-start.56 = (f32[8,128]{1,0:T(8,128)}, f32[8,128]{1,0:T(8,128)S(1)}, u32[]{:S(2)}) copy-start(f32[8,128]{1,0:T(8,128)S(1)} %get-tuple-element.105) | copy-start | bytes 12292
  344.4 14.3 %copy-start.66 = (f32[8]{0:T(128)S(1)}, f32[8]{0:T(128)}, u32[]{:S(2)}) copy-start(f32[8]{0:T(128)} %get-tuple-element.35) | copy-start | bytes 100
  344.4 14.3 %copy-start.68 = (f32[8]{0:T(128)S(1)}, f32[8]{0:T(128)}, u32[]{:S(2)}) copy-start(f32[8]{0:T(128)} %get-tuple-element.34) | copy-start | bytes 100
  510.5 159.2 %all-to-all-start.2 = ((bf16[16,128,1024]{2,1,0:T(8,128)(2,1)}), bf16[16,128,1024]{2,1,0:T(8,128)(2,1)}, u32[]{:S(2)}, u32[]{:S(2)}) async-start(bf16[16,128,1024]{2,1,0:T(8,128)(2,1)} %bitcast.161), calls=%async_computation.2 | async-start | bytes 8388608 | tf_op jit(solution)/shard_map/all_to_all | solution.py:569
  516.1 395.2 %reduce-scatter.2.cloned.1.call-start = ((), (), s32[]{:S(2)}) async-start(), calls=%async_computation.6 | async-start | bytes 13369344 | tf_op jit(solution)/shard_map/reduce_scatter | solution.py:624
  526.2 11.9 %copy-start.8 = (f32[128,4096]{1,0:T(8,128)S(1)}, f32[128,4096]{1,0:T(8,128)}, u32[]{:S(2)}) copy-start(f32[128,4096]{1,0:T(8,128)} %copy-done.7) | copy-start | bytes 6291460
  526.3 11.9 %copy-start.28 = (f32[128,4096]{1,0:T(8,128)S(1)}, f32[128,4096]{1,0:T(8,128)}, u32[]{:S(2)}) copy-start(f32[128,4096]{1,0:T(8,128)} %get-tuple-element.33) | copy-start | bytes 6291460
  528.0 72.2 %collective-permute-start.7 = (bf16[2,128,8,128]{1,3,2,0:T(8,128)(2,1)}, bf16[2,128,8,128]{1,3,2,0:T(8,128)(2,1)}, u32[]{:S(2)}, u32[]{:S(2)}) collective-permute-start(bf16[2,128,8,128]{1,3,2,0:T(8,128)(2,1)} %get-tuple-element.45), channel_id=1, source_target_pairs={{1,0},{2,1},{3,2},{4,3},{5,4},{6,5},{7,6},{8,7},{9,8},{10,9},{11,1... | collective-permute-start | bytes 1572872 | tf_op jit(solution)/shard_map/ppermute | solution.py:25
  532.1 86.8 %collective-permute-start.6 = (bf16[2,128,8,128]{1,3,2,0:T(8,128)(2,1)}, bf16[2,128,8,128]{1,3,2,0:T(8,128)(2,1)}, u32[]{:S(2)}, u32[]{:S(2)}) collective-permute-start(bf16[2,128,8,128]{1,3,2,0:T(8,128)(2,1)} %get-tuple-element.46), channel_id=1, source_target_pairs={{2,0},{3,1},{4,2},{5,3},{6,4},{7,5},{8,6},{9,7},{10,8},{11,9},{12,... | collective-permute-start | bytes 1572872 | tf_op jit(solution)/shard_map/ppermute | solution.py:25
  534.3 96.1 %collective-permute-start.5 = (bf16[2,128,8,128]{1,3,2,0:T(8,128)(2,1)}, bf16[2,128,8,128]{1,3,2,0:T(8,128)(2,1)}, u32[]{:S(2)}, u32[]{:S(2)}) collective-permute-start(bf16[2,128,8,128]{1,3,2,0:T(8,128)(2,1)} %get-tuple-element.47), channel_id=1, source_target_pairs={{3,0},{4,1},{5,2},{6,3},{7,4},{8,5},{9,6},{10,7},{11,8},{12,9},{13... | collective-permute-start | bytes 1572872 | tf_op jit(solution)/shard_map/ppermute | solution.py:25
  536.2 126.9 %collective-permute-start.4 = (bf16[2,128,8,128]{1,3,2,0:T(8,128)(2,1)}, bf16[2,128,8,128]{1,3,2,0:T(8,128)(2,1)}, u32[]{:S(2)}, u32[]{:S(2)}) collective-permute-start(bf16[2,128,8,128]{1,3,2,0:T(8,128)(2,1)} %get-tuple-element.44), channel_id=1, source_target_pairs={{4,0},{5,1},{6,2},{7,3},{8,4},{9,5},{10,6},{11,7},{12,8},{13,9},{1... | collective-permute-start | bytes 1572872 | tf_op jit(solution)/shard_map/ppermute | solution.py:25
  682.4 8.2 copy-start.53
  682.4 7.0 collective-permute-start.9
  684.0 4.5 collective-permute-start.8
  710.2 254.4 %all-gather.9.cloned.1.call-start = ((), (), s32[]{:S(2)}) async-start(), calls=%async_computation.7 | async-start | bytes 2359296 | tf_op jit(solution)/shard_map/all_gather | solution.py:627
  713.6 197.7 %copy-start.6 = (bf16[128,4096]{1,0:T(8,128)(2,1)S(1)}, bf16[128,4096]{1,0:T(8,128)(2,1)}, u32[]{:S(2)}) copy-start(bf16[128,4096]{1,0:T(8,128)(2,1)} %multiply_convert_fusion.1) | copy-start | bytes 3145732
  918.4 45.1 %copy-start.70 = (f32[128]{0:T(128)S(1)}, f32[128]{0:T(128)}, u32[]{:S(2)}) copy-start(f32[128]{0:T(128)} %copy-done.69) | copy-start | bytes 1540
  (63 other events, 186.2 us)
Sparse Core Ops, SparseCore 0:
  14.7 77.7 all-gather.4
  382.1 92.6 all-gather.6
  710.3 200.8 reduce-scatter.1
  912.7 10.2 all-gather.8

commit v3 on v2

--- a/solution.py
+++ b/solution.py
@@ -135,8 +135,13 @@
         ),
         out_shape=[out_shape, out_shape],
         compiler_params=pltpu.CompilerParams(vmem_limit_bytes=VMEM_LIMIT),
+        cost_estimate=lasting(42),
         name="gather_rows",
     )(index, counts, memory_keys, memory_values)
+
+
+def lasting(microseconds):
+    return pl.CostEstimate(flops=0, bytes_accessed=3_000_000 * microseconds, transcendentals=0)
 
 
 def triple(stat):
@@ -245,6 +250,7 @@
         ),
         out_shape=jax.ShapeDtypeStruct((sources * rows, width + 128), jnp.bfloat16),
         compiler_params=pltpu.CompilerParams(vmem_limit_bytes=VMEM_LIMIT),
+        cost_estimate=lasting(41),
         name="memory_forward",
     )(bounds, queries, key_rows, value_rows, row_ids)
 
@@ -303,6 +309,7 @@
             jax.ShapeDtypeStruct((rows, 128), jnp.float32),
         ],
         compiler_params=pltpu.CompilerParams(vmem_limit_bytes=VMEM_LIMIT),
+        cost_estimate=lasting(13),
         name="combine_partials",
     )(partial)
 
@@ -377,8 +384,301 @@
         ),
         out_shape=jax.ShapeDtypeStruct((sources * rows, width), jnp.bfloat16),
         compiler_params=pltpu.CompilerParams(vmem_limit_bytes=VMEM_LIMIT),
+        cost_estimate=lasting(35),
         name="memory_backward",
     )(bounds, queries, grads, key_rows, value_rows, row_ids)
+
+
+def remote(source, target, send_sem, recv_sem, device):
+    return pltpu.make_async_remote_copy(
+        src_ref=source,
+        dst_ref=target,
+        send_sem=send_sem,
+        recv_sem=recv_sem,
+        device_id={"mem": device},
+        device_id_type=pl.DeviceIdType.MESH,
+    )
+
+
+def grid_place(depth):
+    me = lax.axis_index("mem")
+    layer, column = me // 4, me % 4
+    beside_x = column + 1 - 2 * (column % 2)
+    beside_y = column + 2 - 4 * (column // 2)
+    across = 3 - column
+
+    def index_of(step, place):
+        return (layer + step + depth) % depth * 4 + place
+
+    return me, column, beside_x, beside_y, across, index_of
+
+
+def greet(devices):
+    barrier = pltpu.get_barrier_semaphore()
+    for device in devices:
+        pl.semaphore_signal(
+            barrier, inc=1, device_id={"mem": device}, device_id_type=pl.DeviceIdType.MESH
+        )
+    pl.semaphore_wait(barrier, len(devices))
+
+
+def gather_group(block, sources, collective_id):
+    rows, width = block.shape
+    depth, half = sources // 4, rows // 2
+
+    def kernel(x_ref, out_ref, own_sem, send, recv_z, recv_x, recv_y, recv_a, recv_b):
+        me, column, beside_x, beside_y, across, index_of = grid_place(depth)
+        to_x, to_y = index_of(0, beside_x), index_of(0, beside_y)
+        greet([to_x, to_y] + [index_of(-k, column) for k in range(1, depth)])
+
+        def rows_of(index, part=None):
+            if part is None:
+                return out_ref.at[pl.ds(pl.multiple_of(index * rows, rows), rows), :]
+            return out_ref.at[pl.ds(pl.multiple_of(index * rows + part * half, half), half), :]
+
+        own = pltpu.make_async_copy(x_ref, rows_of(me), own_sem)
+        own.start()
+        sent = []
+
+        def push(source, target, kind, k, recv, device):
+            copy = remote(source, target, send.at[kind, k], recv.at[k], device)
+            copy.start()
+            sent.append(copy)
+
+        def arrived(target, recv, k):
+            remote(target, target, send.at[0, 0], recv.at[k], to_x).wait_recv()
+
+        push(x_ref, rows_of(me), 1, 0, recv_x, to_x)
+        push(x_ref, rows_of(me), 2, 0, recv_y, to_y)
+        for k in range(1, depth):
+            push(x_ref, rows_of(me), 0, k, recv_z, index_of(-k, column))
+
+        def pass_on(k):
+            from_x, from_y = index_of(k, beside_x), index_of(k, beside_y)
+            arrived(rows_of(from_x), recv_x, k)
+            push(rows_of(from_x, 0), rows_of(from_x, 0), 3, k, recv_a, to_y)
+            arrived(rows_of(from_y), recv_y, k)
+            push(rows_of(from_y, 1), rows_of(from_y, 1), 4, k, recv_b, to_x)
+
+        for k in range(1, depth):
+            above = index_of(k, column)
+            arrived(rows_of(above), recv_z, k)
+            push(rows_of(above), rows_of(above), 1, k, recv_x, to_x)
+            push(rows_of(above), rows_of(above), 2, k, recv_y, to_y)
+            pass_on(k - 1)
+        pass_on(depth - 1)
+        for k in range(depth):
+            far = index_of(k, across)
+            arrived(rows_of(far, 0), recv_a, k)
+            arrived(rows_of(far, 1), recv_b, k)
+        for copy in sent:
+            copy.wait_send()
+        own.wait()
+
+    return pl.pallas_call(
+        kernel,
+        in_specs=[pl.BlockSpec(memory_space=pl.ANY)],
+        out_specs=pl.BlockSpec(memory_space=pl.ANY),
+        out_shape=jax.ShapeDtypeStruct((sources * rows, width), block.dtype),
+        scratch_shapes=[pltpu.SemaphoreType.DMA, pltpu.SemaphoreType.DMA((5, depth))]
+        + [pltpu.SemaphoreType.DMA((depth,))] * 5,
+        compiler_params=pltpu.CompilerParams(
+            collective_id=collective_id, has_side_effects=True, vmem_limit_bytes=VMEM_LIMIT
+        ),
+        cost_estimate=lasting(50),
+        name="gather_group",
+    )(block)
+
+
+def reduce_group(parts, sources, collective_id, merge, pack, finish, out_shape):
+    rows, width = parts.shape[0] // sources, parts.shape[1]
+    depth, half = sources // 4, rows // 2
+    outs = len(out_shape)
+
+    def kernel(parts_ref, *refs):
+        out_refs = refs[:outs]
+        half_a, half_b, from_x, from_y, from_z, out_x, out_y, out_z = refs[outs : outs + 8]
+        send, recv_a, recv_b, recv_x, recv_y, recv_z = refs[outs + 8 :]
+        me, column, beside_x, beside_y, across, index_of = grid_place(depth)
+        to_x, to_y = index_of(0, beside_x), index_of(0, beside_y)
+        greet([to_x, to_y] + [index_of(-k, column) for k in range(1, depth)])
+        order = [*range(1, depth), 0]
+        sent = []
+
+        def piece(index, part):
+            return parts_ref.at[pl.ds(pl.multiple_of(index * rows + part * half, half), half), :]
+
+        def part_rows(part):
+            return pl.ds(part * half, half)
+
+        def push(source, target, kind, k, recv_sem, device):
+            copy = remote(source, target, send.at[kind, k], recv_sem, device)
+            copy.start()
+            sent.append(copy)
+
+        def arrived(target, recv_sem):
+            remote(target, target, send.at[0, 0], recv_sem, to_x).wait_recv()
+
+        for k in order:
+            far = index_of(k, across)
+            push(piece(far, 0), half_a.at[k], 0, k, recv_a.at[k], to_x)
+            push(piece(far, 1), half_b.at[k], 1, k, recv_b.at[k], to_y)
+        for k in order:
+            push(piece(index_of(k, beside_x), 0), from_x.at[k, part_rows(0)], 2, k, recv_x.at[0, k], to_x)
+            push(piece(index_of(k, beside_y), 1), from_y.at[k, part_rows(1)], 3, k, recv_y.at[1, k], to_y)
+        for k in order:
+            arrived(half_a.at[k], recv_a.at[k])
+            pack(out_y.at[k], merge([piece(index_of(k, beside_y), 0), half_a.at[k]]))
+            push(out_y.at[k], from_y.at[k, part_rows(0)], 4, k, recv_y.at[0, k], to_y)
+            arrived(half_b.at[k], recv_b.at[k])
+            pack(out_x.at[k], merge([piece(index_of(k, beside_x), 1), half_b.at[k]]))
+            push(out_x.at[k], from_x.at[k, part_rows(1)], 5, k, recv_x.at[1, k], to_x)
+        for k in order:
+            for part in (0, 1):
+                arrived(from_x.at[k, part_rows(part)], recv_x.at[part, k])
+                arrived(from_y.at[k, part_rows(part)], recv_y.at[part, k])
+            if k:
+                for part in (0, 1):
+                    here = part_rows(part)
+                    blocks = [piece(index_of(k, column), part), from_x.at[k, here], from_y.at[k, here]]
+                    pack(out_z.at[k, here], merge(blocks))
+                push(out_z.at[k], from_z.at[k], 6, k, recv_z.at[k], index_of(k, column))
+        for k in range(1, depth):
+            arrived(from_z.at[k], recv_z.at[k])
+        for part in (0, 1):
+            here = part_rows(part)
+            blocks = [piece(me, part), from_x.at[0, here], from_y.at[0, here]]
+            blocks += [from_z.at[k, here] for k in range(1, depth)]
+            finish([out.at[here] for out in out_refs], merge(blocks))
+        for copy in sent:
+            copy.wait_send()
+
+    def slots(size):
+        return pltpu.VMEM((depth, size, width), parts.dtype)
+
+    return pl.pallas_call(
+        kernel,
+        in_specs=[pl.BlockSpec(memory_space=pltpu.VMEM)],
+        out_specs=[pl.BlockSpec(memory_space=pltpu.VMEM)] * outs,
+        out_shape=out_shape,
+        scratch_shapes=[slots(half), slots(half), slots(rows), slots(rows), slots(rows)]
+        + [slots(half), slots(half), slots(rows)]
+        + [pltpu.SemaphoreType.DMA((7, depth))]
+        + [pltpu.SemaphoreType.DMA((depth,))] * 2
+        + [pltpu.SemaphoreType.DMA((2, depth))] * 2
+        + [pltpu.SemaphoreType.DMA((depth,))],
+        compiler_params=pltpu.CompilerParams(
+            collective_id=collective_id, has_side_effects=True, vmem_limit_bytes=VMEM_LIMIT
+        ),
+        cost_estimate=lasting(55),
+        name="reduce_group",
+    )(parts)
+
+
+def sum_blocks(parts, sources, collective_id):
+    rows, width = parts.shape[0] // sources, parts.shape[1]
+
+    def merge(blocks):
+        total = blocks[0][...].astype(jnp.float32)
+        for block in blocks[1:]:
+            total = total + block[...].astype(jnp.float32)
+        return total
+
+    def pack(target, total):
+        target[...] = total.astype(parts.dtype)
+
+    def finish(targets, total):
+        targets[0][...] = total
+
+    out_shape = [jax.ShapeDtypeStruct((rows, width), jnp.float32)]
+    return reduce_group(parts, sources, collective_id, merge, pack, finish, out_shape)[0]
+
+
+def merge_partials(parts, sources, collective_id, heads):
+    rows, width = parts.shape[0] // sources, parts.shape[1] - 128
+    head_dim = width // heads
+
+    def merge(blocks):
+        stats = []
+        for block in blocks:
+            stat = block[:, width:].astype(jnp.float32)
+            stats.append(stat + pltpu.roll(stat, 128 - 16, 1) + pltpu.roll(stat, 128 - 32, 1))
+        top = stats[0]
+        for stat in stats[1:]:
+            top = jnp.maximum(top, stat)
+        fades = [jnp.exp(stat - top) for stat in stats]
+        total = sum(fade * pltpu.roll(stat, 128 - heads, 1) for fade, stat in zip(fades, stats))
+        sums = []
+        for head in range(heads):
+            columns = slice(head * head_dim, (head + 1) * head_dim)
+            sums.append(
+                sum(
+                    block[:, columns].astype(jnp.float32) * fade[:, head : head + 1]
+                    for block, fade in zip(blocks, fades)
+                )
+            )
+        return sums, top, total
+
+    def pack(target, merged):
+        sums, top, total = merged
+        for head in range(heads):
+            target[:, head * head_dim : (head + 1) * head_dim] = sums[head].astype(parts.dtype)
+        lane = lax.broadcasted_iota(jnp.int32, top.shape, 1)
+        stat = jnp.where(lane < heads, top, jnp.where(lane < 16, pltpu.roll(total, heads, 1), 0.0))
+        target[:, width:] = triple(stat + pltpu.roll(stat, 16, 1) + pltpu.roll(stat, 32, 1))
+
+    def finish(targets, merged):
+        sums, top, total = merged
+        live = total > 0
+        total = jnp.where(live, total, 1.0)
+        targets[1][...] = jnp.where(live, top + jnp.log(total), 0.0)
+        for head in range(heads):
+            targets[0][:, head * head_dim : (head + 1) * head_dim] = sums[head] / total[:, head : head + 1]
+
+    out_shape = [
+        jax.ShapeDtypeStruct((rows, width), jnp.float32),
+        jax.ShapeDtypeStruct((rows, 128), jnp.float32),
+    ]
+    return reduce_group(parts, sources, collective_id, merge, pack, finish, out_shape)
+
+
+def weight_halves(pairs):
+    core = lax.axis_index("dp")
+    lefts, kept, sent = [], [], []
+    for left, right in pairs:
+        half = right.shape[1] // 2
+        lefts.append(left)
+        kept.append(lax.dynamic_slice_in_dim(right, core * half, half, 1))
+        sent.append(lax.dynamic_slice_in_dim(right, (1 - core) * half, half, 1))
+    other = swapped(jnp.concatenate(lefts + sent, axis=1))
+    partials, left_at, at = [], 0, sum(left.shape[1] for left in lefts)
+    for left, right in zip(lefts, kept):
+        other_left = other[:, left_at : left_at + left.shape[1]]
+        other_right = other[:, at : at + right.shape[1]]
+        left_at, at = left_at + left.shape[1], at + right.shape[1]
+        partials.append(
+            lax.dot_general(
+                jnp.concatenate([left, other_left], axis=0),
+                jnp.concatenate([right, other_right], axis=0),
+                contract_rows,
+                preferred_element_type=jnp.float32,
+            ).astype(jnp.bfloat16)
+        )
+    return jnp.concatenate(partials, axis=1)
+
+
+def scattered(halves):
+    return lax.psum_scatter(halves, "mem", scatter_dimension=0, tiled=True)
+
+
+def whole_grads(sums, widths):
+    both = lax.all_gather(sums, "dp", axis=0).astype(jnp.float32)
+    grads, at = [], 0
+    for size in widths:
+        half = size // 2
+        grads.append(jnp.concatenate([both[0, :, at : at + half], both[1, :, at : at + half]], 1))
+        at += half
+    return grads
 
 
 def on_device(
@@ -484,12 +784,17 @@
         rows,
         score_scale,
     )
-    partial = lax.all_to_all(
-        partial.reshape(groups, rows, width + 128), "mem", split_axis=0, concat_axis=0, tiled=True
-    )
-    memory_out, mem_log = combine_partials(
-        partial.reshape(groups * rows, width + 128), heads, groups, rows
-    )
+    if groups == 16:
+        memory_out, mem_log = merge_partials(partial, groups, 1, heads)
+    else:
+        partial = lax.all_to_all(
+            partial.reshape(groups, rows, width + 128),
+            "mem",
+            split_axis=0,
+            concat_axis=0,
+            tiled=True,
+        ).reshape(groups * rows, width + 128)
+        memory_out, mem_log = combine_partials(partial, heads, groups, rows)
     memory_out = memory_out.reshape(rows, heads, head_dim)
     gate_share = jax.nn.sigmoid(gate_logit)[:, None]
     mixed_heads = (
@@ -520,6 +825,7 @@
         jnp.sum(d_mixed * (memory_out - local_out), axis=(0, 2))
         * (gate_share * (1.0 - gate_share))[:, 0]
     )
+    early_halves = weight_halves([(mixed_heads, d_branch), (normed_mid, d_up), (cotangent, activated)])
     d_memory = (gate_share * d_mixed).astype(jnp.bfloat16)
     d_local_out = ((1.0 - gate_share) * d_mixed).astype(jnp.bfloat16)
     probs_again = jnp.exp(local_scores() - log_total)
@@ -553,7 +859,12 @@
         ],
         axis=1,
     )
-    all_grads = lax.all_gather(sent_grads, "mem", axis=0, tiled=True)
+    sent_grads, early_halves = lax.optimization_barrier((sent_grads, early_halves))
+    early_sums = scattered(early_halves)
+    if groups == 16:
+        all_grads = gather_group(sent_grads, groups, 2)
+    else:
+        all_grads = lax.all_gather(sent_grads, "mem", axis=0, tiled=True)
     d_partial = memory_backward(
         bounds.reshape(-1),
         all_queries,
@@ -566,13 +877,16 @@
         rows,
         score_scale,
     )
-    d_partial = lax.all_to_all(
-        d_partial.reshape(groups, rows, width), "mem", split_axis=0, concat_axis=0, tiled=True
-    )
-    d_queries = (
-        d_queries
-        + jnp.sum(d_partial.astype(jnp.float32), axis=0).reshape(rows, heads, head_dim) * score_scale
-    )
+    if groups == 16:
+        d_partial = sum_blocks(d_partial, groups, 3)
+    else:
+        d_partial = jnp.sum(
+            lax.all_to_all(
+                d_partial.reshape(groups, rows, width), "mem", split_axis=0, concat_axis=0, tiled=True
+            ).astype(jnp.float32),
+            axis=0,
+        )
+    d_queries = d_queries + d_partial.reshape(rows, heads, head_dim) * score_scale
     halo_grads = jnp.stack([d_keys_all[:W], d_values_all[:W]])
     d_tails = jnp.zeros((2, sent_rows, heads, head_dim), jnp.float32)
     for distance in range(repeats, 0, -1):
@@ -595,46 +909,19 @@
     )
     d_tokens_part, attn_gain_part = norm_in_back(d_in)
     tokens_grad = d_residual + d_tokens_part
-    core = lax.axis_index("dp")
-    lefts, rights = [], []
-    for left, right in (
-        (normed_in, d_projected),
-        (mixed_heads, d_branch),
-        (normed_mid, d_up),
-        (cotangent, activated),
-    ):
-        half = right.shape[1] // 2
-        kept = lax.dynamic_slice_in_dim(right, core * half, half, 1)
-        sent = lax.dynamic_slice_in_dim(right, (1 - core) * half, half, 1)
-        lefts.append(left)
-        rights.append((kept, sent))
-    other_left = swapped(jnp.concatenate(lefts, axis=1))
-    other_right = swapped(jnp.concatenate([sent for _, sent in rights], axis=1))
-    partials, at = [], 0
-    for i, (left, (kept, _)) in enumerate(zip(lefts, rights)):
-        half = kept.shape[1]
-        left_both = jnp.concatenate([left, other_left[:, i * width : (i + 1) * width]], axis=0)
-        right_both = jnp.concatenate([kept, other_right[:, at : at + half]], axis=0)
-        at += half
-        partials.append(
-            lax.dot_general(
-                left_both, right_both, contract_rows, preferred_element_type=jnp.float32
-            ).astype(jnp.bfloat16)
-        )
-    summed = lax.psum_scatter(
-        jnp.concatenate(partials, axis=1), "mem", scatter_dimension=0, tiled=True
-    )
-    halves = lax.all_gather(summed, "dp", axis=0).astype(jnp.float32)
-    grads, at = [], 0
-    for kept, _ in rights:
-        half = kept.shape[1]
-        grads.append(jnp.concatenate([halves[0, :, at : at + half], halves[1, :, at : at + half]], 1))
-        at += half
+    late_halves = weight_halves([(normed_in, d_projected)])
+    late_halves, early_sums = lax.optimization_barrier((late_halves, early_sums))
+    late_sums = scattered(late_halves)
+    out_grad, up_grad, down_grad = whole_grads(early_sums, [width, hidden, hidden])
+    qkv_grad = whole_grads(late_sums, [3 * width])[0]
     small_sums = lax.psum((attn_gain_part, ffn_gain_part, bias_part, gate_part), ("dp", "mem"))
     return (
         block_out,
         tokens_grad,
-        *grads,
+        qkv_grad,
+        out_grad,
+        up_grad,
+        down_grad,
         small_sums[0],
         small_sums[1],
         small_sums[2],

time: 989 us -> 778 us (0.79)
  waiting for transfers between devices: 518 us -> 169 us
  Pallas kernels: 133 us -> 314 us
  starting transfers between devices: 75.3 us -> 31.9 us
    pallas_call x1 -> x3, Pallas kernels: 13 us -> 181 us  [the longest x2 132 us: reduce_group(): pl.pallas_call(kernel, in_specs=[pl.BlockSpec(memory_space=pltpu.VMEM)],...]
    ppermute x8, waiting for transfers between devices: 214 us -> 84.3 us  [passed_along(): return lax.ppermute(value, axis, pairs)]
    reduce_scatter x1 -> x2, waiting for transfers between devices: 195 us -> 82.5 us  [scattered(): return lax.psum_scatter(halves, 'mem', scatter_dimension=0, tiled=True)]
    all_gather x2 -> x1, waiting for transfers between devices: 92.8 us -> 0.01 us  [whole_grads(): both = lax.all_gather(sums, 'dp', axis=0).astype(jnp.float32)]
    all_to_all x2 -> x0, starting transfers between devices: 33.2 us -> none  [the longest x1 27.7 us: on_device(): lax.all_to_all(partial.reshape(groups, rows, width + 128), 'mem', split_a...]
    pallas_call x1, Pallas kernels: 42.9 us -> 55.7 us  [gather_rows(): pl.pallas_call(kernel, grid_spec=pltpu.PrefetchScalarGridSpec(num_scalar_...]
    all_to_all x1, waiting for transfers between devices: 12.4 us -> 0.01 us  [on_device(): lax.all_to_all(requests, 'mem', split_axis=0, concat_axis=0, tiled=True)]
    ppermute x8, starting transfers between devices: 33.5 us -> 21.9 us  [passed_along(): return lax.ppermute(value, axis, pairs)]
  transfers between devices with their start and end apart: 17 -> 15, of which waited for: 11 -> 6; matrix products, arithmetic and copies ran while one was open for 9% -> 13% of each run, Pallas kernels for 4% -> 26%
where the time goes in v3:
time: 778 us; the launch traced here: 764 us
  Pallas kernels  314 us (40%)
  waiting for transfers between devices  169 us (22%)
  matrix products  59 us (8%)
  local copies, waits for them, and re-layouts  51.6 us (7%)
  other arithmetic  50 us (6%)
  blocking collectives  44.5 us (6%)
  between operations  44.4 us (6%)
  starting transfers between devices  31.9 us (4%)
    pallas_call x2, Pallas kernels, reduce_group(): pl.pallas_call(kernel, in_specs=[pl.BlockSpec(memory_space=pltpu.VMEM)],...  132 us
    ppermute x8, waiting for transfers between devices, passed_along(): return lax.ppermute(value, axis, pairs)  84.3 us
    reduce_scatter x2, waiting for transfers between devices, scattered(): return lax.psum_scatter(halves, 'mem', scatter_dimension=0, tiled=True)  82.5 us
    pallas_call x1, Pallas kernels, gather_rows(): pl.pallas_call(kernel, grid_spec=pltpu.PrefetchScalarGridSpec(num_scalar_...  55.7 us
    pallas_call x1, Pallas kernels, gather_group(): pl.pallas_call(kernel, in_specs=[pl.BlockSpec(memory_space=pl.ANY)], out_...  48.7 us
    pallas_call x1, Pallas kernels, memory_forward(): pl.pallas_call(kernel, grid_spec=pltpu.PrefetchScalarGridSpec(num_scalar_...  41.8 us
    psum x1, blocking collectives, on_device(): lax.psum((attn_gain_part, ffn_gain_part, bias_part, gate_part), ('dp', 'm...  40.2 us
    pallas_call x1, Pallas kernels, memory_backward(): pl.pallas_call(kernel, grid_spec=pltpu.PrefetchScalarGridSpec(num_scalar_...  35.6 us
  transfers between devices with their start and end apart: 15, of which 6 were waited for; matrix products, arithmetic and copies ran while one was open for 13% of the time, Pallas kernels for 26%

profile of v3, /device:TPU:9, one launch (start us, length us, event | category | flops | bytes accessed | tf_op | source)
XLA Modules:
  0.0 764.3 jit_solution(15302420871192372676)
XLA Ops:
  10.6 3.9 convolution_convert_fusion.3
  17.2 3.1 collective-permute-start.3
  20.3 3.1 collective-permute-start.2
  23.5 4.1 collective-permute-start.1
  27.6 3.2 collective-permute-start
  31.8 17.6 %sort.23 = (s32[32768]{0:T(1024)S(1)}, s32[32768]{0:T(1024)S(1)}, s32[32768]{0:T(1024)}) sort(s32[32768]{0:T(1024)S(1)} %reshape.596, s32[32768]{0:T(1024)S(1)} %reshape.597, s32[32768]{0:T(1024)S(1)} %iota.71), dimensions={0}, to_apply=%region_0.0 | sort | flops 491520 | bytes 786432 | tf_op jit(solution)/shard_map/sort | solution.py:61
  81.2 4.3 all-to-all-start
  87.0 5.5 fusion
  93.2 3.8 copy.143
  102.4 55.7 %gather_rows.1 = (bf16[49152,128]{1,0:T(8,128)(2,1)}, bf16[49152,128]{1,0:T(8,128)(2,1)}) custom-call(s32[49152]{0:T(1024)} %fusion.82.index_ref, s32[16]{0:T(128)} %slice_bitcast_fusion.16.counts_ref, bf16[4096,1024]{1,0:T(8,128)(2,1)} %keys.1, bf16[4096,1024]{1,0:T(8,128)(2,1)} %values.1), custom_call_target="tpu_custom_call" | custom-call | bytes 126000000 | tf_op jit(solution)/shard_map/gather_rows/pallas_call | solution.py:122
  168.2 41.8 %memory_forward.1.parts_ref = bf16[2048,1152]{1,0:T(8,128)(2,1)} custom-call(s32[144]{0:T(256)} %reshape.598.bounds_ref, bf16[2048,1024]{1,0:T(8,128)(2,1)} %all-gather.5.cloned.1.call-done.q_ref, bf16[49152,128]{1,0:T(8,128)(2,1)} %get-tuple-element.24.k_ref, bf16[49152,128]{1,0:T(8,128)(2,1)} %get-tuple-element.25.v_ref, s32[16,1,3072]{2,1,0:T(1,128)} %and_select_fusion.id_ref), custom_call_target="tpu_custom_call" | custom-call | bytes 123000000 | tf_op jit(solution)/shard_map/memory_forward/pallas_call | solution.py:233
  210.0 71.6 %reduce_group.2 = (f32[128,1024]{1,0:T(8,128)}, f32[128,128]{1,0:T(8,128)}) custom-call(bf16[2048,1152]{1,0:T(8,128)(2,1)} %memory_forward.1.parts_ref), custom_call_target="tpu_custom_call" | custom-call | bytes 165000000 | tf_op jit(solution)/shard_map/reduce_group/pallas_call | solution.py:559
  282.9 4.1 add_convert_fusion.1
  292.0 4.8 fusion.111
  296.8 6.8 add_convert_fusion
  304.0 3.0 multiply_reduce_fusion.2
  327.4 4.6 pad_maximum_fusion
  353.0 19.4 %collective-permute-done.5 = bf16[2,128,8,128]{1,3,2,0:T(8,128)(2,1)} collective-permute-done((bf16[2,128,8,128]{1,3,2,0:T(8,128)(2,1)}, bf16[2,128,8,128]{1,3,2,0:T(8,128)(2,1)}, u32[]{:S(2)}, u32[]{:S(2)}) %collective-permute-start.5) | collective-permute-done | bytes 524320 | tf_op jit(solution)/shard_map/ppermute | solution.py:25
  372.5 21.4 %collective-permute-done.8 = bf16[2,128,8,128]{1,3,2,0:T(8,128)(2,1)} collective-permute-done((bf16[2,128,8,128]{1,3,2,0:T(8,128)(2,1)}, bf16[2,128,8,128]{1,3,2,0:T(8,128)(2,1)}, u32[]{:S(2)}, u32[]{:S(2)}) %collective-permute-start.8) | collective-permute-done | bytes 524320 | tf_op jit(solution)/shard_map/ppermute | solution.py:25
  393.8 22.7 %collective-permute-done.7 = bf16[2,128,8,128]{1,3,2,0:T(8,128)(2,1)} collective-permute-done((bf16[2,128,8,128]{1,3,2,0:T(8,128)(2,1)}, bf16[2,128,8,128]{1,3,2,0:T(8,128)(2,1)}, u32[]{:S(2)}, u32[]{:S(2)}) %collective-permute-start.7) | collective-permute-done | bytes 524320 | tf_op jit(solution)/shard_map/ppermute | solution.py:25
  416.5 20.8 %collective-permute-done.6 = bf16[2,128,8,128]{1,3,2,0:T(8,128)(2,1)} collective-permute-done((bf16[2,128,8,128]{1,3,2,0:T(8,128)(2,1)}, bf16[2,128,8,128]{1,3,2,0:T(8,128)(2,1)}, u32[]{:S(2)}, u32[]{:S(2)}) %collective-permute-start.6) | collective-permute-done | bytes 524320 | tf_op jit(solution)/shard_map/ppermute | solution.py:25
  444.0 48.7 %gather_group.1.g_ref = bf16[2048,1152]{1,0:T(8,128)(2,1)} custom-call(bf16[128,1152]{1,0:T(8,128)(2,1)} %concatenate.90.x_ref), custom_call_target="tpu_custom_call" | custom-call | bytes 150000000 | tf_op jit(solution)/shard_map/gather_group/pallas_call | solution.py:478
  492.7 35.6 %memory_backward.1.parts_ref = bf16[2048,1024]{1,0:T(8,128)(2,1)} custom-call(s32[144]{0:T(256)} %reshape.598.bounds_ref, bf16[2048,1024]{1,0:T(8,128)(2,1)} %all-gather.5.cloned.1.call-done.q_ref, bf16[2048,1152]{1,0:T(8,128)(2,1)} %gather_group.1.g_ref, bf16[49152,128]{1,0:T(8,128)(2,1)} %get-tuple-element.24.k_ref, ...), custom_call_target="tpu_custom_call" | custom-call | bytes 105000000 | tf_op jit(solution)/shard_map/memory_backward/pallas_call | solution.py:370
  528.3 60.3 %reduce_group.3 = f32[128,1024]{1,0:T(8,128)} custom-call(bf16[2048,1024]{1,0:T(8,128)(2,1)} %memory_backward.1.parts_ref), custom_call_target="tpu_custom_call" | custom-call | bytes 165000000 | tf_op jit(solution)/shard_map/reduce_group/pallas_call | solution.py:559
  592.6 2.7 fusion.20
  598.4 3.9 collective-permute-start.9
  604.1 2.7 convolution_convert_fusion
  610.8 2.9 fusion.21
  613.8 7.5 fusion.19
  623.8 40.2 %all-reduce.1 = (f32[1024]{0:T(1024)}, f32[1024]{0:T(1024)}, f32[8,32]{1,0:T(8,128)}, f32[8]{0:T(128)}) all-reduce(f32[1024]{0:T(1024)S(1)} %get-tuple-element.34, f32[1024]{0:T(1024)S(1)} %get-tuple-element.32, f32[8,32]{1,0:T(8,128)S(1)} %fusion.21, f32[8]{0:T(128)S(1)} %multiply_multiply_fusion.5), channel_id=1, replica_groups=mesh['dp'=2,'mem'=16] {'dp','mem'}, use_global_device_ids=true, to_apply=%region_17.18 | all-reduce | flops 2312 | bytes 18496 | tf_op jit(solution)/shard_map/psum | solution.py:917
  669.6 82.5 %reduce-scatter.5.cloned.1.call-done = bf16[64,1536]{1,0:T(8,128)(2,1)} async-done(((bf16[1024,1536]{1,0:T(8,128)(2,1)}), bf16[64,1536]{1,0:T(8,128)(2,1)}) %reduce-scatter.5.cloned.1.call-update) | async-done | bytes 196624 | tf_op jit(solution)/shard_map/reduce_scatter | solution.py:671
  752.0 4.3 all-gather
  (285 shorter events, 103.3 us)
Async XLA Ops:
  7.2 280.7 %copy-start = (bf16[1024,1024]{1,0:T(8,128)(2,1)S(1)}, bf16[1024,1024]{1,0:T(8,128)(2,1)}, u32[]{:S(2)}) copy-start(bf16[1024,1024]{1,0:T(8,128)(2,1)} %param.19) | copy-start | bytes 6291460
  7.2 161.0 %all-gather.5.cloned.1.call-start = ((), (), s32[]{:S(2)}) async-start(), calls=%async_computation.3 | async-start | bytes 4456448 | tf_op jit(solution)/shard_map/all_gather | solution.py:774
  14.5 16.4 %copy-start.37 = (s32[128,8,32,1]{0,3,2,1:T(1,128)S(1)}, s32[128,8,32,1]{0,3,2,1:T(1,128)}, u32[]{:S(2)}) copy-start(s32[128,8,32,1]{0,3,2,1:T(1,128)} %param.28) | copy-start | bytes 393220
  14.5 16.4 %copy-start.38 = (s32[128,8,32]{0,2,1:T(8,128)S(1)}, s32[128,8,32]{0,2,1:T(8,128)}, u32[]{:S(2)}) copy-start(s32[128,8,32]{0,2,1:T(8,128)} %param.30) | copy-start | bytes 393220
  15.6 15.7 %copy-start.39 = (s32[128,8,32]{0,2,1:T(8,128)S(1)}, s32[128,8,32]{0,2,1:T(8,128)}, u32[]{:S(2)}) copy-start(s32[128,8,32]{0,2,1:T(8,128)} %param.29) | copy-start | bytes 393220
  17.2 144.2 %collective-permute-start.3 = (bf16[2,128,8,128]{3,1,2,0:T(8,128)(2,1)}, bf16[2,128,8,128]{3,1,2,0:T(8,128)(2,1)}, u32[]{:S(2)}, u32[]{:S(2)}) collective-permute-start(bf16[2,128,8,128]{3,1,2,0:T(8,128)(2,1)} %copy_dynamic-update-slice_fusion), channel_id=1, source_target_pairs={{0,1},{1,2},{2,3},{3,4},{4,5},{5,6},{6,7},{7,8},{8,9},{9,10},{10,1... | collective-permute-start | bytes 1572872 | tf_op jit(solution)/shard_map/ppermute | solution.py:25
  20.3 140.0 %collective-permute-start.2 = (bf16[2,128,8,128]{3,1,2,0:T(8,128)(2,1)}, bf16[2,128,8,128]{3,1,2,0:T(8,128)(2,1)}, u32[]{:S(2)}, u32[]{:S(2)}) collective-permute-start(bf16[2,128,8,128]{3,1,2,0:T(8,128)(2,1)} %copy_dynamic-update-slice_fusion), channel_id=1, source_target_pairs={{0,2},{1,3},{2,4},{3,5},{4,6},{5,7},{6,8},{7,9},{8,10},{9,11},{10,... | collective-permute-start | bytes 1572872 | tf_op jit(solution)/shard_map/ppermute | solution.py:25
  23.5 135.7 %collective-permute-start.1 = (bf16[2,128,8,128]{3,1,2,0:T(8,128)(2,1)}, bf16[2,128,8,128]{3,1,2,0:T(8,128)(2,1)}, u32[]{:S(2)}, u32[]{:S(2)}) collective-permute-start(bf16[2,128,8,128]{3,1,2,0:T(8,128)(2,1)} %copy_dynamic-update-slice_fusion), channel_id=1, source_target_pairs={{0,3},{1,4},{2,5},{3,6},{4,7},{5,8},{6,9},{7,10},{8,11},{9,12},{10... | collective-permute-start | bytes 1572872 | tf_op jit(solution)/shard_map/ppermute | solution.py:25
  27.6 130.5 %collective-permute-start = (bf16[2,128,8,128]{3,1,2,0:T(8,128)(2,1)}, bf16[2,128,8,128]{3,1,2,0:T(8,128)(2,1)}, u32[]{:S(2)}, u32[]{:S(2)}) collective-permute-start(bf16[2,128,8,128]{3,1,2,0:T(8,128)(2,1)} %copy_dynamic-update-slice_fusion), channel_id=1, source_target_pairs={{0,4},{1,5},{2,6},{3,7},{4,8},{5,9},{6,10},{7,11},{8,12},{9,13},{1... | collective-permute-start | bytes 1572872 | tf_op jit(solution)/shard_map/ppermute | solution.py:25
  31.4 54.2 %copy-start.56 = (s32[1,3]{1,0:T(1,128)S(1)}, s32[1,3]{1,0:T(1,128)}, u32[]{:S(2)}) copy-start(s32[1,3]{1,0:T(1,128)} %param.27) | copy-start | bytes 40
  81.2 17.0 %all-to-all-start = ((s32[16,1,3072]{2,1,0:T(1,128)}), s32[16,1,3072]{2,1,0:T(1,128)S(1)}, u32[]{:S(2)}, u32[]{:S(2)}) async-start(s32[16,1,3072]{2,1,0:T(1,128)} %compare_select_fusion.1), calls=%async_computation | async-start | bytes 393216 | tf_op jit(solution)/shard_map/all_to_all | solution.py:766
  85.5 521.2 %reduce-scatter.3.cloned.1.call-start = ((), (), s32[]{:S(2)}) async-start(), calls=%async_computation.4 | async-start | bytes 10027008 | tf_op jit(solution)/shard_map/reduce_scatter | solution.py:671
  86.6 10.5 %copy-start.24 = (s32[128,640]{0,1:T(8,128)}, s32[128,640]{0,1:T(8,128)S(1)}, u32[]{:S(2)}) copy-start(s32[128,640]{0,1:T(8,128)S(1)} %copy.142) | copy-start | bytes 983044
  93.2 70.6 %copy-start.19 = (bf16[128,1024]{0,1:T(8,128)(2,1)}, bf16[128,1024]{0,1:T(8,128)(2,1)S(1)}, u32[]{:S(2)}) copy-start(bf16[128,1024]{0,1:T(8,128)(2,1)S(1)} %copy.167) | copy-start | bytes 786436
  98.2 65.6 %copy-start.26 = (bf16[128,8,128]{2,0,1:T(8,128)(2,1)}, bf16[128,8,128]{2,0,1:T(8,128)(2,1)S(1)}, u32[]{:S(2)}) copy-start(bf16[128,8,128]{2,0,1:T(8,128)(2,1)S(1)} %get-tuple-element.126) | copy-start | bytes 786436
  98.2 184.7 %copy-start.28 = (bf16[128,8,128]{2,0,1:T(8,128)(2,1)}, bf16[128,8,128]{2,0,1:T(8,128)(2,1)S(1)}, u32[]{:S(2)}) copy-start(bf16[128,8,128]{2,0,1:T(8,128)(2,1)S(1)} %get-tuple-element.127) | copy-start | bytes 786436
  165.8 117.1 %copy-start.42 = (f32[8,128]{1,0:T(8,128)}, f32[8,128]{1,0:T(8,128)S(1)}, u32[]{:S(2)}) copy-start(f32[8,128]{1,0:T(8,128)S(1)} %get-tuple-element.114) | copy-start | bytes 12292
  209.9 72.9 %copy-start.49 = (f32[8]{0:T(128)S(1)}, f32[8]{0:T(128)}, u32[]{:S(2)}) copy-start(f32[8]{0:T(128)} %get-tuple-element.45) | copy-start | bytes 100
  210.0 72.9 %copy-start.52 = (f32[8]{0:T(128)S(1)}, f32[8]{0:T(128)}, u32[]{:S(2)}) copy-start(f32[8]{0:T(128)} %get-tuple-element.44) | copy-start | bytes 100
  292.0 11.9 %slice-start = ((s8[8388608]{0:T(1024)(128)(4,1)}), s8[4194304]{0:T(1024)(128)(4,1)S(1)}, s32[]{:S(2)}) async-start(s8[8388608]{0:T(1024)(128)(4,1)} %bitcast.151), calls=%async_computation.7 | async-start | bytes 8388608
  310.5 7.1 collective-permute-start.4
  332.1 333.0 %all-gather.7.cloned.1.call-start = ((), (), s32[]{:S(2)}) async-start(), calls=%async_computation.6 | async-start | bytes 1769472 | tf_op jit(solution)/shard_map/all_gather | solution.py:675
  344.6 27.8 %collective-permute-start.5 = (bf16[2,128,8,128]{1,3,2,0:T(8,128)(2,1)}, bf16[2,128,8,128]{1,3,2,0:T(8,128)(2,1)}, u32[]{:S(2)}, u32[]{:S(2)}) collective-permute-start(bf16[2,128,8,128]{1,3,2,0:T(8,128)(2,1)} %get-tuple-element.52), channel_id=1, source_target_pairs={{4,0},{5,1},{6,2},{7,3},{8,4},{9,5},{10,6},{11,7},{12,8},{13,9},{1... | collective-permute-start | bytes 1572872 | tf_op jit(solution)/shard_map/ppermute | solution.py:25
  346.5 47.3 %collective-permute-start.8 = (bf16[2,128,8,128]{1,3,2,0:T(8,128)(2,1)}, bf16[2,128,8,128]{1,3,2,0:T(8,128)(2,1)}, u32[]{:S(2)}, u32[]{:S(2)}) collective-permute-start(bf16[2,128,8,128]{1,3,2,0:T(8,128)(2,1)} %get-tuple-element.53), channel_id=1, source_target_pairs={{1,0},{2,1},{3,2},{4,3},{5,4},{6,5},{7,6},{8,7},{9,8},{10,9},{11,1... | collective-permute-start | bytes 1572872 | tf_op jit(solution)/shard_map/ppermute | solution.py:25
  348.5 68.0 %collective-permute-start.7 = (bf16[2,128,8,128]{1,3,2,0:T(8,128)(2,1)}, bf16[2,128,8,128]{1,3,2,0:T(8,128)(2,1)}, u32[]{:S(2)}, u32[]{:S(2)}) collective-permute-start(bf16[2,128,8,128]{1,3,2,0:T(8,128)(2,1)} %get-tuple-element.54), channel_id=1, source_target_pairs={{2,0},{3,1},{4,2},{5,3},{6,4},{7,5},{8,6},{9,7},{10,8},{11,9},{12,... | collective-permute-start | bytes 1572872 | tf_op jit(solution)/shard_map/ppermute | solution.py:25
  351.1 86.3 %collective-permute-start.6 = (bf16[2,128,8,128]{1,3,2,0:T(8,128)(2,1)}, bf16[2,128,8,128]{1,3,2,0:T(8,128)(2,1)}, u32[]{:S(2)}, u32[]{:S(2)}) collective-permute-start(bf16[2,128,8,128]{1,3,2,0:T(8,128)(2,1)} %get-tuple-element.55), channel_id=1, source_target_pairs={{3,0},{4,1},{5,2},{6,3},{7,4},{8,5},{9,6},{10,7},{11,8},{12,9},{13... | collective-permute-start | bytes 1572872 | tf_op jit(solution)/shard_map/ppermute | solution.py:25
  598.4 5.6 collective-permute-start.9
  606.8 145.2 %reduce-scatter.5.cloned.1.call-start = ((), (), s32[]{:S(2)}) async-start(), calls=%async_computation.5 | async-start | bytes 3342336 | tf_op jit(solution)/shard_map/reduce_scatter | solution.py:671
  609.3 12.0 %slice-start.2 = ((s8[6291456]{0:T(1024)(128)(4,1)}), s8[4194304]{0:T(1024)(128)(4,1)S(1)}, s32[]{:S(2)}) async-start(s8[6291456]{0:T(1024)(128)(4,1)} %bitcast.153), calls=%async_computation.9 | async-start | bytes 8388608
  621.4 42.5 %copy-start.55 = (f32[128]{0:T(128)S(1)}, f32[128]{0:T(128)}, u32[]{:S(2)}) copy-start(f32[128]{0:T(128)} %copy-done.54) | copy-start | bytes 1540
  621.4 42.5 %copy-start.48 = (f32[128]{0:T(128)S(1)}, f32[128]{0:T(128)}, u32[]{:S(2)}) copy-start(f32[128]{0:T(128)} %copy-done.47) | copy-start | bytes 1540
  668.5 88.8 %copy-start.1 = (bf16[1024,1024]{1,0:T(8,128)(2,1)S(1)}, bf16[1024,1024]{1,0:T(8,128)(2,1)}, u32[]{:S(2)}) copy-start(bf16[1024,1024]{1,0:T(8,128)(2,1)} %param.19) | copy-start | bytes 6291460
  (47 other events, 176.5 us)
Sparse Core Ops, SparseCore 0:
  30.9 87.0 all-gather.4
  332.2 229.1 reduce-scatter.2
  606.9 10.1 all-gather.6
  622.7 129.2 reduce-scatter.4

commit v4 on v3

--- a/solution.py
+++ b/solution.py
@@ -74,12 +74,6 @@
     )
     used = jnp.arange(capacity, dtype=jnp.int32)[None, :] < (ends - starts)[:, None]
     return jnp.where(used, lists, heads * rows * slots)
-
-
-def split3(stat):
-    high = lax.reduce_precision(stat, 8, 7)
-    middle = lax.reduce_precision(stat - high, 8, 7)
-    return jnp.concatenate([high, middle, stat - high - middle], axis=1).astype(jnp.bfloat16)
 
 
 def gather_rows(index, counts, memory_keys, memory_values, heads, sources, capacity):
@@ -322,14 +316,10 @@
     def kernel(bounds_ref, q_ref, g_ref, k_ref, v_ref, id_ref, out_ref, sums):
         source = pl.program_id(0)
         token = lax.broadcasted_iota(jnp.int32, (rows, span), 0)
-        stat = g_ref[:, width : width + 128].astype(jnp.float32)
+        stat = joined_tile(g_ref[:, width : width + 128])
 
         def term(column):
-            return (
-                stat[:, column : column + 1]
-                + stat[:, column + 16 : column + 17]
-                + stat[:, column + 32 : column + 33]
-            )
+            return stat[:, column : column + 1]
 
         def part_of(head, start, least):
             here = pl.ds(pl.multiple_of(start, 128), span)
@@ -671,14 +661,371 @@
     return lax.psum_scatter(halves, "mem", scatter_dimension=0, tiled=True)
 
 
-def whole_grads(sums, widths):
-    both = lax.all_gather(sums, "dp", axis=0).astype(jnp.float32)
+def whole_grads(both, widths):
+    both = both.astype(jnp.float32)
     grads, at = [], 0
     for size in widths:
         half = size // 2
         grads.append(jnp.concatenate([both[0, :, at : at + half], both[1, :, at : at + half]], 1))
         at += half
     return grads
+
+
+def lane_tile(columns, rows):
+    lane = lax.broadcasted_iota(jnp.int32, (rows, 128), 1)
+    tile = jnp.zeros((rows, 128), jnp.float32)
+    for i, column in enumerate(columns):
+        tile = jnp.where(lane == i, column, tile)
+    return tile
+
+
+def split_tile(tile):
+    lane = lax.broadcasted_iota(jnp.int32, tile.shape, 1)
+    kept = jnp.where(lane < 32, tile, 0.0)
+    kept = kept + pltpu.roll(kept, 32, 1) + pltpu.roll(kept, 64, 1)
+    high = kept.astype(jnp.bfloat16).astype(jnp.float32)
+    middle = (kept - high).astype(jnp.bfloat16).astype(jnp.float32)
+    low = kept - high - middle
+    part = lane // 32
+    return jnp.where(part == 0, high, jnp.where(part == 1, middle, low)).astype(jnp.bfloat16)
+
+
+def joined_tile(tile):
+    tile = tile.astype(jnp.float32)
+    return tile + pltpu.roll(tile, 128 - 32, 1) + pltpu.roll(tile, 128 - 64, 1)
+
+
+def slanted(base, rows):
+    return pltpu.roll(jnp.broadcast_to(base, (rows, base.shape[1])), 0, 1, stride=1, stride_axis=0)
+
+
+def local_forward(base, book_column, book_row, own, halos, heads, score_scale):
+    rows, width = own.shape[0], own.shape[1] // 3
+    head_dim = width // heads
+    count = len(halos) + 1
+
+    def kernel(base_ref, column_ref, row_ref, own_ref, *refs):
+        halo_refs, (out_ref, log_ref) = refs[: count - 1], refs[count - 1 :]
+        same = column_ref[:, :1] == row_ref[:1, :]
+        logs = []
+        for head in range(heads):
+            columns = slice(head * head_dim, (head + 1) * head_dim)
+            above = slice(width + head * head_dim, width + (head + 1) * head_dim)
+            twice = slice(2 * width + head * head_dim, 2 * width + (head + 1) * head_dim)
+            keys = [ref[:, columns] for ref in halo_refs] + [own_ref[:, above]]
+            values = [ref[:, above] for ref in halo_refs] + [own_ref[:, twice]]
+            q = own_ref[:, columns]
+            raw = [
+                lax.dot_general(q, k, contract_cols, preferred_element_type=jnp.float32) for k in keys
+            ]
+            bias = slanted(base_ref[head : head + 1, :], rows)[:, : count * rows]
+            scores = jnp.concatenate(raw, axis=1) * score_scale + bias
+            scores = jnp.where(same, scores, masked_score)
+            top = jnp.max(scores, axis=1, keepdims=True)
+            weights = jnp.exp(scores - top)
+            total = jnp.sum(weights, axis=1, keepdims=True)
+            weights = (weights / total).astype(jnp.bfloat16)
+            out_ref[:, columns] = sum(
+                jnp.dot(
+                    weights[:, i * rows : (i + 1) * rows], v, preferred_element_type=jnp.float32
+                )
+                for i, v in enumerate(values)
+            )
+            logs.append(top + jnp.log(total))
+        log_ref[...] = lane_tile(logs, rows)
+
+    return pl.pallas_call(
+        kernel,
+        out_shape=[
+            jax.ShapeDtypeStruct((rows, width), jnp.float32),
+            jax.ShapeDtypeStruct((rows, 128), jnp.float32),
+        ],
+        compiler_params=pltpu.CompilerParams(vmem_limit_bytes=VMEM_LIMIT),
+        cost_estimate=lasting(10),
+        name="local_forward",
+    )(base, book_column, book_row, own, *halos)
+
+
+def local_queries(
+    base, book_column, book_row, own, halos, d_mixed, memory_out, local_out, mem_log, local_log, share, heads, score_scale
+):
+    rows, width = d_mixed.shape
+    head_dim = width // heads
+    count = len(halos) + 1
+    span = base.shape[1]
+
+    def kernel(
+        base_ref, column_ref, row_ref, own_ref, mix_ref, mem_ref, loc_ref, mem_log_ref, log_ref, share_ref, *refs
+    ):
+        halo_refs, (dq_ref, diagonal_ref, gate_ref, sent_ref) = refs[: count - 1], refs[count - 1 :]
+        same = column_ref[:, :1] == row_ref[:1, :]
+        turned = (
+            lax.broadcasted_iota(jnp.int32, (rows, rows), 0)
+            + lax.broadcasted_iota(jnp.int32, (rows, rows), 1)
+            == rows - 1
+        ).astype(jnp.bfloat16)
+        mem_deltas, deltas = [], []
+        for head in range(heads):
+            columns = slice(head * head_dim, (head + 1) * head_dim)
+            above = slice(width + head * head_dim, width + (head + 1) * head_dim)
+            twice = slice(2 * width + head * head_dim, 2 * width + (head + 1) * head_dim)
+            keys = [ref[:, columns] for ref in halo_refs] + [own_ref[:, above]]
+            values = [ref[:, above] for ref in halo_refs] + [own_ref[:, twice]]
+            q = own_ref[:, columns]
+            share_here = share_ref[head]
+            d_mix, mem_here, loc_here = mix_ref[:, columns], mem_ref[:, columns], loc_ref[:, columns]
+            d_mem = (share_here * d_mix).astype(jnp.bfloat16)
+            d_out = ((1.0 - share_here) * d_mix).astype(jnp.bfloat16)
+            sent_ref[:, columns] = d_mem
+            mem_deltas.append(
+                jnp.sum(d_mem.astype(jnp.float32) * mem_here, axis=1, keepdims=True)
+            )
+            delta = jnp.sum(d_out.astype(jnp.float32) * loc_here, axis=1, keepdims=True)
+            deltas.append(delta)
+            gate_ref[head : head + 1, :] = jnp.sum(
+                d_mix * (mem_here - loc_here), axis=0, keepdims=True
+            )
+            raw = [
+                lax.dot_general(q, k, contract_cols, preferred_element_type=jnp.float32) for k in keys
+            ]
+            bias = slanted(base_ref[head : head + 1, :], rows)[:, : count * rows]
+            scores = jnp.concatenate(raw, axis=1) * score_scale + bias
+            probs = jnp.exp(jnp.where(same, scores - log_ref[:, head : head + 1], masked_score))
+            products = [
+                lax.dot_general(d_out, v, contract_cols, preferred_element_type=jnp.float32)
+                for v in values
+            ]
+            slopes = (probs * (jnp.concatenate(products, axis=1) - delta)).astype(jnp.bfloat16)
+            slope_blocks = [slopes[:, i * rows : (i + 1) * rows] for i in range(count)]
+            dq_ref[:, columns] = score_scale * sum(
+                jnp.dot(s, k, preferred_element_type=jnp.float32) for s, k in zip(slope_blocks, keys)
+            )
+            mirrored = [
+                jnp.dot(s, turned, preferred_element_type=jnp.float32) for s in slope_blocks[::-1]
+            ]
+            mirrored.append(jnp.zeros((rows, span - count * rows), jnp.float32))
+            leaned = pltpu.roll(jnp.concatenate(mirrored, axis=1), 0, 1, stride=1, stride_axis=0)
+            diagonal_ref[head : head + 1, :] = jnp.sum(leaned, axis=0, keepdims=True)
+        mem_logs = [mem_log_ref[:, head : head + 1] for head in range(heads)]
+        logs = [log_ref[:, head : head + 1] for head in range(heads)]
+        sent_ref[:, width:] = split_tile(lane_tile(mem_logs + mem_deltas + logs + deltas, rows))
+
+    vmem = pl.BlockSpec(memory_space=pltpu.VMEM)
+    return pl.pallas_call(
+        kernel,
+        in_specs=[vmem] * 9 + [pl.BlockSpec(memory_space=pltpu.SMEM)] + [vmem] * len(halos),
+        out_shape=[
+            jax.ShapeDtypeStruct((rows, width), jnp.float32),
+            jax.ShapeDtypeStruct((heads, span), jnp.float32),
+            jax.ShapeDtypeStruct((heads, head_dim), jnp.float32),
+            jax.ShapeDtypeStruct((rows, width + 128), jnp.bfloat16),
+        ],
+        compiler_params=pltpu.CompilerParams(vmem_limit_bytes=VMEM_LIMIT),
+        cost_estimate=lasting(15),
+        name="local_queries",
+    )(base, book_column, book_row, own, d_mixed, memory_out, local_out, mem_log, local_log, share, *halos)
+
+
+def local_keys(base, book_column, book_row, own, queries, sent, ratio, me, count, heads, score_scale):
+    rows, width = own.shape[0], own.shape[1] // 3
+    head_dim = width // heads
+    groups = queries.shape[0] // rows
+
+    def kernel(me_ref, base_ref, column_ref, row_ref, own_ref, ratio_ref, *refs):
+        q_refs, g_refs, out_ref = refs[:count], refs[count : 2 * count], refs[2 * count]
+        same = column_ref[:, :1] == row_ref[:1, :]
+        stats = jnp.concatenate([joined_tile(ref[:, width:]).T for ref in g_refs], axis=1)
+        for head in range(heads):
+            columns = slice(head * head_dim, (head + 1) * head_dim)
+            above = slice(width + head * head_dim, width + (head + 1) * head_dim)
+            twice = slice(2 * width + head * head_dim, 2 * width + (head + 1) * head_dim)
+            k, v = own_ref[:, above], own_ref[:, twice]
+            qs = [ref[:, columns] for ref in q_refs]
+            gs = [
+                (ref[:, columns].astype(jnp.float32) * ratio_ref[head]).astype(jnp.bfloat16)
+                for ref in g_refs
+            ]
+            raw = [
+                lax.dot_general(k, q, contract_cols, preferred_element_type=jnp.float32) for q in qs
+            ]
+            bias = slanted(base_ref[head : head + 1, :], rows)[:, : count * rows]
+            scores = jnp.concatenate(raw, axis=1) * score_scale + bias
+            log = stats[2 * heads + head : 2 * heads + head + 1, :]
+            delta = stats[3 * heads + head : 3 * heads + head + 1, :]
+            probs = jnp.exp(jnp.where(same, scores - log, masked_score))
+            products = [
+                lax.dot_general(v, g, contract_cols, preferred_element_type=jnp.float32) for g in gs
+            ]
+            slopes = (probs * (jnp.concatenate(products, axis=1) - delta)).astype(jnp.bfloat16)
+            weights = probs.astype(jnp.bfloat16)
+            blocks = [slice(i * rows, (i + 1) * rows) for i in range(count)]
+            d_key = sum(
+                jnp.dot(slopes[:, b], q, preferred_element_type=jnp.float32) for b, q in zip(blocks, qs)
+            )
+            d_value = sum(
+                jnp.dot(weights[:, b], g, preferred_element_type=jnp.float32)
+                for b, g in zip(blocks, gs)
+            )
+            out_ref[:, columns] = (d_key * score_scale).astype(jnp.bfloat16)
+            out_ref[:, above] = d_value.astype(jnp.bfloat16)
+
+    def whole(array):
+        return pl.BlockSpec(array.shape, lambda i, *_: (0, 0))
+
+    def later(distance, size):
+        return pl.BlockSpec((rows, size), lambda i, m: (jnp.minimum(m[0] + distance, groups - 1), 0))
+
+    return pl.pallas_call(
+        kernel,
+        grid_spec=pltpu.PrefetchScalarGridSpec(
+            num_scalar_prefetch=1,
+            grid=(1,),
+            in_specs=[whole(base), whole(book_column), whole(book_row), whole(own)]
+            + [pl.BlockSpec(memory_space=pltpu.SMEM)]
+            + [later(i, width) for i in range(count)]
+            + [later(i, width + 128) for i in range(count)],
+            out_specs=pl.BlockSpec((rows, 2 * width), lambda i, *_: (0, 0)),
+        ),
+        out_shape=jax.ShapeDtypeStruct((rows, 2 * width), jnp.bfloat16),
+        compiler_params=pltpu.CompilerParams(vmem_limit_bytes=VMEM_LIMIT),
+        cost_estimate=lasting(15),
+        name="local_keys",
+    )(me, base, book_column, book_row, own, ratio, *([queries] * count), *([sent] * count))
+
+
+def finish_grads(parts, early, small, sources, collective_id):
+    rows, width = parts.shape[0] // sources, parts.shape[1]
+    depth, half = sources // 4, rows // 2
+    early_width = early.shape[1]
+    mesh_type = pl.DeviceIdType.MESH
+
+    def kernel(parts_ref, early_ref, small_ref, late_out, early_out, small_out, *refs):
+        half_a, half_b, from_x, from_y, from_z, out_x, out_y, out_z, smalls, core_small = refs[:10]
+        send, recv_a, recv_b, recv_x, recv_y, recv_z, small_send, small_recv, core_send, core_recv = refs[10:]
+        me, column, beside_x, beside_y, across, index_of = grid_place(depth)
+        core = lax.axis_index("dp")
+        to_x, to_y = index_of(0, beside_x), index_of(0, beside_y)
+        barrier = pltpu.get_barrier_semaphore()
+        peers = [lax.rem(me + k, sources) for k in range(1, sources)]
+        for peer in peers:
+            pl.semaphore_signal(barrier, inc=1, device_id={"mem": peer}, device_id_type=mesh_type)
+        pl.semaphore_signal(barrier, inc=1, device_id={"dp": 1 - core}, device_id_type=mesh_type)
+        pl.semaphore_wait(barrier, sources)
+        order = [*range(1, depth), 0]
+        sent = []
+
+        def piece(index, part):
+            return parts_ref.at[pl.ds(pl.multiple_of(index * rows + part * half, half), half), :]
+
+        def part_rows(part):
+            return pl.ds(part * half, half)
+
+        def push(source, target, kind, k, recv_sem, device):
+            copy = remote(source, target, send.at[kind, k], recv_sem, device)
+            copy.start()
+            sent.append(copy)
+
+        def arrived(target, recv_sem):
+            remote(target, target, send.at[0, 0], recv_sem, to_x).wait_recv()
+
+        def added(blocks):
+            total = blocks[0][...].astype(jnp.float32)
+            for block in blocks[1:]:
+                total = total + block[...].astype(jnp.float32)
+            return total
+
+        def across_cores(source, target, i):
+            copy = pltpu.make_async_remote_copy(
+                src_ref=source,
+                dst_ref=target,
+                send_sem=core_send.at[i],
+                recv_sem=core_recv.at[i],
+                device_id={"dp": 1 - core},
+                device_id_type=mesh_type,
+            )
+            copy.start()
+            return copy
+
+        for k in order:
+            far = index_of(k, across)
+            push(piece(far, 0), half_a.at[k], 0, k, recv_a.at[k], to_x)
+            push(piece(far, 1), half_b.at[k], 1, k, recv_b.at[k], to_y)
+        smalls[me] = small_ref[...]
+        for i, peer in enumerate(peers):
+            copy = remote(small_ref, smalls.at[me], small_send.at[i], small_recv.at[me], peer)
+            copy.start()
+            sent.append(copy)
+        early_copy = across_cores(early_ref, early_out.at[core], 0)
+        early_out[core] = early_ref[...]
+        for k in order:
+            push(piece(index_of(k, beside_x), 0), from_x.at[k, part_rows(0)], 2, k, recv_x.at[0, k], to_x)
+            push(piece(index_of(k, beside_y), 1), from_y.at[k, part_rows(1)], 3, k, recv_y.at[1, k], to_y)
+        for k in order:
+            arrived(half_a.at[k], recv_a.at[k])
+            out_y[k] = added([piece(index_of(k, beside_y), 0), half_a.at[k]]).astype(parts.dtype)
+            push(out_y.at[k], from_y.at[k, part_rows(0)], 4, k, recv_y.at[0, k], to_y)
+            arrived(half_b.at[k], recv_b.at[k])
+            out_x[k] = added([piece(index_of(k, beside_x), 1), half_b.at[k]]).astype(parts.dtype)
+            push(out_x.at[k], from_x.at[k, part_rows(1)], 5, k, recv_x.at[1, k], to_x)
+        for peer in peers:
+            arrived(smalls.at[peer], small_recv.at[peer])
+        group_small = smalls[0]
+        for i in range(1, sources):
+            group_small = group_small + smalls[i]
+        core_small[0] = group_small
+        small_copy = across_cores(core_small.at[0], core_small.at[1], 1)
+        for k in order:
+            for part in (0, 1):
+                arrived(from_x.at[k, part_rows(part)], recv_x.at[part, k])
+                arrived(from_y.at[k, part_rows(part)], recv_y.at[part, k])
+            if k:
+                for part in (0, 1):
+                    here = part_rows(part)
+                    blocks = [piece(index_of(k, column), part), from_x.at[k, here], from_y.at[k, here]]
+                    out_z[k, here] = added(blocks).astype(parts.dtype)
+                push(out_z.at[k], from_z.at[k], 6, k, recv_z.at[k], index_of(k, column))
+        for k in range(1, depth):
+            arrived(from_z.at[k], recv_z.at[k])
+        for part in (0, 1):
+            here = part_rows(part)
+            blocks = [piece(me, part), from_x.at[0, here], from_y.at[0, here]]
+            blocks += [from_z.at[k, here] for k in range(1, depth)]
+            late_out[core, here] = added(blocks).astype(parts.dtype)
+        late_copy = across_cores(late_out.at[core], late_out.at[core], 2)
+        for copy in (early_copy, small_copy, late_copy):
+            copy.wait()
+        small_out[...] = core_small[0] + core_small[1]
+        for copy in sent:
+            copy.wait_send()
+
+    def slots(size):
+        return pltpu.VMEM((depth, size, width), parts.dtype)
+
+    vmem = pl.BlockSpec(memory_space=pltpu.VMEM)
+    return pl.pallas_call(
+        kernel,
+        in_specs=[vmem] * 3,
+        out_specs=[vmem] * 3,
+        out_shape=[
+            jax.ShapeDtypeStruct((2, rows, width), parts.dtype),
+            jax.ShapeDtypeStruct((2, rows, early_width), early.dtype),
+            jax.ShapeDtypeStruct(small.shape, small.dtype),
+        ],
+        scratch_shapes=[slots(half), slots(half), slots(rows), slots(rows), slots(rows)]
+        + [slots(half), slots(half), slots(rows)]
+        + [pltpu.VMEM((sources, *small.shape), small.dtype), pltpu.VMEM((2, *small.shape), small.dtype)]
+        + [pltpu.SemaphoreType.DMA((7, depth))]
+        + [pltpu.SemaphoreType.DMA((depth,))] * 2
+        + [pltpu.SemaphoreType.DMA((2, depth))] * 2
+        + [pltpu.SemaphoreType.DMA((depth,))]
+        + [pltpu.SemaphoreType.DMA((sources,))] * 2
+        + [pltpu.SemaphoreType.DMA((3,))] * 2,
+        compiler_params=pltpu.CompilerParams(
+            collective_id=collective_id, has_side_effects=True, vmem_limit_bytes=VMEM_LIMIT
+        ),
+        cost_estimate=lasting(55),
+        name="finish_grads",
+    )(parts, early, small)
 
 
 def on_device(
@@ -707,59 +1054,36 @@
     groups = lax.axis_size("mem")
     capacity = max(2, 3 * rows * heads * top_count // (2 * groups))
     score_scale = 1.0 / math.sqrt(head_dim)
-    sent_rows = min(W, rows)
-    repeats = W // sent_rows
-    first_pos = lax.axis_index("mem") * rows
-    query_pos = first_pos + jnp.arange(rows, dtype=jnp.int32)
-    key_pos = first_pos - W + jnp.arange(W + rows, dtype=jnp.int32)
+    repeats = W // rows
+    span = W + 2 * rows
+    me = lax.axis_index("mem")
+    first_pos = me * rows
     lengths = book_lengths[0]
-    query_book = book_of(query_pos, lengths)
+    window = jnp.arange(W + rows, dtype=jnp.int32)
+    key_pos = first_pos - W + window
     key_book = jnp.where(key_pos >= 0, book_of(key_pos, lengths), -1)
-    offset = (
-        jnp.arange(rows, dtype=jnp.int32)[:, None]
-        + W
-        - jnp.arange(W + rows, dtype=jnp.int32)[None, :]
-    )
-    allowed = (offset >= 0) & (offset < W) & (query_book[:, None] == key_book[None, :])
-    bucket = bucket_of(jnp.maximum(offset, 0))
-    one_hot_f = (bucket[:, :, None] == jnp.arange(buckets, dtype=jnp.int32)).astype(jnp.float32)
-    score_bias = jnp.einsum("qkb,hb->hqk", one_hot_f, bias_table, precision=lax.Precision.HIGHEST)
+    later_book = book_of(first_pos + window, lengths)
+    own_book = jnp.broadcast_to(later_book[:rows, None], (rows, 128))
+    key_book = jnp.broadcast_to(key_book[None, :], (8, W + rows))
+    later_book = jnp.broadcast_to(later_book[None, :], (8, W + rows))
+    bucket = bucket_of(jnp.arange(W, dtype=jnp.int32))
+    one_hot = (bucket[:, None] == jnp.arange(buckets, dtype=jnp.int32)).astype(jnp.float32)
+    offset_bias = jnp.einsum("rb,hb->hr", one_hot, bias_table, precision=lax.Precision.HIGHEST)
+    after_bias = jnp.pad(offset_bias, ((0, 0), (0, span - W)), constant_values=masked_score)
+    before_bias = jnp.pad(
+        offset_bias[:, ::-1], ((0, 0), (1, span - W - 1)), constant_values=masked_score
+    )
     tokens_f = tokens.astype(jnp.float32)
     normed_f, norm_in_back = jax.vjp(normed, tokens_f, attn_gain)
     normed_in = normed_f.astype(jnp.bfloat16)
     projected = jnp.dot(normed_in, qkv_weight, preferred_element_type=jnp.float32).astype(
         jnp.bfloat16
     )
-    queries = projected[:, :width].reshape(rows, heads, head_dim)
-    keys_own = projected[:, width : 2 * width].reshape(rows, heads, head_dim)
-    values_own = projected[:, 2 * width :].reshape(rows, heads, head_dim)
-    tail_rows = jnp.stack([keys_own, values_own])
-    received = []
-    for distance in range(repeats, 0, -1):
-        received.append(passed_along(tail_rows, "mem", distance))
-    halo_rows = jnp.concatenate(received, axis=1)
-    keys_all = jnp.concatenate([halo_rows[0], keys_own], axis=0)
-    values_all = jnp.concatenate([halo_rows[1], values_own], axis=0)
-
-    def local_scores():
-        raw_scores = (
-            jnp.einsum("qhd,khd->hqk", queries, keys_all, preferred_element_type=jnp.float32)
-            * score_scale
-            + score_bias
-        )
-        return jnp.where(allowed[None], raw_scores, masked_score)
-
-    scores = local_scores()
-    row_max = jnp.max(scores, axis=-1, keepdims=True)
-    exp_scores = jnp.exp(scores - row_max)
-    sums_local = jnp.sum(exp_scores, axis=-1, keepdims=True)
-    local_probs = exp_scores / sums_local
-    log_total = row_max + jnp.log(sums_local)
-    local_out = jnp.einsum(
-        "hqk,khd->qhd",
-        local_probs.astype(jnp.bfloat16),
-        values_all,
-        preferred_element_type=jnp.float32,
+    halos = [
+        passed_along(projected[:, width:], "mem", distance) for distance in range(repeats, 0, -1)
+    ]
+    local_out, local_log = local_forward(
+        before_bias, own_book, key_book, projected, halos, heads, score_scale
     )
     slots = memory_keys.shape[0]
     requests = place_requests(slot_shard, slot_index, slot_live, groups, capacity, slots)
@@ -795,13 +1119,9 @@
             tiled=True,
         ).reshape(groups * rows, width + 128)
         memory_out, mem_log = combine_partials(partial, heads, groups, rows)
-    memory_out = memory_out.reshape(rows, heads, head_dim)
-    gate_share = jax.nn.sigmoid(gate_logit)[:, None]
-    mixed_heads = (
-        (gate_share * memory_out + (1.0 - gate_share) * local_out)
-        .reshape(rows, width)
-        .astype(jnp.bfloat16)
-    )
+    gate_share = jax.nn.sigmoid(gate_logit)
+    share_wide = jnp.repeat(gate_share, head_dim)[None, :]
+    mixed_heads = (share_wide * memory_out + (1.0 - share_wide) * local_out).astype(jnp.bfloat16)
     residual = tokens_f + jnp.dot(mixed_heads, out_weight, preferred_element_type=jnp.float32)
     normed_mid_f, norm_mid_back = jax.vjp(normed, residual, ffn_gain)
     normed_mid = normed_mid_f.astype(jnp.bfloat16)
@@ -820,45 +1140,25 @@
     d_branch = d_residual.astype(jnp.bfloat16)
     d_mixed = lax.dot_general(
         d_branch, out_weight, contract_cols, preferred_element_type=jnp.float32
-    ).reshape(rows, heads, head_dim)
-    gate_part = (
-        jnp.sum(d_mixed * (memory_out - local_out), axis=(0, 2))
-        * (gate_share * (1.0 - gate_share))[:, 0]
     )
     early_halves = weight_halves([(mixed_heads, d_branch), (normed_mid, d_up), (cotangent, activated)])
-    d_memory = (gate_share * d_mixed).astype(jnp.bfloat16)
-    d_local_out = ((1.0 - gate_share) * d_mixed).astype(jnp.bfloat16)
-    probs_again = jnp.exp(local_scores() - log_total)
-    d_lw = jnp.einsum("qhd,khd->hqk", d_local_out, values_all, preferred_element_type=jnp.float32)
-    d_local = (probs_again * (d_lw - jnp.sum(probs_again * d_lw, axis=-1, keepdims=True))).astype(
-        jnp.bfloat16
-    )
-    d_values_all = jnp.einsum(
-        "hqk,qhd->khd",
-        probs_again.astype(jnp.bfloat16),
-        d_local_out,
-        preferred_element_type=jnp.float32,
-    )
-    d_keys_all = (
-        jnp.einsum("hqk,qhd->khd", d_local, queries, preferred_element_type=jnp.float32)
-        * score_scale
-    )
-    d_queries = (
-        jnp.einsum("hqk,khd->qhd", d_local, keys_all, preferred_element_type=jnp.float32)
-        * score_scale
-    )
-    bias_part = jnp.einsum(
-        "hqk,qkb->hb", d_local, one_hot_f.astype(jnp.bfloat16), preferred_element_type=jnp.float32
-    )
-    mem_delta = jnp.sum(d_memory.astype(jnp.float32) * memory_out, axis=-1)
-    sent_grads = jnp.concatenate(
-        [
-            d_memory.reshape(rows, width),
-            split3(jnp.concatenate([mem_log[:, :heads], mem_delta], axis=1)),
-            jnp.zeros((rows, 80), jnp.bfloat16),
-        ],
-        axis=1,
-    )
+    d_queries, diagonals, gate_products, sent_grads = local_queries(
+        before_bias,
+        own_book,
+        key_book,
+        projected,
+        halos,
+        d_mixed,
+        memory_out,
+        local_out,
+        mem_log,
+        local_log,
+        gate_share,
+        heads,
+        score_scale,
+    )
+    gate_part = jnp.sum(gate_products, axis=1) * gate_share * (1.0 - gate_share)
+    bias_part = jnp.dot(diagonals[:, rows - 1 : rows - 1 + W], one_hot, precision=lax.Precision.HIGHEST)
     sent_grads, early_halves = lax.optimization_barrier((sent_grads, early_halves))
     early_sums = scattered(early_halves)
     if groups == 16:
@@ -877,33 +1177,31 @@
         rows,
         score_scale,
     )
+    d_keys_values = local_keys(
+        after_bias,
+        own_book,
+        later_book,
+        projected,
+        all_queries,
+        all_grads,
+        (1.0 - gate_share) / gate_share,
+        me[None],
+        repeats + 1,
+        heads,
+        score_scale,
+    )
     if groups == 16:
         d_partial = sum_blocks(d_partial, groups, 3)
     else:
+        d_partial, d_keys_values = lax.optimization_barrier((d_partial, d_keys_values))
         d_partial = jnp.sum(
             lax.all_to_all(
                 d_partial.reshape(groups, rows, width), "mem", split_axis=0, concat_axis=0, tiled=True
             ).astype(jnp.float32),
             axis=0,
         )
-    d_queries = d_queries + d_partial.reshape(rows, heads, head_dim) * score_scale
-    halo_grads = jnp.stack([d_keys_all[:W], d_values_all[:W]])
-    d_tails = jnp.zeros((2, sent_rows, heads, head_dim), jnp.float32)
-    for distance in range(repeats, 0, -1):
-        first_row = (repeats - distance) * sent_rows
-        d_tails = d_tails + passed_along(
-            halo_grads[:, first_row : first_row + sent_rows].astype(jnp.bfloat16), "mem", -distance
-        ).astype(jnp.float32)
-    d_keys = d_keys_all[W:] + d_tails[0]
-    d_values = d_values_all[W:] + d_tails[1]
-    d_projected = jnp.concatenate(
-        [
-            d_queries.reshape(rows, width),
-            d_keys.reshape(rows, width),
-            d_values.reshape(rows, width),
-        ],
-        axis=1,
-    ).astype(jnp.bfloat16)
+    d_queries = (d_queries + d_partial * score_scale).astype(jnp.bfloat16)
+    d_projected = jnp.concatenate([d_queries, d_keys_values], axis=1)
     d_in = lax.dot_general(
         d_projected, qkv_weight, contract_cols, preferred_element_type=jnp.float32
     )
@@ -911,10 +1209,20 @@
     tokens_grad = d_residual + d_tokens_part
     late_halves = weight_halves([(normed_in, d_projected)])
     late_halves, early_sums = lax.optimization_barrier((late_halves, early_sums))
-    late_sums = scattered(late_halves)
-    out_grad, up_grad, down_grad = whole_grads(early_sums, [width, hidden, hidden])
-    qkv_grad = whole_grads(late_sums, [3 * width])[0]
-    small_sums = lax.psum((attn_gain_part, ffn_gain_part, bias_part, gate_part), ("dp", "mem"))
+    small = jnp.concatenate(
+        [attn_gain_part, ffn_gain_part, bias_part.reshape(-1), gate_part], axis=0
+    )
+    small = jnp.pad(small, (0, -small.shape[0] % 1024)).reshape(-1, 128)
+    if groups == 16:
+        late_both, early_both, small = finish_grads(late_halves, early_sums, small, groups, 4)
+    else:
+        late_both = lax.all_gather(scattered(late_halves), "dp", axis=0)
+        early_both = lax.all_gather(early_sums, "dp", axis=0)
+        small = lax.psum(small, ("dp", "mem"))
+    small = small.reshape(-1)
+    out_grad, up_grad, down_grad = whole_grads(early_both, [width, hidden, hidden])
+    qkv_grad = whole_grads(late_both, [3 * width])[0]
+    at_bias = 2 * width + heads * buckets
     return (
         block_out,
         tokens_grad,
@@ -922,10 +1230,10 @@
         out_grad,
         up_grad,
         down_grad,
-        small_sums[0],
-        small_sums[1],
-        small_sums[2],
-        small_sums[3],
+        small[:width],
+        small[width : 2 * width],
+        small[2 * width : at_bias].reshape(heads, buckets),
+        small[at_bias : at_bias + heads],
     )
 
 

time: 778 us -> 608 us (0.78)
  waiting for transfers between devices: 169 us -> 4.78 us
  Pallas kernels: 314 us -> 421 us
  blocking collectives: 44.5 us -> 0 us
  local copies, waits for them, and re-layouts: 51.6 us -> 22.1 us
  matrix products: 59 us -> 39.1 us
    ppermute x8 -> x4, waiting for transfers between devices: 84.3 us -> 0.01 us  [passed_along(): return lax.ppermute(value, axis, pairs)]
    reduce_scatter x2 -> x1, waiting for transfers between devices: 82.5 us -> 1.37 us  [scattered(): return lax.psum_scatter(halves, 'mem', scatter_dimension=0, tiled=True)]
    pallas_call x0 -> x4, Pallas kernels: none -> 69.1 us  [the longest x1 49.4 us: finish_grads(): pl.pallas_call(kernel, in_specs=[vmem] * 3, out_specs=[vmem] * 3, out_sha...]
    pallas_call x2, Pallas kernels: 132 us -> 175 us  [reduce_group(): pl.pallas_call(kernel, in_specs=[pl.BlockSpec(memory_space=pltpu.VMEM)],...]
    psum x1 -> x0, blocking collectives: 40.2 us -> none  [on_device(): lax.psum((attn_gain_part, ffn_gain_part, bias_part, gate_part), ('dp', 'm...]
    dot_general x8 -> x2, matrix products: 20.5 us -> 0.6 us  [the longest x1 0.32 us: on_device(): jnp.einsum('rb,hb->hr', one_hot, bias_table, precision=lax.Precision.HIGH...]
    unnamed x154 -> x102, local copies, waits for them, and re-layouts: 17.6 us -> 5.39 us
    pallas_call x1, Pallas kernels: 55.7 us -> 44.9 us  [gather_rows(): pl.pallas_call(kernel, grid_spec=pltpu.PrefetchScalarGridSpec(num_scalar_...]
  transfers between devices with their start and end apart: 15 -> 9, of which waited for: 6 -> 2; matrix products, arithmetic and copies ran while one was open for 13% -> 9% of each run, Pallas kernels for 26% -> 42%
where the time goes in v4:
time: 608 us; the launch traced here: 598 us
  Pallas kernels  421 us (69%)
  between operations  44 us (7%)
  other arithmetic  43.1 us (7%)
  matrix products  39.1 us (6%)
  starting transfers between devices  24.4 us (4%)
  local copies, waits for them, and re-layouts  22.1 us (4%)
    pallas_call x2, Pallas kernels, reduce_group(): pl.pallas_call(kernel, in_specs=[pl.BlockSpec(memory_space=pltpu.VMEM)],...  175 us
    pallas_call x1, Pallas kernels, gather_group(): pl.pallas_call(kernel, in_specs=[pl.BlockSpec(memory_space=pl.ANY)], out_...  54.1 us
    pallas_call x1, Pallas kernels, finish_grads(): pl.pallas_call(kernel, in_specs=[vmem] * 3, out_specs=[vmem] * 3, out_sha...  49.4 us
    pallas_call x1, Pallas kernels, gather_rows(): pl.pallas_call(kernel, grid_spec=pltpu.PrefetchScalarGridSpec(num_scalar_...  44.9 us
    pallas_call x1, Pallas kernels, memory_forward(): pl.pallas_call(kernel, grid_spec=pltpu.PrefetchScalarGridSpec(num_scalar_...  42 us
    pallas_call x1, Pallas kernels, memory_backward(): pl.pallas_call(kernel, grid_spec=pltpu.PrefetchScalarGridSpec(num_scalar_...  35.3 us
    sort x1, other arithmetic, place_requests(): lax.sort(((owner * entries + place).reshape(-1), slot_index.reshape(-1)),...  18.5 us
    ppermute x4, starting transfers between devices, passed_along(): return lax.ppermute(value, axis, pairs)  13.5 us
  transfers between devices with their start and end apart: 9, of which 2 were waited for; matrix products, arithmetic and copies ran while one was open for 9% of the time, Pallas kernels for 42%

profile of v4, /device:TPU:9, one launch (start us, length us, event | category | flops | bytes accessed | tf_op | source)
XLA Modules:
  0.0 597.9 jit_solution(4812695952765211964)
XLA Ops:
  10.7 3.9 convolution_convert_fusion.3.own_ref
  15.5 3.1 collective-permute-start.3
  18.6 3.1 collective-permute-start.2
  21.8 4.1 collective-permute-start.1
  25.9 3.2 collective-permute-start
  32.4 18.5 %sort.23 = (s32[32768]{0:T(1024)S(1)}, s32[32768]{0:T(1024)S(1)}, s32[32768]{0:T(1024)}) sort(s32[32768]{0:T(1024)S(1)} %reshape.515, s32[32768]{0:T(1024)} %reshape.516, s32[32768]{0:T(1024)S(1)} %iota.59), dimensions={0}, to_apply=%region_0.0 | sort | flops 491520 | bytes 786432 | tf_op jit(solution)/shard_map/sort | solution.py:61
  82.5 4.3 all-to-all-start
  89.6 3.4 all-to-all-done
  95.6 44.9 %gather_rows.1 = (bf16[49152,128]{1,0:T(8,128)(2,1)}, bf16[49152,128]{1,0:T(8,128)(2,1)}) custom-call(s32[49152]{0:T(1024)} %fusion.46.index_ref, s32[16]{0:T(128)} %slice_bitcast_fusion.10.counts_ref, bf16[4096,1024]{1,0:T(8,128)(2,1)} %keys.1, bf16[4096,1024]{1,0:T(8,128)(2,1)} %values.1), custom_call_target="tpu_custom_call" | custom-call | bytes 126000000 | tf_op jit(solution)/shard_map/gather_rows/pallas_call | solution.py:116
  140.5 1.6 and_select_fusion.id_ref
  143.4 6.7 %local_forward.1 = (f32[128,1024]{1,0:T(8,128)}, f32[128,128]{1,0:T(8,128)}) custom-call(f32[8,768]{1,0:T(8,128)} %pad.13.base_ref, s32[128,128]{1,0:T(8,128)} %broadcast_in_dim.29.column_ref, s32[8,640]{1,0:T(8,128)} %broadcast_in_dim.31.row_ref, bf16[128,3072]{1,0:T(8,128)(2,1)} %copy-done.2, bf16[128,2048]{1,0:T(8,128)(2,1)} %collective-permute-done.refs_0_, ...), custom_call_target="tpu_custom_call" | custom-call | bytes 30000000 | tf_op jit(solution)/shard_map/local_forward/pallas_call | solution.py:737
  150.1 42.0 %memory_forward.1.parts_ref = bf16[2048,1152]{1,0:T(8,128)(2,1)} custom-call(s32[144]{0:T(256)} %reshape.517.bounds_ref, bf16[2048,1024]{1,0:T(8,128)(2,1)} %all-gather.2.cloned.1.call-done.q_ref.refs_0_.refs_1_.refs_2_.refs_3_.refs_4_, bf16[49152,128]{1,0:T(8,128)(2,1)} %get-tuple-element.33.k_ref, bf16[49152,128]{1,0:T(8,128)(2,1)} %get-tuple-element.34.v_ref, ...), custom_call_target="tpu_custom_call" | custom-call | bytes 123000000 | tf_op jit(solution)/shard_map/memory_forward/pallas_call | solution.py:227
  192.2 78.3 %reduce_group.2 = (f32[128,1024]{1,0:T(8,128)}, f32[128,128]{1,0:T(8,128)}) custom-call(bf16[2048,1152]{1,0:T(8,128)(2,1)} %memory_forward.1.parts_ref), custom_call_target="tpu_custom_call" | custom-call | bytes 165000000 | tf_op jit(solution)/shard_map/reduce_group/pallas_call | solution.py:549
  270.5 1.9 constant_dynamic-update-slice_fusion.18
  274.6 4.8 fusion.70
  279.5 6.8 %add_convert_fusion = (bf16[128,4096]{1,0:T(8,128)(2,1)S(1)}, f32[128,4096]{1,0:T(8,128)S(1)}) fusion(f32[128,4096]{1,0:T(8,128)S(1)} %fusion.70, bf16[128,1024]{1,0:T(8,128)(2,1)S(1)} %copy-done.5, bf16[1024,4096]{1,0:T(8,128)(2,1)S(1)} %bitcast.89), kind=kOutput, calls=%fused_computation.7 | convolution fusion | flops 1111490560 | bytes 13893632 | tf_op jit(solution)/shard_map/dot_general | solution.py:1135
  286.5 3.0 multiply_reduce_fusion
  293.0 5.1 collective-permute-start.4
  298.0 1.6 fusion.71.mix_ref
  299.7 7.0 %local_queries.1 = (f32[128,1024]{1,0:T(8,128)}, f32[8,768]{1,0:T(8,128)}, f32[8,128]{1,0:T(8,128)}, bf16[128,1152]{1,0:T(8,128)(2,1)}) custom-call(f32[8,768]{1,0:T(8,128)} %pad.13.base_ref, s32[128,128]{1,0:T(8,128)} %broadcast_in_dim.29.column_ref, s32[8,640]{1,0:T(8,128)} %broadcast_in_dim.31.row_ref, bf16[128,3072]{1,0:T(8,128)(2,1)} %copy-done.2, ...), custom_call_target="tpu_custom_call" | custom-call | bytes 45000000 | tf_op jit(solution)/shard_map/local_queries/pallas_call | solution.py:814
  310.0 4.9 pad_maximum_fusion
  316.8 7.0 %fusion.6 = bf16[128,1024]{1,0:T(8,128)(2,1)} fusion(f32[128,1024]{1,0:T(8,128)S(1)} %get-tuple-element.119, bf16[128,4096]{1,0:T(8,128)(2,1)S(1)} %copy-done.4, bf16[1024,4096]{1,0:T(8,128)(2,1)} %param.24), kind=kOutput, calls=%fused_computation.27 | convolution fusion | flops 1074003968 | bytes 10223616 | tf_op jit(solution)/shard_map/dot_general | solution.py:1131
  323.8 54.1 %gather_group.1.g_ref.refs_5_.refs_6_.refs_7_.refs_8_.refs_9_ = bf16[2048,1152]{1,0:T(8,128)(2,1)} custom-call(bf16[128,1152]{1,0:T(8,128)(2,1)} %get-tuple-element.41.x_ref), custom_call_target="tpu_custom_call" | custom-call | bytes 150000000 | tf_op jit(solution)/shard_map/gather_group/pallas_call | solution.py:468
  377.8 35.3 %memory_backward.1.parts_ref = bf16[2048,1024]{1,0:T(8,128)(2,1)} custom-call(s32[144]{0:T(256)} %reshape.517.bounds_ref, bf16[2048,1024]{1,0:T(8,128)(2,1)} %all-gather.2.cloned.1.call-done.q_ref.refs_0_.refs_1_.refs_2_.refs_3_.refs_4_, bf16[2048,1152]{1,0:T(8,128)(2,1)} %gather_group.1.g_ref.refs_5_.refs_6_.refs_7_.refs_8_.refs_9_, ...), custom_call_target="tpu_custom_call" | custom-call | bytes 105000000 | tf_op jit(solution)/shard_map/memory_backward/pallas_call | solution.py:360
  413.1 96.7 %reduce_group.3 = f32[128,1024]{1,0:T(8,128)} custom-call(bf16[2048,1024]{1,0:T(8,128)(2,1)} %memory_backward.1.parts_ref), custom_call_target="tpu_custom_call" | custom-call | bytes 165000000 | tf_op jit(solution)/shard_map/reduce_group/pallas_call | solution.py:549
  510.5 6.1 %local_keys.1 = bf16[128,2048]{1,0:T(8,128)(2,1)} custom-call(s32[1]{0:T(128)} %bitcast.38.me_ref, f32[8,768]{1,0:T(8,128)} %pad.14.base_ref, s32[128,128]{1,0:T(8,128)} %broadcast_in_dim.29.column_ref, s32[8,640]{1,0:T(8,128)} %broadcast_in_dim.35.row_ref, bf16[128,3072]{1,0:T(8,128)(2,1)} %copy-done.2, f32[8]{0:T(128)} %get-tuple-element.56.ratio_ref, ...), custom_call_target="tpu_custom_call" | custom-call | bytes 45000000 | tf_op jit(solution)/shard_map/local_keys/pallas_call | solution.py:878
  518.1 1.4 collective-permute-start.5
  519.5 5.2 fusion.20
  526.5 2.7 convolution_convert_fusion.parts_ref
  529.1 1.4 reduce-scatter.2.cloned.1.call-done.early_ref
  530.5 49.4 %finish_grads.1 = (bf16[2,64,1536]{2,1,0:T(8,128)(2,1)}, bf16[2,64,4608]{2,1,0:T(8,128)(2,1)}, f32[24,128]{1,0:T(8,128)}) custom-call(bf16[1024,1536]{1,0:T(8,128)(2,1)} %convolution_convert_fusion.parts_ref, bf16[64,4608]{1,0:T(8,128)(2,1)} %reduce-scatter.2.cloned.1.call-done.early_ref, f32[24,128]{1,0:T(8,128)} %fusion.57.small_ref), custom_call_target="tpu_custom_call" | custom-call | bytes 165000000 | tf_op jit(solution)/shard_map/finish_grads/pallas_call | solution.py:1005
  581.9 1.5 convert_element_type.236
  (197 shorter events, 41.1 us)
Async XLA Ops:
  7.2 265.3 %copy-start = (bf16[1024,1024]{1,0:T(8,128)(2,1)S(1)}, bf16[1024,1024]{1,0:T(8,128)(2,1)}, u32[]{:S(2)}) copy-start(bf16[1024,1024]{1,0:T(8,128)(2,1)} %param.19) | copy-start | bytes 6291460
  7.2 142.9 %all-gather.2.cloned.1.call-start = ((), (), s32[]{:S(2)}) async-start(), calls=%async_computation.2 | async-start | bytes 4456448 | tf_op jit(solution)/shard_map/all_gather | solution.py:1098
  10.7 4.0 copy-start.8
  10.7 19.3 %copy-start.17 = (s32[128,8,32,1]{0,3,2,1:T(1,128)S(1)}, s32[128,8,32,1]{0,3,2,1:T(1,128)}, u32[]{:S(2)}) copy-start(s32[128,8,32,1]{0,3,2,1:T(1,128)} %param.28) | copy-start | bytes 393220
  10.7 19.2 %copy-start.18 = (s32[128,8,32]{0,2,1:T(8,128)S(1)}, s32[128,8,32]{0,2,1:T(8,128)}, u32[]{:S(2)}) copy-start(s32[128,8,32]{0,2,1:T(8,128)} %param.30) | copy-start | bytes 393220
  14.6 16.9 %copy-start.2 = (bf16[128,3072]{1,0:T(8,128)(2,1)}, bf16[128,3072]{1,0:T(8,128)(2,1)S(1)}, u32[]{:S(2)}) copy-start(bf16[128,3072]{1,0:T(8,128)(2,1)S(1)} %convolution_convert_fusion.3.own_ref) | copy-start | bytes 2359300
  15.5 126.6 %collective-permute-start.3 = (bf16[128,2048]{1,0:T(8,128)(2,1)}, bf16[128,2048]{1,0:T(8,128)(2,1)}, u32[]{:S(2)}, u32[]{:S(2)}) collective-permute-start(bf16[128,2048]{1,0:T(8,128)(2,1)} %slice.193), channel_id=1, source_target_pairs={{0,1},{1,2},{2,3},{3,4},{4,5},{5,6},{6,7},{7,8},{8,9},{9,10},{10,1... | collective-permute-start | bytes 1572872 | tf_op jit(solution)/shard_map/ppermute | solution.py:25
  18.6 123.5 %collective-permute-start.2 = (bf16[128,2048]{1,0:T(8,128)(2,1)}, bf16[128,2048]{1,0:T(8,128)(2,1)}, u32[]{:S(2)}, u32[]{:S(2)}) collective-permute-start(bf16[128,2048]{1,0:T(8,128)(2,1)} %slice.193), channel_id=1, source_target_pairs={{0,2},{1,3},{2,4},{3,5},{4,6},{5,7},{6,8},{7,9},{8,10},{9,11},{10,... | collective-permute-start | bytes 1572872 | tf_op jit(solution)/shard_map/ppermute | solution.py:25
  21.8 120.3 %collective-permute-start.1 = (bf16[128,2048]{1,0:T(8,128)(2,1)}, bf16[128,2048]{1,0:T(8,128)(2,1)}, u32[]{:S(2)}, u32[]{:S(2)}) collective-permute-start(bf16[128,2048]{1,0:T(8,128)(2,1)} %slice.193), channel_id=1, source_target_pairs={{0,3},{1,4},{2,5},{3,6},{4,7},{5,8},{6,9},{7,10},{8,11},{9,12},{10... | collective-permute-start | bytes 1572872 | tf_op jit(solution)/shard_map/ppermute | solution.py:25
  25.9 116.2 %collective-permute-start = (bf16[128,2048]{1,0:T(8,128)(2,1)}, bf16[128,2048]{1,0:T(8,128)(2,1)}, u32[]{:S(2)}, u32[]{:S(2)}) collective-permute-start(bf16[128,2048]{1,0:T(8,128)(2,1)} %slice.193), channel_id=1, source_target_pairs={{0,4},{1,5},{2,6},{3,7},{4,8},{5,9},{6,10},{7,11},{8,12},{9,13},{1... | collective-permute-start | bytes 1572872 | tf_op jit(solution)/shard_map/ppermute | solution.py:25
  30.4 56.5 %copy-start.36 = (s32[1,3]{1,0:T(1,128)S(1)}, s32[1,3]{1,0:T(1,128)}, u32[]{:S(2)}) copy-start(s32[1,3]{1,0:T(1,128)} %param.27) | copy-start | bytes 40
  30.4 56.7 %copy-start.37 = (f32[8]{0:T(128)S(1)}, f32[8]{0:T(128)}, u32[]{:S(2)}) copy-start(f32[8]{0:T(128)} %param.21) | copy-start | bytes 100
  30.4 57.8 %copy-start.35 = (f32[8,32]{1,0:T(8,128)S(1)}, f32[8,32]{1,0:T(8,128)}, u32[]{:S(2)}) copy-start(f32[8,32]{1,0:T(8,128)} %param.20) | copy-start | bytes 3076
  82.5 10.5 %all-to-all-start = ((s32[16,1,3072]{2,1,0:T(1,128)}), s32[16,1,3072]{2,1,0:T(1,128)S(1)}, u32[]{:S(2)}, u32[]{:S(2)}) async-start(s32[16,1,3072]{2,1,0:T(1,128)} %compare_select_fusion), calls=%async_computation | async-start | bytes 393216 | tf_op jit(solution)/shard_map/all_to_all | solution.py:1090
  86.8 443.7 %reduce-scatter.2.cloned.1.call-start = ((), (), s32[]{:S(2)}) async-start(), calls=%async_computation.3 | async-start | bytes 10027008 | tf_op jit(solution)/shard_map/reduce_scatter | solution.py:661
  88.5 52.0 %copy-start.20 = (f32[8,512]{1,0:T(8,128)}, f32[8,512]{1,0:T(8,128)S(1)}, u32[]{:S(2)}) copy-start(f32[8,512]{1,0:T(8,128)S(1)} %convolution_bitcast_fusion) | copy-start | bytes 49156
  192.1 78.4 %copy-start.12 = (f32[128,1024]{1,0:T(8,128)S(1)}, f32[128,1024]{1,0:T(8,128)}, u32[]{:S(2)}) copy-start(f32[128,1024]{1,0:T(8,128)} %get-tuple-element.36.loc_ref) | copy-start | bytes 1572868
  192.1 80.3 %copy-start.6 = (bf16[128,1024]{1,0:T(8,128)(2,1)S(1)}, bf16[128,1024]{1,0:T(8,128)(2,1)}, u32[]{:S(2)}) copy-start(bf16[128,1024]{1,0:T(8,128)(2,1)} %param.16) | copy-start | bytes 786436
  270.5 3.3 copy-start.5
  272.5 7.0 %slice-start.2 = ((s8[8388608]{0:T(1024)(128)(4,1)}), s8[4194304]{0:T(1024)(128)(4,1)S(1)}, s32[]{:S(2)}) async-start(s8[8388608]{0:T(1024)(128)(4,1)} %bitcast.88), calls=%async_computation.6 | async-start | bytes 8388608
  274.6 4.8 slice-start.3
  274.6 11.9 %slice-start = ((s8[8388608]{0:T(1024)(128)(4,1)}), s8[4194304]{0:T(1024)(128)(4,1)S(1)}, s32[]{:S(2)}) async-start(s8[8388608]{0:T(1024)(128)(4,1)} %bitcast.86), calls=%async_computation.4 | async-start | bytes 8388608
  279.4 7.1 %slice-start.1 = ((s8[8388608]{0:T(1024)(128)(4,1)}), s8[4194304]{0:T(1024)(128)(4,1)S(1)}, s32[]{:S(2)}) async-start(s8[8388608]{0:T(1024)(128)(4,1)} %bitcast.86), calls=%async_computation.5 | async-start | bytes 8388608
  286.5 5.5 copy-start.3
  293.0 13.7 %collective-permute-start.4 = (bf16[128,7680]{1,0:T(8,128)(2,1)}, bf16[128,7680]{1,0:T(8,128)(2,1)S(1)}, u32[]{:S(2)}, u32[]{:S(2)}) collective-permute-start(bf16[128,7680]{1,0:T(8,128)(2,1)} %get-tuple-element.78), channel_id=1, source_target_pairs={{0,16},{16,0},{1,17},{17,1},{2,18},{18,2},{3,19},{19,3},{4,20},{20... | collective-permute-start | bytes 5898248 | tf_op jit(solution)/shard_map/ppermute | solution.py:29
  510.5 6.1 %copy-start.11 = (f32[128,1024]{1,0:T(8,128)S(1)}, f32[128,1024]{1,0:T(8,128)}, u32[]{:S(2)}) copy-start(f32[128,1024]{1,0:T(8,128)} %reduce_group.3) | copy-start | bytes 1572868
  510.5 6.1 %copy-start.15 = (f32[128,1024]{1,0:T(8,128)S(1)}, f32[128,1024]{1,0:T(8,128)}, u32[]{:S(2)}) copy-start(f32[128,1024]{1,0:T(8,128)} %get-tuple-element.39) | copy-start | bytes 1572868
  518.1 7.2 %copy-start.33 = (f32[128]{0:T(128)S(1)}, f32[128]{0:T(128)}, u32[]{:S(2)}) copy-start(f32[128]{0:T(128)} %copy-done.32) | copy-start | bytes 1540
  518.1 7.2 %copy-start.29 = (f32[128]{0:T(128)S(1)}, f32[128]{0:T(128)}, u32[]{:S(2)}) copy-start(f32[128]{0:T(128)} %copy-done.28) | copy-start | bytes 1540
  518.1 8.3 %collective-permute-start.5 = (bf16[128,2560]{1,0:T(8,128)(2,1)S(1)}, bf16[128,2560]{1,0:T(8,128)(2,1)S(1)}, u32[]{:S(2)}, u32[]{:S(2)}) collective-permute-start(bf16[128,2560]{1,0:T(8,128)(2,1)S(1)} %pad_maximum_fusion.6), channel_id=1, source_target_pairs={{0,16},{16,0},{1,17},{17,1},{2,18},{18,2},{3,19},{19,3},{4,20},{20... | collective-permute-start | bytes 1966088 | tf_op jit(solution)/shard_map/ppermute | solution.py:29
  583.4 3.0 copy-start.16
  587.5 3.2 copy-start.1
  (19 other events, 30.4 us)
Sparse Core Ops, SparseCore 0:
  30.0 87.7 all-gather.1
  315.1 215.2 reduce-scatter.1

commit v5 on v4

--- a/solution.py
+++ b/solution.py
@@ -66,14 +66,35 @@
         axis=1,
     )
     starts = jnp.concatenate([jnp.zeros((1,), jnp.int32), ends[:-1]])
-    codes = jnp.concatenate(
-        [(keys % entries) // top_count * slots + picked, jnp.zeros((capacity,), jnp.int32)]
-    )
-    lists = jnp.stack(
-        [lax.dynamic_slice_in_dim(codes, starts[i], capacity) for i in range(owners)]
-    )
-    used = jnp.arange(capacity, dtype=jnp.int32)[None, :] < (ends - starts)[:, None]
-    return jnp.where(used, lists, heads * rows * slots)
+    codes = keys % entries // top_count * slots + picked
+    tall = -(-entries // 128)
+    codes = jnp.pad(codes, (0, tall * 128 - entries)).reshape(tall, 128)
+    long = capacity // 128
+    empty = heads * rows * slots
+
+    def kernel(starts_ref, ends_ref, codes_ref, lists_ref, padded):
+        padded[:tall, :] = codes_ref[...]
+        padded[tall:, :] = jnp.zeros((long + 8, 128), jnp.int32)
+        lane = lax.broadcasted_iota(jnp.int32, (long, 128), 1)
+        place = lax.broadcasted_iota(jnp.int32, (long, 128), 0) * 128 + lane
+
+        @pl.loop(0, owners)
+        def _(i):
+            start, end = starts_ref[i], ends_ref[i]
+            shift = start % 128
+            lines = padded[pl.ds(start // 128, long + 1), :]
+            turned = pltpu.roll(lines, (128 - shift) % 128, 1)
+            joined = jnp.where(lane < 128 - shift, turned[:long], turned[1:])
+            lists_ref[i] = jnp.where(place < end - start, joined, empty)
+
+    return pl.pallas_call(
+        kernel,
+        in_specs=[pl.BlockSpec(memory_space=pltpu.SMEM)] * 2 + [pl.BlockSpec(memory_space=pltpu.VMEM)],
+        out_shape=jax.ShapeDtypeStruct((owners, long, 128), jnp.int32),
+        scratch_shapes=[pltpu.VMEM((tall + long + 8, 128), jnp.int32)],
+        cost_estimate=lasting(3),
+        name="make_lists",
+    )(starts, ends, codes)
 
 
 def gather_rows(index, counts, memory_keys, memory_values, heads, sources, capacity):
@@ -156,6 +177,19 @@
     return start, extra
 
 
+def owned(id_ref, start, head, rows, span, least):
+    lines = id_ref[0, pl.ds(start // 128, span // 128), :]
+    token = lax.broadcasted_iota(jnp.int32, (rows, 128), 0) + head * rows
+    masks = []
+    for i in range(span // 128):
+        mask = lines[i : i + 1, :] == token
+        if least is not None:
+            place = lax.broadcasted_iota(jnp.int32, (1, 128), 1) + start + i * 128
+            mask = mask & (place >= least)
+        masks.append(mask)
+    return jnp.concatenate(masks, axis=1)
+
+
 def memory_forward(bounds, queries, key_rows, value_rows, row_ids, heads, sources, rows, score_scale):
     capacity, head_dim = key_rows.shape[0] // sources, key_rows.shape[1]
     width = heads * head_dim
@@ -163,16 +197,11 @@
 
     def kernel(bounds_ref, q_ref, k_ref, v_ref, id_ref, out_ref, sums, tops, totals):
         source = pl.program_id(0)
-        token = lax.broadcasted_iota(jnp.int32, (rows, span), 0)
         lane = lax.broadcasted_iota(jnp.int32, (rows, 128), 1) % 16
 
         def scores_of(head, start, least):
             here = pl.ds(pl.multiple_of(start, 128), span)
-            ids = id_ref[0, :, here]
-            mine = ids == token + head * rows
-            if least is not None:
-                place = lax.broadcasted_iota(jnp.int32, (1, span), 1) + start
-                mine = mine & (place >= least)
+            mine = owned(id_ref, start, head, rows, span, least)
             q = q_ref[:, head * head_dim : (head + 1) * head_dim]
             raw = lax.dot_general(q, k_ref[here, :], contract_cols, preferred_element_type=jnp.float32)
             return jnp.where(mine, raw * score_scale, masked_score), mine, v_ref[here, :]
@@ -233,7 +262,7 @@
                 pl.BlockSpec((rows, width), lambda i, *_: (i, 0)),
                 pl.BlockSpec((capacity, head_dim), lambda i, *_: (i, 0)),
                 pl.BlockSpec((capacity, head_dim), lambda i, *_: (i, 0)),
-                pl.BlockSpec((1, 1, capacity), lambda i, *_: (i, 0, 0)),
+                pl.BlockSpec((1, capacity // 128, 128), lambda i, *_: (i, 0, 0)),
             ],
             out_specs=pl.BlockSpec((rows, width + 128), lambda i, *_: (i, 0)),
             scratch_shapes=[
@@ -315,7 +344,6 @@
 
     def kernel(bounds_ref, q_ref, g_ref, k_ref, v_ref, id_ref, out_ref, sums):
         source = pl.program_id(0)
-        token = lax.broadcasted_iota(jnp.int32, (rows, span), 0)
         stat = joined_tile(g_ref[:, width : width + 128])
 
         def term(column):
@@ -324,10 +352,7 @@
         def part_of(head, start, least):
             here = pl.ds(pl.multiple_of(start, 128), span)
             columns = slice(head * head_dim, (head + 1) * head_dim)
-            mine = id_ref[0, :, here] == token + head * rows
-            if least is not None:
-                place = lax.broadcasted_iota(jnp.int32, (1, span), 1) + start
-                mine = mine & (place >= least)
+            mine = owned(id_ref, start, head, rows, span, least)
             k, v = k_ref[here, :], v_ref[here, :]
             raw = lax.dot_general(
                 q_ref[:, columns], k, contract_cols, preferred_element_type=jnp.float32
@@ -367,7 +392,7 @@
                 pl.BlockSpec((rows, width + 128), lambda i, *_: (i, 0)),
                 pl.BlockSpec((capacity, head_dim), lambda i, *_: (i, 0)),
                 pl.BlockSpec((capacity, head_dim), lambda i, *_: (i, 0)),
-                pl.BlockSpec((1, 1, capacity), lambda i, *_: (i, 0, 0)),
+                pl.BlockSpec((1, capacity // 128, 128), lambda i, *_: (i, 0, 0)),
             ],
             out_specs=pl.BlockSpec((rows, width), lambda i, *_: (i, 0)),
             scratch_shapes=[pltpu.VMEM((rows, width), jnp.float32)],
@@ -415,54 +440,139 @@
 def gather_group(block, sources, collective_id):
     rows, width = block.shape
     depth, half = sources // 4, rows // 2
-
-    def kernel(x_ref, out_ref, own_sem, send, recv_z, recv_x, recv_y, recv_a, recv_b):
-        me, column, beside_x, beside_y, across, index_of = grid_place(depth)
-        to_x, to_y = index_of(0, beside_x), index_of(0, beside_y)
-        greet([to_x, to_y] + [index_of(-k, column) for k in range(1, depth)])
-
-        def rows_of(index, part=None):
-            if part is None:
-                return out_ref.at[pl.ds(pl.multiple_of(index * rows, rows), rows), :]
-            return out_ref.at[pl.ds(pl.multiple_of(index * rows + part * half, half), half), :]
-
-        own = pltpu.make_async_copy(x_ref, rows_of(me), own_sem)
+    slots = 2 * depth - 1
+
+    def kernel(x_ref, out_ref, own_sem, send, recv):
+        me = lax.axis_index("mem")
+        layer, column = me // 4, me % 4
+        to_x = me + 1 - 2 * (column % 2)
+        to_y = me + 2 - 4 * (column // 2)
+        across = layer * 4 + 3 - column
+        has_above, has_below = layer + 1 < depth, layer > 0
+        barrier = pltpu.get_barrier_semaphore()
+
+        def signal(device):
+            pl.semaphore_signal(
+                barrier, inc=1, device_id={"mem": device}, device_id_type=pl.DeviceIdType.MESH
+            )
+
+        signal(to_x)
+        signal(to_y)
+        pl.when(has_above)(lambda: signal(me + 4))
+        pl.when(has_below)(lambda: signal(me - 4))
+        pl.semaphore_wait(barrier, 2 + has_above.astype(jnp.int32) + has_below.astype(jnp.int32))
+
+        def part_of(index, part):
+            start = pl.multiple_of(index * rows + part * half, half)
+            return out_ref.at[pl.ds(start, half), :]
+
+        own = pltpu.make_async_copy(x_ref, out_ref.at[pl.ds(pl.multiple_of(me * rows, rows), rows), :], own_sem)
         own.start()
         sent = []
 
-        def push(source, target, kind, k, recv, device):
-            copy = remote(source, target, send.at[kind, k], recv.at[k], device)
-            copy.start()
-            sent.append(copy)
-
-        def arrived(target, recv, k):
-            remote(target, target, send.at[0, 0], recv.at[k], to_x).wait_recv()
-
-        push(x_ref, rows_of(me), 1, 0, recv_x, to_x)
-        push(x_ref, rows_of(me), 2, 0, recv_y, to_y)
-        for k in range(1, depth):
-            push(x_ref, rows_of(me), 0, k, recv_z, index_of(-k, column))
-
-        def pass_on(k):
-            from_x, from_y = index_of(k, beside_x), index_of(k, beside_y)
-            arrived(rows_of(from_x), recv_x, k)
-            push(rows_of(from_x, 0), rows_of(from_x, 0), 3, k, recv_a, to_y)
-            arrived(rows_of(from_y), recv_y, k)
-            push(rows_of(from_y, 1), rows_of(from_y, 1), 4, k, recv_b, to_x)
-
-        for k in range(1, depth):
-            above = index_of(k, column)
-            arrived(rows_of(above), recv_z, k)
-            push(rows_of(above), rows_of(above), 1, k, recv_x, to_x)
-            push(rows_of(above), rows_of(above), 2, k, recv_y, to_y)
-            pass_on(k - 1)
-        pass_on(depth - 1)
-        for k in range(depth):
-            far = index_of(k, across)
-            arrived(rows_of(far, 0), recv_a, k)
-            arrived(rows_of(far, 1), recv_b, k)
-        for copy in sent:
-            copy.wait_send()
+        def push(condition, source, target, kind, slot, to_slot, part, device):
+            copy = remote(source, target, send.at[kind, slot, part], recv.at[kind, to_slot, part], device)
+            if condition is None:
+                copy.start()
+            else:
+                pl.when(condition)(copy.start)
+            sent.append((condition, copy))
+
+        def arrived(index, kind, slot, part):
+            target = part_of(index, part)
+            remote(target, target, send.at[kind, slot, part], recv.at[kind, slot, part], to_x).wait_recv()
+
+        def up_slot(distance):
+            return distance
+
+        def down_slot(distance):
+            return depth - 1 + distance
+
+        for part in (0, 1):
+            mine = x_ref.at[pl.ds(part * half, half), :]
+            push(has_above, mine, part_of(me, part), 0, 0, down_slot(1), part, me + 4)
+            push(has_below, mine, part_of(me, part), 1, 0, up_slot(1), part, me - 4)
+            mine_y = x_ref.at[pl.ds((1 - part) * half, half), :]
+            push(None, mine, part_of(me, part), 2, 0, 0, part, to_x)
+            push(None, mine_y, part_of(me, 1 - part), 3, 0, 0, 1 - part, to_y)
+
+        def pass_on(condition, step, slot):
+            def go():
+                arrived(to_x + step, 2, slot, 0)
+                copy_a.start()
+                arrived(to_y + step, 3, slot, 1)
+                copy_b.start()
+
+            source_a, source_b = part_of(to_x + step, 0), part_of(to_y + step, 1)
+            copy_a = remote(source_a, source_a, send.at[4, slot, 0], recv.at[4, slot, 0], to_y)
+            copy_b = remote(source_b, source_b, send.at[5, slot, 1], recv.at[5, slot, 1], to_x)
+            sent.append((condition, copy_a))
+            sent.append((condition, copy_b))
+            if condition is None:
+                go()
+            else:
+                pl.when(condition)(go)
+
+        for distance in range(1, depth):
+            from_above, from_below = layer + distance < depth, layer - distance >= 0
+
+            def take(kind, back_kind, step, slot, next_slot, onward, onward_device):
+                for part in (0, 1):
+                    arrived(me + step, kind, slot, part)
+                    here = part_of(me + step, part)
+                    if next_slot is not None:
+                        pl.when(onward)(
+                            remote(
+                                here, here, send.at[kind, slot, part], recv.at[kind, next_slot, part], onward_device
+                            ).start
+                        )
+                    remote(here, here, send.at[2, slot, part], recv.at[2, slot, part], to_x).start()
+                    remote(here, here, send.at[3, slot, part], recv.at[3, slot, part], to_y).start()
+
+            last = distance == depth - 1
+            pl.when(from_above)(
+                lambda: take(
+                    1, 0, 4 * distance, up_slot(distance), None if last else up_slot(distance + 1), has_below, me - 4
+                )
+            )
+            pl.when(from_below)(
+                lambda: take(
+                    0, 1, -4 * distance, down_slot(distance), None if last else down_slot(distance + 1), has_above, me + 4
+                )
+            )
+            for condition, step, slot, kind, onward in (
+                (from_above, 4 * distance, up_slot(distance), 1, has_below),
+                (from_below, -4 * distance, down_slot(distance), 0, has_above),
+            ):
+                for part in (0, 1):
+                    here = part_of(me + step, part)
+                    if not last:
+                        sent.append((condition & onward, remote(here, here, send.at[kind, slot, part], own_sem, me)))
+                    sent.append((condition, remote(here, here, send.at[2, slot, part], own_sem, to_x)))
+                    sent.append((condition, remote(here, here, send.at[3, slot, part], own_sem, to_y)))
+            if distance == 1:
+                pass_on(None, 0, 0)
+            else:
+                pass_on(layer + distance - 1 < depth, 4 * (distance - 1), up_slot(distance - 1))
+                pass_on(layer - distance + 1 >= 0, -4 * (distance - 1), down_slot(distance - 1))
+        pass_on(layer + depth - 1 < depth, 4 * (depth - 1), up_slot(depth - 1))
+        pass_on(layer - depth + 1 >= 0, -4 * (depth - 1), down_slot(depth - 1))
+
+        def close(step, slot):
+            arrived(to_x + step, 2, slot, 1)
+            arrived(to_y + step, 3, slot, 0)
+            arrived(across + step, 4, slot, 0)
+            arrived(across + step, 5, slot, 1)
+
+        close(0, 0)
+        for distance in range(1, depth):
+            pl.when(layer + distance < depth)(lambda: close(4 * distance, up_slot(distance)))
+            pl.when(layer - distance >= 0)(lambda: close(-4 * distance, down_slot(distance)))
+        for condition, copy in sent:
+            if condition is None:
+                copy.wait_send()
+            else:
+                pl.when(condition)(copy.wait_send)
         own.wait()
 
     return pl.pallas_call(
@@ -470,8 +580,11 @@
         in_specs=[pl.BlockSpec(memory_space=pl.ANY)],
         out_specs=pl.BlockSpec(memory_space=pl.ANY),
         out_shape=jax.ShapeDtypeStruct((sources * rows, width), block.dtype),
-        scratch_shapes=[pltpu.SemaphoreType.DMA, pltpu.SemaphoreType.DMA((5, depth))]
-        + [pltpu.SemaphoreType.DMA((depth,))] * 5,
+        scratch_shapes=[
+            pltpu.SemaphoreType.DMA,
+            pltpu.SemaphoreType.DMA((6, slots, 2)),
+            pltpu.SemaphoreType.DMA((6, slots, 2)),
+        ],
         compiler_params=pltpu.CompilerParams(
             collective_id=collective_id, has_side_effects=True, vmem_limit_bytes=VMEM_LIMIT
         ),
@@ -480,83 +593,118 @@
     )(block)
 
 
+def reduce_steps(parts_ref, sources, refs, sems, merge, pack):
+    half_a, half_b, from_x, from_y, from_z, out_x, out_y, out_z = refs
+    send, recv_a, recv_b, recv_x, recv_y, recv_z = sems
+    rows = parts_ref.shape[0] // sources
+    depth, half = sources // 4, rows // 2
+    me, column, beside_x, beside_y, across, index_of = grid_place(depth)
+    to_x, to_y = index_of(0, beside_x), index_of(0, beside_y)
+    order = [*range(1, depth), 0]
+    queues, sent = {"x": [], "y": [], "z": []}, []
+
+    def piece(index, part):
+        return parts_ref.at[pl.ds(pl.multiple_of(index * rows + part * half, half), half), :]
+
+    def part_rows(part):
+        return pl.ds(part * half, half)
+
+    def push(link, source, target, kind, k, recv_sem, device):
+        queue = queues[link]
+        if link != "z" and len(queue) >= 2:
+            queue.pop(0).wait_send()
+        copy = remote(source, target, send.at[kind, k], recv_sem, device)
+        copy.start()
+        queue.append(copy)
+
+    def arrived(target, recv_sem):
+        remote(target, target, send.at[0, 0], recv_sem, to_x).wait_recv()
+
+    def plane_rest(k):
+        push("x", piece(index_of(k, beside_x), 0), from_x.at[k, part_rows(0)], 2, k, recv_x.at[0, k], to_x)
+        push("y", piece(index_of(k, beside_y), 1), from_y.at[k, part_rows(1)], 3, k, recv_y.at[1, k], to_y)
+
+    def plane_merged(k):
+        arrived(half_a.at[k], recv_a.at[k])
+        pack(out_y.at[k], merge([piece(index_of(k, beside_y), 0), half_a.at[k]]))
+        push("y", out_y.at[k], from_y.at[k, part_rows(0)], 4, k, recv_y.at[0, k], to_y)
+        arrived(half_b.at[k], recv_b.at[k])
+        pack(out_x.at[k], merge([piece(index_of(k, beside_x), 1), half_b.at[k]]))
+        push("x", out_x.at[k], from_x.at[k, part_rows(1)], 5, k, recv_x.at[1, k], to_x)
+
+    def column_step(k):
+        for part in (0, 1):
+            here = part_rows(part)
+            arrived(from_x.at[k, here], recv_x.at[part, k])
+            arrived(from_y.at[k, here], recv_y.at[part, k])
+            if k:
+                blocks = [piece(index_of(k, column), part), from_x.at[k, here], from_y.at[k, here]]
+                pack(out_z.at[k, here], merge(blocks))
+        if k:
+            push("z", out_z.at[k], from_z.at[k], 6, k, recv_z.at[k], index_of(k, column))
+
+    for k in order:
+        far = index_of(k, across)
+        push("x", piece(far, 0), half_a.at[k], 0, k, recv_a.at[k], to_x)
+        push("y", piece(far, 1), half_b.at[k], 1, k, recv_b.at[k], to_y)
+    for i, k in enumerate(order):
+        plane_rest(k)
+        plane_merged(k)
+        if i:
+            column_step(order[i - 1])
+    column_step(order[-1])
+    for k in range(1, depth):
+        arrived(from_z.at[k], recv_z.at[k])
+    final = []
+    for part in (0, 1):
+        here = part_rows(part)
+        blocks = [piece(me, part), from_x.at[0, here], from_y.at[0, here]]
+        final.append((here, blocks + [from_z.at[k, here] for k in range(1, depth)]))
+    return final, [copy for queue in queues.values() for copy in queue]
+
+
+def reduce_scratch(rows, width, dtype, sources):
+    depth, half = sources // 4, rows // 2
+
+    def slots(size):
+        return pltpu.VMEM((depth, size, width), dtype)
+
+    refs = [slots(half), slots(half), slots(rows), slots(rows), slots(rows)]
+    refs += [slots(half), slots(half), slots(rows)]
+    sems = [pltpu.SemaphoreType.DMA((7, depth))]
+    sems += [pltpu.SemaphoreType.DMA((depth,))] * 2
+    sems += [pltpu.SemaphoreType.DMA((2, depth))] * 2
+    sems += [pltpu.SemaphoreType.DMA((depth,))]
+    return refs, sems
+
+
 def reduce_group(parts, sources, collective_id, merge, pack, finish, out_shape):
     rows, width = parts.shape[0] // sources, parts.shape[1]
-    depth, half = sources // 4, rows // 2
+    depth = sources // 4
     outs = len(out_shape)
+    ref_shapes, sem_shapes = reduce_scratch(rows, width, parts.dtype, sources)
 
     def kernel(parts_ref, *refs):
-        out_refs = refs[:outs]
-        half_a, half_b, from_x, from_y, from_z, out_x, out_y, out_z = refs[outs : outs + 8]
-        send, recv_a, recv_b, recv_x, recv_y, recv_z = refs[outs + 8 :]
+        out_refs, refs = refs[:outs], refs[outs:]
         me, column, beside_x, beside_y, across, index_of = grid_place(depth)
-        to_x, to_y = index_of(0, beside_x), index_of(0, beside_y)
-        greet([to_x, to_y] + [index_of(-k, column) for k in range(1, depth)])
-        order = [*range(1, depth), 0]
-        sent = []
-
-        def piece(index, part):
-            return parts_ref.at[pl.ds(pl.multiple_of(index * rows + part * half, half), half), :]
-
-        def part_rows(part):
-            return pl.ds(part * half, half)
-
-        def push(source, target, kind, k, recv_sem, device):
-            copy = remote(source, target, send.at[kind, k], recv_sem, device)
-            copy.start()
-            sent.append(copy)
-
-        def arrived(target, recv_sem):
-            remote(target, target, send.at[0, 0], recv_sem, to_x).wait_recv()
-
-        for k in order:
-            far = index_of(k, across)
-            push(piece(far, 0), half_a.at[k], 0, k, recv_a.at[k], to_x)
-            push(piece(far, 1), half_b.at[k], 1, k, recv_b.at[k], to_y)
-        for k in order:
-            push(piece(index_of(k, beside_x), 0), from_x.at[k, part_rows(0)], 2, k, recv_x.at[0, k], to_x)
-            push(piece(index_of(k, beside_y), 1), from_y.at[k, part_rows(1)], 3, k, recv_y.at[1, k], to_y)
-        for k in order:
-            arrived(half_a.at[k], recv_a.at[k])
-            pack(out_y.at[k], merge([piece(index_of(k, beside_y), 0), half_a.at[k]]))
-            push(out_y.at[k], from_y.at[k, part_rows(0)], 4, k, recv_y.at[0, k], to_y)
-            arrived(half_b.at[k], recv_b.at[k])
-            pack(out_x.at[k], merge([piece(index_of(k, beside_x), 1), half_b.at[k]]))
-            push(out_x.at[k], from_x.at[k, part_rows(1)], 5, k, recv_x.at[1, k], to_x)
-        for k in order:
-            for part in (0, 1):
-                arrived(from_x.at[k, part_rows(part)], recv_x.at[part, k])
-                arrived(from_y.at[k, part_rows(part)], recv_y.at[part, k])
-            if k:
-                for part in (0, 1):
-                    here = part_rows(part)
-                    blocks = [piece(index_of(k, column), part), from_x.at[k, here], from_y.at[k, here]]
-                    pack(out_z.at[k, here], merge(blocks))
-                push(out_z.at[k], from_z.at[k], 6, k, recv_z.at[k], index_of(k, column))
-        for k in range(1, depth):
-            arrived(from_z.at[k], recv_z.at[k])
-        for part in (0, 1):
-            here = part_rows(part)
-            blocks = [piece(me, part), from_x.at[0, here], from_y.at[0, here]]
-            blocks += [from_z.at[k, here] for k in range(1, depth)]
+        greet(
+            [index_of(0, beside_x), index_of(0, beside_y)]
+            + [index_of(-k, column) for k in range(1, depth)]
+        )
+        final, still_open = reduce_steps(
+            parts_ref, sources, refs[: len(ref_shapes)], refs[len(ref_shapes) :], merge, pack
+        )
+        for here, blocks in final:
             finish([out.at[here] for out in out_refs], merge(blocks))
-        for copy in sent:
+        for copy in still_open:
             copy.wait_send()
-
-    def slots(size):
-        return pltpu.VMEM((depth, size, width), parts.dtype)
 
     return pl.pallas_call(
         kernel,
         in_specs=[pl.BlockSpec(memory_space=pltpu.VMEM)],
         out_specs=[pl.BlockSpec(memory_space=pltpu.VMEM)] * outs,
         out_shape=out_shape,
-        scratch_shapes=[slots(half), slots(half), slots(rows), slots(rows), slots(rows)]
-        + [slots(half), slots(half), slots(rows)]
-        + [pltpu.SemaphoreType.DMA((7, depth))]
-        + [pltpu.SemaphoreType.DMA((depth,))] * 2
-        + [pltpu.SemaphoreType.DMA((2, depth))] * 2
-        + [pltpu.SemaphoreType.DMA((depth,))],
+        scratch_shapes=ref_shapes + sem_shapes,
         compiler_params=pltpu.CompilerParams(
             collective_id=collective_id, has_side_effects=True, vmem_limit_bytes=VMEM_LIMIT
         ),
@@ -895,44 +1043,29 @@
 
 def finish_grads(parts, early, small, sources, collective_id):
     rows, width = parts.shape[0] // sources, parts.shape[1]
-    depth, half = sources // 4, rows // 2
-    early_width = early.shape[1]
     mesh_type = pl.DeviceIdType.MESH
+    ref_shapes, sem_shapes = reduce_scratch(rows, width, parts.dtype, sources)
 
     def kernel(parts_ref, early_ref, small_ref, late_out, early_out, small_out, *refs):
-        half_a, half_b, from_x, from_y, from_z, out_x, out_y, out_z, smalls, core_small = refs[:10]
-        send, recv_a, recv_b, recv_x, recv_y, recv_z, small_send, small_recv, core_send, core_recv = refs[10:]
-        me, column, beside_x, beside_y, across, index_of = grid_place(depth)
-        core = lax.axis_index("dp")
-        to_x, to_y = index_of(0, beside_x), index_of(0, beside_y)
+        steps_refs, refs = refs[: len(ref_shapes)], refs[len(ref_shapes) :]
+        steps_sems, refs = refs[: len(sem_shapes)], refs[len(sem_shapes) :]
+        smalls, core_small, small_send, small_recv, core_send, core_recv = refs
+        me, core = lax.axis_index("mem"), lax.axis_index("dp")
         barrier = pltpu.get_barrier_semaphore()
         peers = [lax.rem(me + k, sources) for k in range(1, sources)]
         for peer in peers:
             pl.semaphore_signal(barrier, inc=1, device_id={"mem": peer}, device_id_type=mesh_type)
         pl.semaphore_signal(barrier, inc=1, device_id={"dp": 1 - core}, device_id_type=mesh_type)
         pl.semaphore_wait(barrier, sources)
-        order = [*range(1, depth), 0]
-        sent = []
-
-        def piece(index, part):
-            return parts_ref.at[pl.ds(pl.multiple_of(index * rows + part * half, half), half), :]
-
-        def part_rows(part):
-            return pl.ds(part * half, half)
-
-        def push(source, target, kind, k, recv_sem, device):
-            copy = remote(source, target, send.at[kind, k], recv_sem, device)
-            copy.start()
-            sent.append(copy)
-
-        def arrived(target, recv_sem):
-            remote(target, target, send.at[0, 0], recv_sem, to_x).wait_recv()
-
-        def added(blocks):
+
+        def merge(blocks):
             total = blocks[0][...].astype(jnp.float32)
             for block in blocks[1:]:
                 total = total + block[...].astype(jnp.float32)
             return total
+
+        def pack(target, total):
+            target[...] = total.astype(parts.dtype)
 
         def across_cores(source, target, i):
             copy = pltpu.make_async_remote_copy(
@@ -946,60 +1079,33 @@
             copy.start()
             return copy
 
-        for k in order:
-            far = index_of(k, across)
-            push(piece(far, 0), half_a.at[k], 0, k, recv_a.at[k], to_x)
-            push(piece(far, 1), half_b.at[k], 1, k, recv_b.at[k], to_y)
         smalls[me] = small_ref[...]
-        for i, peer in enumerate(peers):
-            copy = remote(small_ref, smalls.at[me], small_send.at[i], small_recv.at[me], peer)
+        small_copies = [
+            remote(small_ref, smalls.at[me], small_send.at[i], small_recv.at[me], peer)
+            for i, peer in enumerate(peers)
+        ]
+        for copy in small_copies:
             copy.start()
-            sent.append(copy)
         early_copy = across_cores(early_ref, early_out.at[core], 0)
         early_out[core] = early_ref[...]
-        for k in order:
-            push(piece(index_of(k, beside_x), 0), from_x.at[k, part_rows(0)], 2, k, recv_x.at[0, k], to_x)
-            push(piece(index_of(k, beside_y), 1), from_y.at[k, part_rows(1)], 3, k, recv_y.at[1, k], to_y)
-        for k in order:
-            arrived(half_a.at[k], recv_a.at[k])
-            out_y[k] = added([piece(index_of(k, beside_y), 0), half_a.at[k]]).astype(parts.dtype)
-            push(out_y.at[k], from_y.at[k, part_rows(0)], 4, k, recv_y.at[0, k], to_y)
-            arrived(half_b.at[k], recv_b.at[k])
-            out_x[k] = added([piece(index_of(k, beside_x), 1), half_b.at[k]]).astype(parts.dtype)
-            push(out_x.at[k], from_x.at[k, part_rows(1)], 5, k, recv_x.at[1, k], to_x)
+        final, still_open = reduce_steps(parts_ref, sources, steps_refs, steps_sems, merge, pack)
+        for here, blocks in final:
+            late_out[core, here] = merge(blocks).astype(parts.dtype)
+        late_copy = across_cores(late_out.at[core], late_out.at[core], 2)
         for peer in peers:
-            arrived(smalls.at[peer], small_recv.at[peer])
+            remote(
+                smalls.at[peer], smalls.at[peer], small_send.at[0], small_recv.at[peer], peer
+            ).wait_recv()
         group_small = smalls[0]
         for i in range(1, sources):
             group_small = group_small + smalls[i]
         core_small[0] = group_small
         small_copy = across_cores(core_small.at[0], core_small.at[1], 1)
-        for k in order:
-            for part in (0, 1):
-                arrived(from_x.at[k, part_rows(part)], recv_x.at[part, k])
-                arrived(from_y.at[k, part_rows(part)], recv_y.at[part, k])
-            if k:
-                for part in (0, 1):
-                    here = part_rows(part)
-                    blocks = [piece(index_of(k, column), part), from_x.at[k, here], from_y.at[k, here]]
-                    out_z[k, here] = added(blocks).astype(parts.dtype)
-                push(out_z.at[k], from_z.at[k], 6, k, recv_z.at[k], index_of(k, column))
-        for k in range(1, depth):
-            arrived(from_z.at[k], recv_z.at[k])
-        for part in (0, 1):
-            here = part_rows(part)
-            blocks = [piece(me, part), from_x.at[0, here], from_y.at[0, here]]
-            blocks += [from_z.at[k, here] for k in range(1, depth)]
-            late_out[core, here] = added(blocks).astype(parts.dtype)
-        late_copy = across_cores(late_out.at[core], late_out.at[core], 2)
-        for copy in (early_copy, small_copy, late_copy):
+        for copy in (early_copy, late_copy, small_copy):
             copy.wait()
         small_out[...] = core_small[0] + core_small[1]
-        for copy in sent:
+        for copy in still_open + small_copies:
             copy.wait_send()
-
-    def slots(size):
-        return pltpu.VMEM((depth, size, width), parts.dtype)
 
     vmem = pl.BlockSpec(memory_space=pltpu.VMEM)
     return pl.pallas_call(
@@ -1008,22 +1114,18 @@
         out_specs=[vmem] * 3,
         out_shape=[
             jax.ShapeDtypeStruct((2, rows, width), parts.dtype),
-            jax.ShapeDtypeStruct((2, rows, early_width), early.dtype),
+            jax.ShapeDtypeStruct((2, *early.shape), early.dtype),
             jax.ShapeDtypeStruct(small.shape, small.dtype),
         ],
-        scratch_shapes=[slots(half), slots(half), slots(rows), slots(rows), slots(rows)]
-        + [slots(half), slots(half), slots(rows)]
+        scratch_shapes=ref_shapes
+        + sem_shapes
         + [pltpu.VMEM((sources, *small.shape), small.dtype), pltpu.VMEM((2, *small.shape), small.dtype)]
-        + [pltpu.SemaphoreType.DMA((7, depth))]
-        + [pltpu.SemaphoreType.DMA((depth,))] * 2
-        + [pltpu.SemaphoreType.DMA((2, depth))] * 2
-        + [pltpu.SemaphoreType.DMA((depth,))]
         + [pltpu.SemaphoreType.DMA((sources,))] * 2
         + [pltpu.SemaphoreType.DMA((3,))] * 2,
         compiler_params=pltpu.CompilerParams(
             collective_id=collective_id, has_side_effects=True, vmem_limit_bytes=VMEM_LIMIT
         ),
-        cost_estimate=lasting(55),
+        cost_estimate=lasting(45),
         name="finish_grads",
     )(parts, early, small)
 
@@ -1052,7 +1154,7 @@
     top_count = slot_index.shape[2]
     hidden = up_weight.shape[1]
     groups = lax.axis_size("mem")
-    capacity = max(2, 3 * rows * heads * top_count // (2 * groups))
+    capacity = -(-3 * rows * heads * top_count // (2 * groups) // 128) * 128
     score_scale = 1.0 / math.sqrt(head_dim)
     repeats = W // rows
     span = W + 2 * rows
@@ -1090,19 +1192,18 @@
     incoming = lax.all_to_all(requests, "mem", split_axis=0, concat_axis=0, tiled=True)
     row_ids = incoming // slots
     limits = jnp.arange(heads + 1, dtype=jnp.int32) * (rows * slots)
-    bounds = jnp.sum((incoming[:, None, :] < limits[None, :, None]).astype(jnp.int32), axis=2)
+    bounds = jnp.sum((incoming[:, None] < limits[None, :, None, None]).astype(jnp.int32), axis=(2, 3))
     index = jnp.where(row_ids < heads * rows, row_ids // rows * slots + incoming % slots, 0)
     key_rows, value_rows = gather_rows(
         index.reshape(-1), bounds[:, heads], memory_keys, memory_values, heads, groups, capacity
     )
     all_queries = lax.all_gather(projected[:, :width], "mem", axis=0, tiled=True)
-    entry_rows = row_ids[:, None, :]
     partial = memory_forward(
         bounds.reshape(-1),
         all_queries,
         key_rows,
         value_rows,
-        entry_rows,
+        row_ids,
         heads,
         groups,
         rows,
@@ -1171,7 +1272,7 @@
         all_grads,
         key_rows,
         value_rows,
-        entry_rows,
+        row_ids,
         heads,
         groups,
         rows,

time: 608 us -> 589 us (0.969)
  waiting for transfers between devices: 4.78 us -> 36.2 us
  Pallas kernels: 421 us -> 390 us
  between operations: 44 us -> 15.3 us
  starting transfers between devices: 24.4 us -> 33.9 us
    pallas_call x2, Pallas kernels: 175 us -> 145 us  [reduce_group(): pl.pallas_call(kernel, in_specs=[pl.BlockSpec(memory_space=pltpu.VMEM)],...]
    all_to_all x1, waiting for transfers between devices: 3.36 us -> 27.7 us  [on_device(): lax.all_to_all(requests, 'mem', split_axis=0, concat_axis=0, tiled=True)]
    ppermute x2, starting transfers between devices: 6.45 us -> 16 us  [swapped(): return lax.ppermute(value, 'dp', [(0, 1), (1, 0)])]
    reduce_scatter x1, waiting for transfers between devices: 1.37 us -> 8.45 us  [scattered(): return lax.psum_scatter(halves, 'mem', scatter_dimension=0, tiled=True)]
where the time goes in v5:
time: 589 us; the launch traced here: 579 us
  Pallas kernels  390 us (66%)
  other arithmetic  44.2 us (8%)
  matrix products  39.1 us (7%)
  waiting for transfers between devices  36.2 us (6%)
  starting transfers between devices  33.9 us (6%)
  local copies, waits for them, and re-layouts  20.5 us (3%)
  between operations  15.3 us (3%)
    pallas_call x2, Pallas kernels, reduce_group(): pl.pallas_call(kernel, in_specs=[pl.BlockSpec(memory_space=pltpu.VMEM)],...  145 us
    pallas_call x1, Pallas kernels, gather_group(): pl.pallas_call(kernel, in_specs=[pl.BlockSpec(memory_space=pl.ANY)], out_...  57 us
    pallas_call x1, Pallas kernels, finish_grads(): pl.pallas_call(kernel, in_specs=[vmem] * 3, out_specs=[vmem] * 3, out_sha...  44.2 us
    pallas_call x1, Pallas kernels, gather_rows(): pl.pallas_call(kernel, grid_spec=pltpu.PrefetchScalarGridSpec(num_scalar_...  43.2 us
    pallas_call x1, Pallas kernels, memory_forward(): pl.pallas_call(kernel, grid_spec=pltpu.PrefetchScalarGridSpec(num_scalar_...  42 us
    pallas_call x1, Pallas kernels, memory_backward(): pl.pallas_call(kernel, grid_spec=pltpu.PrefetchScalarGridSpec(num_scalar_...  35.5 us
    all_to_all x1, waiting for transfers between devices, on_device(): lax.all_to_all(requests, 'mem', split_axis=0, concat_axis=0, tiled=True)  27.7 us
    sort x1, other arithmetic, place_requests(): lax.sort(((owner * entries + place).reshape(-1), slot_index.reshape(-1)),...  18.5 us
  transfers between devices with their start and end apart: 9, of which 2 were waited for; matrix products, arithmetic and copies ran while one was open for 9% of the time, Pallas kernels for 42%

profile of v5, /device:TPU:9, one launch (start us, length us, event | category | flops | bytes accessed | tf_op | source)
XLA Modules:
  0.0 579.1 jit_solution(4275263965945901055)
XLA Ops:
  10.8 3.9 convolution_convert_fusion.3.own_ref
  16.3 3.1 collective-permute-start.3
  19.4 3.2 collective-permute-start.2
  22.6 4.1 collective-permute-start.1
  26.7 3.2 collective-permute-start
  32.4 18.5 %sort.23 = (s32[32768]{0:T(1024)S(1)}, s32[32768]{0:T(1024)S(1)}, s32[32768]{0:T(1024)}) sort(s32[32768]{0:T(1024)S(1)} %reshape.246, s32[32768]{0:T(1024)} %reshape.247, s32[32768]{0:T(1024)S(1)} %iota.53), dimensions={0}, to_apply=%region_0.0 | sort | flops 491520 | bytes 786432 | tf_op jit(solution)/shard_map/sort | solution.py:61
  52.9 2.8 make_lists.1
  55.7 4.3 all-to-all-start
  62.4 27.7 %all-to-all-done = s32[16,24,128]{2,1,0:T(8,128)S(1)} async-done(((s32[16,24,128]{2,1,0:T(8,128)}), s32[16,24,128]{2,1,0:T(8,128)S(1)}, u32[]{:S(2)}, u32[]{:S(2)}) %all-to-all-start) | async-done | bytes 196640 | tf_op jit(solution)/shard_map/all_to_all | solution.py:1192
  90.0 2.7 convert_reduce_fusion.1
  95.1 43.2 %gather_rows.1 = (bf16[49152,128]{1,0:T(8,128)(2,1)}, bf16[49152,128]{1,0:T(8,128)(2,1)}) custom-call(s32[49152]{0:T(1024)} %bitcast.56, s32[16]{0:T(128)} %slice_reduce_fusion.counts_ref, bf16[4096,1024]{1,0:T(8,128)(2,1)} %keys.1, bf16[4096,1024]{1,0:T(8,128)(2,1)} %values.1), custom_call_target="tpu_custom_call" | custom-call | bytes 126000000 | tf_op jit(solution)/shard_map/gather_rows/pallas_call | solution.py:137
  139.7 6.7 %local_forward.1 = (f32[128,1024]{1,0:T(8,128)}, f32[128,128]{1,0:T(8,128)}) custom-call(f32[8,768]{1,0:T(8,128)} %pad.12.base_ref, s32[128,128]{1,0:T(8,128)} %broadcast_in_dim.24.column_ref, s32[8,640]{1,0:T(8,128)} %broadcast_in_dim.26.row_ref, bf16[128,3072]{1,0:T(8,128)(2,1)} %copy-done.2, bf16[128,2048]{1,0:T(8,128)(2,1)} %collective-permute-done.refs_0_, ...), custom_call_target="tpu_custom_call" | custom-call | bytes 30000000 | tf_op jit(solution)/shard_map/local_forward/pallas_call | solution.py:885
  146.4 42.0 %memory_forward.1.parts_ref = bf16[2048,1152]{1,0:T(8,128)(2,1)} custom-call(s32[144]{0:T(256)} %reshape.249.bounds_ref, bf16[2048,1024]{1,0:T(8,128)(2,1)} %all-gather.2.cloned.1.call-done.q_ref.refs_0_.refs_1_.refs_2_.refs_3_.refs_4_, bf16[49152,128]{1,0:T(8,128)(2,1)} %get-tuple-element.33.k_ref, bf16[49152,128]{1,0:T(8,128)(2,1)} %get-tuple-element.34.v_ref, ...), custom_call_target="tpu_custom_call" | custom-call | bytes 123000000 | tf_op jit(solution)/shard_map/memory_forward/pallas_call | solution.py:256
  188.5 63.3 %reduce_group.2 = (f32[128,1024]{1,0:T(8,128)}, f32[128,128]{1,0:T(8,128)}) custom-call(bf16[2048,1152]{1,0:T(8,128)(2,1)} %memory_forward.1.parts_ref), custom_call_target="tpu_custom_call" | custom-call | bytes 165000000 | tf_op jit(solution)/shard_map/reduce_group/pallas_call | solution.py:702
  251.8 2.0 constant_dynamic-update-slice_fusion.2
  255.9 4.8 fusion.71
  260.7 6.8 %add_convert_fusion = (bf16[128,4096]{1,0:T(8,128)(2,1)S(1)}, f32[128,4096]{1,0:T(8,128)S(1)}) fusion(f32[128,4096]{1,0:T(8,128)S(1)} %fusion.71, bf16[128,1024]{1,0:T(8,128)(2,1)S(1)} %copy-done.5, bf16[1024,4096]{1,0:T(8,128)(2,1)S(1)} %bitcast.55), kind=kOutput, calls=%fused_computation.7 | convolution fusion | flops 1111490560 | bytes 13893632 | tf_op jit(solution)/shard_map/dot_general | solution.py:1236
  267.8 3.0 multiply_reduce_fusion
  274.1 15.3 %collective-permute-start.4 = (bf16[128,7680]{1,0:T(8,128)(2,1)}, bf16[128,7680]{1,0:T(8,128)(2,1)S(1)}, u32[]{:S(2)}, u32[]{:S(2)}) collective-permute-start(bf16[128,7680]{1,0:T(8,128)(2,1)} %get-tuple-element.78), channel_id=1, source_target_pairs={{0,16},{16,0},{1,17},{17,1},{2,18},{18,2},{3,19},{19,3},{4,20},{20... | collective-permute-start | bytes 5898248 | tf_op jit(solution)/shard_map/ppermute | solution.py:29
  289.4 1.6 fusion.72.mix_ref
  291.1 7.0 %local_queries.1 = (f32[128,1024]{1,0:T(8,128)}, f32[8,768]{1,0:T(8,128)}, f32[8,128]{1,0:T(8,128)}, bf16[128,1152]{1,0:T(8,128)(2,1)}) custom-call(f32[8,768]{1,0:T(8,128)} %pad.12.base_ref, s32[128,128]{1,0:T(8,128)} %broadcast_in_dim.24.column_ref, s32[8,640]{1,0:T(8,128)} %broadcast_in_dim.26.row_ref, bf16[128,3072]{1,0:T(8,128)(2,1)} %copy-done.2, ...), custom_call_target="tpu_custom_call" | custom-call | bytes 45000000 | tf_op jit(solution)/shard_map/local_queries/pallas_call | solution.py:962
  301.4 4.9 pad_maximum_fusion
  308.2 7.0 %fusion.6 = bf16[128,1024]{1,0:T(8,128)(2,1)} fusion(f32[128,1024]{1,0:T(8,128)S(1)} %get-tuple-element.90, bf16[128,4096]{1,0:T(8,128)(2,1)S(1)} %copy-done.4, bf16[1024,4096]{1,0:T(8,128)(2,1)} %param.24), kind=kOutput, calls=%fused_computation.27 | convolution fusion | flops 1074003968 | bytes 10223616 | tf_op jit(solution)/shard_map/dot_general | solution.py:1232
  315.2 57.0 %gather_group.1.g_ref.refs_5_.refs_6_.refs_7_.refs_8_.refs_9_ = bf16[2048,1152]{1,0:T(8,128)(2,1)} custom-call(bf16[128,1152]{1,0:T(8,128)(2,1)} %get-tuple-element.41.x_ref), custom_call_target="tpu_custom_call" | custom-call | bytes 150000000 | tf_op jit(solution)/shard_map/gather_group/pallas_call | solution.py:578
  372.1 35.5 %memory_backward.1.parts_ref = bf16[2048,1024]{1,0:T(8,128)(2,1)} custom-call(s32[144]{0:T(256)} %reshape.249.bounds_ref, bf16[2048,1024]{1,0:T(8,128)(2,1)} %all-gather.2.cloned.1.call-done.q_ref.refs_0_.refs_1_.refs_2_.refs_3_.refs_4_, bf16[2048,1152]{1,0:T(8,128)(2,1)} %gather_group.1.g_ref.refs_5_.refs_6_.refs_7_.refs_8_.refs_9_, ...), custom_call_target="tpu_custom_call" | custom-call | bytes 105000000 | tf_op jit(solution)/shard_map/memory_backward/pallas_call | solution.py:385
  407.6 82.2 %reduce_group.3 = f32[128,1024]{1,0:T(8,128)} custom-call(bf16[2048,1024]{1,0:T(8,128)(2,1)} %memory_backward.1.parts_ref), custom_call_target="tpu_custom_call" | custom-call | bytes 165000000 | tf_op jit(solution)/shard_map/reduce_group/pallas_call | solution.py:702
  490.5 6.2 %local_keys.1 = bf16[128,2048]{1,0:T(8,128)(2,1)} custom-call(s32[1]{0:T(128)} %bitcast.7.me_ref, f32[8,768]{1,0:T(8,128)} %pad.13.base_ref, s32[128,128]{1,0:T(8,128)} %broadcast_in_dim.24.column_ref, s32[8,640]{1,0:T(8,128)} %broadcast_in_dim.30.row_ref, bf16[128,3072]{1,0:T(8,128)(2,1)} %copy-done.2, f32[8]{0:T(128)} %get-tuple-element.56.ratio_ref, ...), custom_call_target="tpu_custom_call" | custom-call | bytes 45000000 | tf_op jit(solution)/shard_map/local_keys/pallas_call | solution.py:1026
  498.9 5.1 fusion.20
  505.8 2.7 convolution_convert_fusion.parts_ref
  508.4 8.4 %reduce-scatter.2.cloned.1.call-done.early_ref = bf16[64,4608]{1,0:T(8,128)(2,1)} async-done(((bf16[1024,4608]{1,0:T(8,128)(2,1)}), bf16[64,4608]{1,0:T(8,128)(2,1)}) %reduce-scatter.2.cloned.1.call-update) | async-done | bytes 589840 | tf_op jit(solution)/shard_map/reduce_scatter | solution.py:809
  516.9 44.2 %finish_grads.1 = (bf16[2,64,1536]{2,1,0:T(8,128)(2,1)}, bf16[2,64,4608]{2,1,0:T(8,128)(2,1)}, f32[24,128]{1,0:T(8,128)}) custom-call(bf16[1024,1536]{1,0:T(8,128)(2,1)} %convolution_convert_fusion.parts_ref, bf16[64,4608]{1,0:T(8,128)(2,1)} %reduce-scatter.2.cloned.1.call-done.early_ref, f32[24,128]{1,0:T(8,128)} %fusion.59.small_ref), custom_call_target="tpu_custom_call" | custom-call | bytes 135000000 | tf_op jit(solution)/shard_map/finish_grads/pallas_call | solution.py:1111
  563.0 1.5 convert_element_type.236
  (177 shorter events, 40.1 us)
Async XLA Ops:
  7.2 246.6 %copy-start = (bf16[1024,1024]{1,0:T(8,128)(2,1)S(1)}, bf16[1024,1024]{1,0:T(8,128)(2,1)}, u32[]{:S(2)}) copy-start(bf16[1024,1024]{1,0:T(8,128)(2,1)} %param.19) | copy-start | bytes 6291460
  7.2 139.2 %all-gather.2.cloned.1.call-start = ((), (), s32[]{:S(2)}) async-start(), calls=%async_computation.2 | async-start | bytes 4456448 | tf_op jit(solution)/shard_map/all_gather | solution.py:1200
  10.7 4.0 copy-start.8
  10.7 19.2 %copy-start.17 = (s32[128,8,32,1]{0,3,2,1:T(1,128)S(1)}, s32[128,8,32,1]{0,3,2,1:T(1,128)}, u32[]{:S(2)}) copy-start(s32[128,8,32,1]{0,3,2,1:T(1,128)} %param.28) | copy-start | bytes 393220
  10.7 19.2 %copy-start.18 = (s32[128,8,32]{0,2,1:T(8,128)S(1)}, s32[128,8,32]{0,2,1:T(8,128)}, u32[]{:S(2)}) copy-start(s32[128,8,32]{0,2,1:T(8,128)} %param.30) | copy-start | bytes 393220
  14.7 16.9 %copy-start.2 = (bf16[128,3072]{1,0:T(8,128)(2,1)}, bf16[128,3072]{1,0:T(8,128)(2,1)S(1)}, u32[]{:S(2)}) copy-start(bf16[128,3072]{1,0:T(8,128)(2,1)S(1)} %convolution_convert_fusion.3.own_ref) | copy-start | bytes 2359300
  16.3 122.1 %collective-permute-start.3 = (bf16[128,2048]{1,0:T(8,128)(2,1)}, bf16[128,2048]{1,0:T(8,128)(2,1)}, u32[]{:S(2)}, u32[]{:S(2)}) collective-permute-start(bf16[128,2048]{1,0:T(8,128)(2,1)} %slice.118), channel_id=1, source_target_pairs={{0,1},{1,2},{2,3},{3,4},{4,5},{5,6},{6,7},{7,8},{8,9},{9,10},{10,1... | collective-permute-start | bytes 1572872 | tf_op jit(solution)/shard_map/ppermute | solution.py:25
  19.4 119.0 %collective-permute-start.2 = (bf16[128,2048]{1,0:T(8,128)(2,1)}, bf16[128,2048]{1,0:T(8,128)(2,1)}, u32[]{:S(2)}, u32[]{:S(2)}) collective-permute-start(bf16[128,2048]{1,0:T(8,128)(2,1)} %slice.118), channel_id=1, source_target_pairs={{0,2},{1,3},{2,4},{3,5},{4,6},{5,7},{6,8},{7,9},{8,10},{9,11},{10,... | collective-permute-start | bytes 1572872 | tf_op jit(solution)/shard_map/ppermute | solution.py:25
  22.6 115.8 %collective-permute-start.1 = (bf16[128,2048]{1,0:T(8,128)(2,1)}, bf16[128,2048]{1,0:T(8,128)(2,1)}, u32[]{:S(2)}, u32[]{:S(2)}) collective-permute-start(bf16[128,2048]{1,0:T(8,128)(2,1)} %slice.118), channel_id=1, source_target_pairs={{0,3},{1,4},{2,5},{3,6},{4,7},{5,8},{6,9},{7,10},{8,11},{9,12},{10... | collective-permute-start | bytes 1572872 | tf_op jit(solution)/shard_map/ppermute | solution.py:25
  26.7 111.8 %collective-permute-start = (bf16[128,2048]{1,0:T(8,128)(2,1)}, bf16[128,2048]{1,0:T(8,128)(2,1)}, u32[]{:S(2)}, u32[]{:S(2)}) collective-permute-start(bf16[128,2048]{1,0:T(8,128)(2,1)} %slice.118), channel_id=1, source_target_pairs={{0,4},{1,5},{2,6},{3,7},{4,8},{5,9},{6,10},{7,11},{8,12},{9,13},{1... | collective-permute-start | bytes 1572872 | tf_op jit(solution)/shard_map/ppermute | solution.py:25
  30.0 30.1 %copy-start.37 = (s32[1,3]{1,0:T(1,128)S(1)}, s32[1,3]{1,0:T(1,128)}, u32[]{:S(2)}) copy-start(s32[1,3]{1,0:T(1,128)} %param.27) | copy-start | bytes 40
  30.0 30.3 %copy-start.38 = (f32[8]{0:T(128)S(1)}, f32[8]{0:T(128)}, u32[]{:S(2)}) copy-start(f32[8]{0:T(128)} %param.21) | copy-start | bytes 100
  30.0 31.0 %copy-start.36 = (f32[8,32]{1,0:T(8,128)S(1)}, f32[8,32]{1,0:T(8,128)}, u32[]{:S(2)}) copy-start(f32[8,32]{1,0:T(8,128)} %param.20) | copy-start | bytes 3076
  55.7 34.3 %all-to-all-start = ((s32[16,24,128]{2,1,0:T(8,128)}), s32[16,24,128]{2,1,0:T(8,128)S(1)}, u32[]{:S(2)}, u32[]{:S(2)}) async-start(s32[16,24,128]{2,1,0:T(8,128)} %make_lists.1), calls=%async_computation | async-start | bytes 393216 | tf_op jit(solution)/shard_map/all_to_all | solution.py:1192
  60.0 456.9 %reduce-scatter.2.cloned.1.call-start = ((), (), s32[]{:S(2)}) async-start(), calls=%async_computation.3 | async-start | bytes 10027008 | tf_op jit(solution)/shard_map/reduce_scatter | solution.py:809
  60.9 77.5 %copy-start.23 = (f32[8]{0:T(128)}, f32[8]{0:T(128)S(1)}, u32[]{:S(2)}) copy-start(f32[8]{0:T(128)S(1)} %get-tuple-element.57.share_ref) | copy-start | bytes 100
  61.0 77.3 %copy-start.31 = (s32[512]{0:T(512)}, s32[512]{0:T(512)S(1)}, u32[]{:S(2)}) copy-start(s32[512]{0:T(512)S(1)} %iota_select_fusion) | copy-start | bytes 6148
  188.4 63.3 %copy-start.12 = (f32[128,1024]{1,0:T(8,128)S(1)}, f32[128,1024]{1,0:T(8,128)}, u32[]{:S(2)}) copy-start(f32[128,1024]{1,0:T(8,128)} %get-tuple-element.36.loc_ref) | copy-start | bytes 1572868
  188.4 65.3 %copy-start.6 = (bf16[128,1024]{1,0:T(8,128)(2,1)S(1)}, bf16[128,1024]{1,0:T(8,128)(2,1)}, u32[]{:S(2)}) copy-start(bf16[128,1024]{1,0:T(8,128)(2,1)} %param.16) | copy-start | bytes 786436
  251.8 3.4 copy-start.5
  253.7 6.9 %slice-start.2 = ((s8[8388608]{0:T(1024)(128)(4,1)}), s8[4194304]{0:T(1024)(128)(4,1)S(1)}, s32[]{:S(2)}) async-start(s8[8388608]{0:T(1024)(128)(4,1)} %bitcast.54), calls=%async_computation.6 | async-start | bytes 8388608
  255.9 4.8 slice-start.3
  255.9 11.9 %slice-start = ((s8[8388608]{0:T(1024)(128)(4,1)}), s8[4194304]{0:T(1024)(128)(4,1)S(1)}, s32[]{:S(2)}) async-start(s8[8388608]{0:T(1024)(128)(4,1)} %bitcast.52), calls=%async_computation.4 | async-start | bytes 8388608
  260.7 7.1 %slice-start.1 = ((s8[8388608]{0:T(1024)(128)(4,1)}), s8[4194304]{0:T(1024)(128)(4,1)S(1)}, s32[]{:S(2)}) async-start(s8[8388608]{0:T(1024)(128)(4,1)} %bitcast.52), calls=%async_computation.5 | async-start | bytes 8388608
  267.8 5.5 copy-start.3
  274.1 23.9 %collective-permute-start.4 = (bf16[128,7680]{1,0:T(8,128)(2,1)}, bf16[128,7680]{1,0:T(8,128)(2,1)S(1)}, u32[]{:S(2)}, u32[]{:S(2)}) collective-permute-start(bf16[128,7680]{1,0:T(8,128)(2,1)} %get-tuple-element.78), channel_id=1, source_target_pairs={{0,16},{16,0},{1,17},{17,1},{2,18},{18,2},{3,19},{19,3},{4,20},{20... | collective-permute-start | bytes 5898248 | tf_op jit(solution)/shard_map/ppermute | solution.py:29
  490.4 6.2 %copy-start.11 = (f32[128,1024]{1,0:T(8,128)S(1)}, f32[128,1024]{1,0:T(8,128)}, u32[]{:S(2)}) copy-start(f32[128,1024]{1,0:T(8,128)} %reduce_group.3) | copy-start | bytes 1572868
  490.5 6.2 %copy-start.15 = (f32[128,1024]{1,0:T(8,128)S(1)}, f32[128,1024]{1,0:T(8,128)}, u32[]{:S(2)}) copy-start(f32[128,1024]{1,0:T(8,128)} %get-tuple-element.39) | copy-start | bytes 1572868
  498.1 6.5 %copy-start.34 = (f32[128]{0:T(128)S(1)}, f32[128]{0:T(128)}, u32[]{:S(2)}) copy-start(f32[128]{0:T(128)} %copy-done.33) | copy-start | bytes 1540
  498.1 6.5 %copy-start.29 = (f32[128]{0:T(128)S(1)}, f32[128]{0:T(128)}, u32[]{:S(2)}) copy-start(f32[128]{0:T(128)} %copy-done.28) | copy-start | bytes 1540
  498.2 7.6 %collective-permute-start.5 = (bf16[128,2560]{1,0:T(8,128)(2,1)S(1)}, bf16[128,2560]{1,0:T(8,128)(2,1)S(1)}, u32[]{:S(2)}, u32[]{:S(2)}) collective-permute-start(bf16[128,2560]{1,0:T(8,128)(2,1)S(1)} %pad_maximum_fusion.6), channel_id=1, source_target_pairs={{0,16},{16,0},{1,17},{17,1},{2,18},{18,2},{3,19},{19,3},{4,20},{20... | collective-permute-start | bytes 1966088 | tf_op jit(solution)/shard_map/ppermute | solution.py:29
  568.7 3.2 copy-start.1
  (20 other events, 31.2 us)
Sparse Core Ops, SparseCore 0:
  15.6 100.9 all-gather.1
  306.6 210.2 reduce-scatter.1

commit v6 on v5

--- a/solution.py
+++ b/solution.py
@@ -100,15 +100,10 @@
 def gather_rows(index, counts, memory_keys, memory_values, heads, sources, capacity):
     slots, width = memory_keys.shape
     head_dim = width // heads
-    step = 16
+    step, part = 128, 16
 
     def kernel(index_ref, counts_ref, keys, values, out_keys, out_values, key_table, value_table, key_rows, value_rows):
         i = pl.program_id(0)
-
-        @pl.when(i == 0)
-        def _():
-            key_rows[...] = jnp.zeros_like(key_rows)
-            value_rows[...] = jnp.zeros_like(value_rows)
 
         @pl.when(i < heads)
         def _():
@@ -120,16 +115,30 @@
         def _():
             source = i - heads
 
-            @pl.loop(0, (counts_ref[source] + step - 1) // step)
+            used = (counts_ref[source] + step - 1) // step
+
+            def store(group):
+                for at in range(0, step, part):
+                    here = pl.ds(pl.multiple_of(group * step, step) + at, part)
+                    out_keys[here, :] = key_rows[at : at + part, :].astype(jnp.bfloat16)
+                    out_values[here, :] = value_rows[at : at + part, :].astype(jnp.bfloat16)
+
+            @pl.loop(0, used)
             def _(group):
-                first = pl.multiple_of(group * step, step)
+                store(jnp.maximum(group - 1, 0))
+                first = source * capacity + group * step
                 for u in range(step):
-                    row = index_ref[source * capacity + first + u]
-                    key_rows[pl.ds(first + u, 1), :] = key_table[pl.ds(row, 1), :]
-                    value_rows[pl.ds(first + u, 1), :] = value_table[pl.ds(row, 1), :]
-
-            out_keys[...] = key_rows[...].astype(jnp.bfloat16)
-            out_values[...] = value_rows[...].astype(jnp.bfloat16)
+                    row = index_ref[first + u]
+                    key_rows[u : u + 1, :] = key_table[pl.ds(row, 1), :]
+                    value_rows[u : u + 1, :] = value_table[pl.ds(row, 1), :]
+
+            pl.when(used > 0)(lambda: store(used - 1))
+
+            @pl.loop(used, capacity // step)
+            def _(group):
+                here = pl.ds(pl.multiple_of(group * step, step), step)
+                out_keys[here, :] = jnp.zeros((step, head_dim), jnp.bfloat16)
+                out_values[here, :] = jnp.zeros((step, head_dim), jnp.bfloat16)
 
     table_spec = pl.BlockSpec((slots, head_dim), lambda i, *_: (0, jnp.minimum(i, heads - 1)))
     out_spec = pl.BlockSpec((capacity, head_dim), lambda i, *_: (jnp.maximum(i - heads, 0), 0))
@@ -144,8 +153,8 @@
             scratch_shapes=[
                 pltpu.VMEM((heads * slots, head_dim), jnp.float32),
                 pltpu.VMEM((heads * slots, head_dim), jnp.float32),
-                pltpu.VMEM((capacity, head_dim), jnp.float32),
-                pltpu.VMEM((capacity, head_dim), jnp.float32),
+                pltpu.VMEM((step, head_dim), jnp.float32),
+                pltpu.VMEM((step, head_dim), jnp.float32),
             ],
         ),
         out_shape=[out_shape, out_shape],
@@ -172,17 +181,30 @@
 def window_of(bounds, source, head, heads, span, capacity):
     first = bounds[source * (heads + 1) + head]
     last = bounds[source * (heads + 1) + head + 1]
-    start = jnp.minimum((first // 128) * 128, capacity - span)
-    extra = jnp.maximum(last - start - span + span - 1, 0) // span
+    start = jnp.minimum(first // 16 * 16, capacity - span)
+    extra = jnp.maximum(last - start - 1, 0) // span
     return start, extra
 
 
-def owned(id_ref, start, head, rows, span, least):
-    lines = id_ref[0, pl.ds(start // 128, span // 128), :]
-    token = lax.broadcasted_iota(jnp.int32, (rows, 128), 0) + head * rows
+def columns_of(head, head_dim):
+    if isinstance(head, int):
+        return slice(head * head_dim, (head + 1) * head_dim)
+    return pl.ds(pl.multiple_of(head * head_dim, head_dim), head_dim)
+
+
+def window_ids(id_ref, start, span):
+    lines = id_ref[0, pl.ds(start // 128, span // 128 + 1), :]
+    shift = start % 128
+    turned = pltpu.roll(lines, (128 - shift) % 128, 1)
+    lane = lax.broadcasted_iota(jnp.int32, (span // 128, 128), 1)
+    return jnp.where(lane < 128 - shift, turned[:-1], turned[1:])
+
+
+def owned(lines, first_row, count, start, least):
+    row = lax.broadcasted_iota(jnp.int32, (count, 128), 0) + first_row
     masks = []
-    for i in range(span // 128):
-        mask = lines[i : i + 1, :] == token
+    for i in range(lines.shape[0]):
+        mask = lines[i : i + 1, :] == row
         if least is not None:
             place = lax.broadcasted_iota(jnp.int32, (1, 128), 1) + start + i * 128
             mask = mask & (place >= least)
@@ -193,65 +215,71 @@
 def memory_forward(bounds, queries, key_rows, value_rows, row_ids, heads, sources, rows, score_scale):
     capacity, head_dim = key_rows.shape[0] // sources, key_rows.shape[1]
     width = heads * head_dim
-    span = min(512, capacity)
-
-    def kernel(bounds_ref, q_ref, k_ref, v_ref, id_ref, out_ref, sums, tops, totals):
+    span = min(384, capacity)
+    chunk = math.gcd(rows, 32)
+
+    def kernel(bounds_ref, q_ref, k_ref, v_ref, id_ref, out_ref, sums, tops, totals, raw, weights):
         source = pl.program_id(0)
-        lane = lax.broadcasted_iota(jnp.int32, (rows, 128), 1) % 16
-
-        def scores_of(head, start, least):
-            here = pl.ds(pl.multiple_of(start, 128), span)
-            mine = owned(id_ref, start, head, rows, span, least)
-            q = q_ref[:, head * head_dim : (head + 1) * head_dim]
-            raw = lax.dot_general(q, k_ref[here, :], contract_cols, preferred_element_type=jnp.float32)
-            return jnp.where(mine, raw * score_scale, masked_score), mine, v_ref[here, :]
-
-        windows = [window_of(bounds_ref, source, head, heads, span, capacity) for head in range(heads)]
-        top_tile = jnp.zeros((rows, 128), jnp.float32)
-        total_tile = jnp.zeros((rows, 128), jnp.float32)
-        for head in range(heads):
-            scores, mine, v = scores_of(head, windows[head][0], None)
-            top = jnp.max(scores, axis=1, keepdims=True)
-            weights = jnp.where(mine, jnp.exp(scores - top), 0.0)
-            sums[:, head * head_dim : (head + 1) * head_dim] = jnp.dot(
-                weights.astype(jnp.bfloat16), v, preferred_element_type=jnp.float32
-            )
-            top_tile = jnp.where(lane == head, top, top_tile)
-            total_tile = jnp.where(
-                lane == heads + head, jnp.sum(weights, axis=1, keepdims=True), total_tile
-            )
-        tops[...] = top_tile
-        totals[...] = total_tile
-        more = sum(extra for _, extra in windows)
-
-        @pl.when(more > 0)
-        def _():
-            for head in range(heads):
-                start, extra = windows[head]
-                columns = slice(head * head_dim, (head + 1) * head_dim)
-
-                @pl.loop(0, extra)
-                def _(turn):
-                    least = start + (turn + 1) * span
-                    scores, mine, v = scores_of(head, jnp.minimum(least, capacity - span), least)
-                    old_top = jnp.max(
-                        jnp.where(lane == head, tops[...], masked_score), axis=1, keepdims=True
-                    )
-                    top = jnp.maximum(old_top, jnp.max(scores, axis=1, keepdims=True))
-                    weights = jnp.where(mine, jnp.exp(scores - top), 0.0)
-                    faded = jnp.exp(old_top - top)
-                    sums[:, columns] = sums[:, columns] * faded + jnp.dot(
-                        weights.astype(jnp.bfloat16), v, preferred_element_type=jnp.float32
-                    )
-                    tops[...] = jnp.where(lane == head, top, tops[...])
-                    totals[...] = jnp.where(
-                        lane == heads + head,
-                        totals[...] * faded + jnp.sum(weights, axis=1, keepdims=True),
-                        totals[...],
-                    )
+        lane = lax.broadcasted_iota(jnp.int32, (chunk, 128), 1) % 16
+
+        def window(heads_here, starts, least):
+            here = [pl.ds(pl.multiple_of(start, 16), span) for start in starts]
+            columns = [columns_of(head, head_dim) for head in heads_here]
+            for slot in range(len(starts)):
+                raw[slot] = lax.dot_general(
+                    q_ref[:, columns[slot]],
+                    k_ref[here[slot], :],
+                    contract_cols,
+                    preferred_element_type=jnp.float32,
+                )
+            for slot, (head, start) in enumerate(zip(heads_here, starts)):
+                lines = window_ids(id_ref, start, span)
+                for at in range(0, rows, chunk):
+                    some = slice(at, at + chunk)
+                    mine = owned(lines, head * rows + at, chunk, start, least)
+                    scores = jnp.where(mine, raw[slot, some, :], masked_score)
+                    top = jnp.maximum(jnp.max(scores, axis=1, keepdims=True), 0.1 * masked_score)
+                    if least is not None:
+                        old_top = jnp.max(
+                            jnp.where(lane == head, tops[some, :], masked_score), axis=1, keepdims=True
+                        )
+                        top = jnp.maximum(top, old_top)
+                    exps = jnp.exp((scores - top) * score_scale)
+                    weights[slot, some, :] = exps.astype(jnp.bfloat16)
+                    total = jnp.sum(exps, axis=1, keepdims=True)
+                    if least is not None:
+                        faded = jnp.exp((old_top - top) * score_scale)
+                        sums[some, columns[slot]] = sums[some, columns[slot]] * faded
+                        total = total + totals[some, :] * faded
+                    tops[some, :] = jnp.where(lane == head, top, tops[some, :])
+                    totals[some, :] = jnp.where(lane == heads + head, total, totals[some, :])
+            for slot in range(len(starts)):
+                found = jnp.dot(
+                    weights[slot], v_ref[here[slot], :], preferred_element_type=jnp.float32
+                )
+                sums[:, columns[slot]] = found if least is None else sums[:, columns[slot]] + found
+
+        tops[...] = jnp.zeros_like(tops)
+        totals[...] = jnp.zeros_like(totals)
+
+        window(
+            list(range(heads)),
+            [window_of(bounds_ref, source, head, heads, span, capacity)[0] for head in range(heads)],
+            None,
+        )
+
+        @pl.loop(0, heads)
+        def _(head):
+            start, extra = window_of(bounds_ref, source, head, heads, span, capacity)
+
+            @pl.loop(0, extra)
+            def _(turn):
+                least = start + (turn + 1) * span
+                window([head], [jnp.minimum(least, capacity - span)], least)
 
         out_ref[:, :width] = sums[...].astype(jnp.bfloat16)
-        out_ref[:, width:] = triple(jnp.where(lane < heads, tops[...], totals[...]))
+        wide = lax.broadcasted_iota(jnp.int32, (rows, 128), 1) % 16
+        out_ref[:, width:] = triple(jnp.where(wide < heads, tops[...] * score_scale, totals[...]))
 
     return pl.pallas_call(
         kernel,
@@ -262,18 +290,20 @@
                 pl.BlockSpec((rows, width), lambda i, *_: (i, 0)),
                 pl.BlockSpec((capacity, head_dim), lambda i, *_: (i, 0)),
                 pl.BlockSpec((capacity, head_dim), lambda i, *_: (i, 0)),
-                pl.BlockSpec((1, capacity // 128, 128), lambda i, *_: (i, 0, 0)),
+                pl.BlockSpec((1, *row_ids.shape[1:]), lambda i, *_: (i, 0, 0)),
             ],
             out_specs=pl.BlockSpec((rows, width + 128), lambda i, *_: (i, 0)),
             scratch_shapes=[
                 pltpu.VMEM((rows, width), jnp.float32),
                 pltpu.VMEM((rows, 128), jnp.float32),
                 pltpu.VMEM((rows, 128), jnp.float32),
+                pltpu.VMEM((heads, rows, span), jnp.float32),
+                pltpu.VMEM((heads, rows, span), jnp.bfloat16),
             ],
         ),
         out_shape=jax.ShapeDtypeStruct((sources * rows, width + 128), jnp.bfloat16),
         compiler_params=pltpu.CompilerParams(vmem_limit_bytes=VMEM_LIMIT),
-        cost_estimate=lasting(41),
+        cost_estimate=lasting(25),
         name="memory_forward",
     )(bounds, queries, key_rows, value_rows, row_ids)
 
@@ -340,45 +370,64 @@
 def memory_backward(bounds, queries, grads, key_rows, value_rows, row_ids, heads, sources, rows, score_scale):
     capacity, head_dim = key_rows.shape[0] // sources, key_rows.shape[1]
     width = heads * head_dim
-    span = min(512, capacity)
-
-    def kernel(bounds_ref, q_ref, g_ref, k_ref, v_ref, id_ref, out_ref, sums):
+    span = min(384, capacity)
+    chunk = math.gcd(rows, 32)
+
+    def kernel(bounds_ref, q_ref, g_ref, k_ref, v_ref, id_ref, out_ref, sums, stats, raw, products, slopes):
         source = pl.program_id(0)
-        stat = joined_tile(g_ref[:, width : width + 128])
-
-        def term(column):
-            return stat[:, column : column + 1]
-
-        def part_of(head, start, least):
-            here = pl.ds(pl.multiple_of(start, 128), span)
-            columns = slice(head * head_dim, (head + 1) * head_dim)
-            mine = owned(id_ref, start, head, rows, span, least)
-            k, v = k_ref[here, :], v_ref[here, :]
-            raw = lax.dot_general(
-                q_ref[:, columns], k, contract_cols, preferred_element_type=jnp.float32
-            )
-            products = lax.dot_general(
-                g_ref[:, columns], v, contract_cols, preferred_element_type=jnp.float32
-            )
-            probs = jnp.exp(jnp.where(mine, raw * score_scale - term(head), dead_score))
-            slopes = (probs * (products - term(heads + head))).astype(jnp.bfloat16)
-            return jnp.dot(slopes, k, preferred_element_type=jnp.float32)
-
-        windows = [window_of(bounds_ref, source, head, heads, span, capacity) for head in range(heads)]
-        for head in range(heads):
-            sums[:, head * head_dim : (head + 1) * head_dim] = part_of(head, windows[head][0], None)
-        more = sum(extra for _, extra in windows)
-
-        @pl.when(more > 0)
-        def _():
-            for head in range(heads):
-                start, extra = windows[head]
-                columns = slice(head * head_dim, (head + 1) * head_dim)
-
-                @pl.loop(0, extra)
-                def _(turn):
-                    least = start + (turn + 1) * span
-                    sums[:, columns] += part_of(head, jnp.minimum(least, capacity - span), least)
+        stats[...] = joined_tile(g_ref[:, width : width + 128])
+
+        def window(heads_here, starts, least):
+            here = [pl.ds(pl.multiple_of(start, 16), span) for start in starts]
+            columns = [columns_of(head, head_dim) for head in heads_here]
+            for slot in range(len(starts)):
+                raw[slot] = lax.dot_general(
+                    q_ref[:, columns[slot]],
+                    k_ref[here[slot], :],
+                    contract_cols,
+                    preferred_element_type=jnp.float32,
+                )
+                products[slot] = lax.dot_general(
+                    g_ref[:, columns[slot]],
+                    v_ref[here[slot], :],
+                    contract_cols,
+                    preferred_element_type=jnp.float32,
+                )
+            for slot, (head, start) in enumerate(zip(heads_here, starts)):
+                lines = window_ids(id_ref, start, span)
+                turned = stats[...]
+                if least is not None:
+                    turned = pltpu.roll(turned, 128 - head, 1)
+                elif head:
+                    turned = turned[:, head:]
+                for at in range(0, rows, chunk):
+                    some = slice(at, at + chunk)
+                    mine = owned(lines, head * rows + at, chunk, start, least)
+                    log, delta = turned[some, :1], turned[some, heads : heads + 1]
+                    probs = jnp.exp(jnp.where(mine, raw[slot, some, :] * score_scale - log, dead_score))
+                    slopes[slot, some, :] = (probs * (products[slot, some, :] - delta)).astype(
+                        jnp.bfloat16
+                    )
+            for slot in range(len(starts)):
+                found = jnp.dot(
+                    slopes[slot], k_ref[here[slot], :], preferred_element_type=jnp.float32
+                )
+                sums[:, columns[slot]] = found if least is None else sums[:, columns[slot]] + found
+
+        window(
+            list(range(heads)),
+            [window_of(bounds_ref, source, head, heads, span, capacity)[0] for head in range(heads)],
+            None,
+        )
+
+        @pl.loop(0, heads)
+        def _(head):
+            start, extra = window_of(bounds_ref, source, head, heads, span, capacity)
+
+            @pl.loop(0, extra)
+            def _(turn):
+                least = start + (turn + 1) * span
+                window([head], [jnp.minimum(least, capacity - span)], least)
 
         out_ref[...] = sums[...].astype(jnp.bfloat16)
 
@@ -392,14 +441,20 @@
                 pl.BlockSpec((rows, width + 128), lambda i, *_: (i, 0)),
                 pl.BlockSpec((capacity, head_dim), lambda i, *_: (i, 0)),
                 pl.BlockSpec((capacity, head_dim), lambda i, *_: (i, 0)),
-                pl.BlockSpec((1, capacity // 128, 128), lambda i, *_: (i, 0, 0)),
+                pl.BlockSpec((1, *row_ids.shape[1:]), lambda i, *_: (i, 0, 0)),
             ],
             out_specs=pl.BlockSpec((rows, width), lambda i, *_: (i, 0)),
-            scratch_shapes=[pltpu.VMEM((rows, width), jnp.float32)],
+            scratch_shapes=[
+                pltpu.VMEM((rows, width), jnp.float32),
+                pltpu.VMEM((rows, 128), jnp.float32),
+                pltpu.VMEM((heads, rows, span), jnp.float32),
+                pltpu.VMEM((heads, rows, span), jnp.float32),
+                pltpu.VMEM((heads, rows, span), jnp.bfloat16),
+            ],
         ),
         out_shape=jax.ShapeDtypeStruct((sources * rows, width), jnp.bfloat16),
         compiler_params=pltpu.CompilerParams(vmem_limit_bytes=VMEM_LIMIT),
-        cost_estimate=lasting(35),
+        cost_estimate=lasting(25),
         name="memory_backward",
     )(bounds, queries, grads, key_rows, value_rows, row_ids)
 
@@ -1181,29 +1236,29 @@
     projected = jnp.dot(normed_in, qkv_weight, preferred_element_type=jnp.float32).astype(
         jnp.bfloat16
     )
-    halos = [
-        passed_along(projected[:, width:], "mem", distance) for distance in range(repeats, 0, -1)
-    ]
-    local_out, local_log = local_forward(
-        before_bias, own_book, key_book, projected, halos, heads, score_scale
-    )
     slots = memory_keys.shape[0]
     requests = place_requests(slot_shard, slot_index, slot_live, groups, capacity, slots)
     incoming = lax.all_to_all(requests, "mem", split_axis=0, concat_axis=0, tiled=True)
+    keys_values, _ = lax.optimization_barrier((projected[:, width:], requests))
+    halos = [passed_along(keys_values, "mem", distance) for distance in range(repeats, 0, -1)]
     row_ids = incoming // slots
     limits = jnp.arange(heads + 1, dtype=jnp.int32) * (rows * slots)
     bounds = jnp.sum((incoming[:, None] < limits[None, :, None, None]).astype(jnp.int32), axis=(2, 3))
     index = jnp.where(row_ids < heads * rows, row_ids // rows * slots + incoming % slots, 0)
+    padded_ids = jnp.pad(row_ids, ((0, 0), (0, 1), (0, 0)), constant_values=heads * rows)
     key_rows, value_rows = gather_rows(
         index.reshape(-1), bounds[:, heads], memory_keys, memory_values, heads, groups, capacity
     )
     all_queries = lax.all_gather(projected[:, :width], "mem", axis=0, tiled=True)
+    local_out, local_log = local_forward(
+        before_bias, own_book, key_book, projected, halos, heads, score_scale
+    )
     partial = memory_forward(
         bounds.reshape(-1),
         all_queries,
         key_rows,
         value_rows,
-        row_ids,
+        padded_ids,
         heads,
         groups,
         rows,
@@ -1272,7 +1327,7 @@
         all_grads,
         key_rows,
         value_rows,
-        row_ids,
+        padded_ids,
         heads,
         groups,
         rows,

time: 589 us -> 547 us (0.929)
  waiting for transfers between devices: 36.2 us -> 12.6 us
  starting transfers between devices: 33.9 us -> 21.2 us
  Pallas kernels: 390 us -> 382 us
    all_to_all x1, waiting for transfers between devices: 27.7 us -> 0.01 us  [on_device(): lax.all_to_all(requests, 'mem', split_axis=0, concat_axis=0, tiled=True)]
    pallas_call x1, Pallas kernels: 42 us -> 26.6 us  [memory_forward(): pl.pallas_call(kernel, grid_spec=pltpu.PrefetchScalarGridSpec(num_scalar_...]
    ppermute x2, starting transfers between devices: 16 us -> 1.23 us  [swapped(): return lax.ppermute(value, 'dp', [(0, 1), (1, 0)])]
    pallas_call x1, Pallas kernels: 43.2 us -> 56 us  [gather_rows(): pl.pallas_call(kernel, grid_spec=pltpu.PrefetchScalarGridSpec(num_scalar_...]
    pallas_call x1, Pallas kernels: 35.5 us -> 27.3 us  [memory_backward(): pl.pallas_call(kernel, grid_spec=pltpu.PrefetchScalarGridSpec(num_scalar_...]
  transfers between devices with their start and end apart: 9 -> 9, of which waited for: 2 -> 1; matrix products, arithmetic and copies ran while one was open for 9% -> 10% of each run, Pallas kernels for 42% -> 47%
where the time goes in v6:
time: 547 us; the launch traced here: 536 us
  Pallas kernels  382 us (70%)
  other arithmetic  44 us (8%)
  matrix products  39.1 us (7%)
  local copies, waits for them, and re-layouts  22 us (4%)
  starting transfers between devices  21.2 us (4%)
  between operations  15.2 us (3%)
  waiting for transfers between devices  12.6 us (2%)
    pallas_call x2, Pallas kernels, reduce_group(): pl.pallas_call(kernel, in_specs=[pl.BlockSpec(memory_space=pltpu.VMEM)],...  149 us
    pallas_call x1, Pallas kernels, gather_group(): pl.pallas_call(kernel, in_specs=[pl.BlockSpec(memory_space=pl.ANY)], out_...  56.4 us
    pallas_call x1, Pallas kernels, gather_rows(): pl.pallas_call(kernel, grid_spec=pltpu.PrefetchScalarGridSpec(num_scalar_...  56 us
    pallas_call x1, Pallas kernels, finish_grads(): pl.pallas_call(kernel, in_specs=[vmem] * 3, out_specs=[vmem] * 3, out_sha...  44.5 us
    pallas_call x1, Pallas kernels, memory_backward(): pl.pallas_call(kernel, grid_spec=pltpu.PrefetchScalarGridSpec(num_scalar_...  27.3 us
    pallas_call x1, Pallas kernels, memory_forward(): pl.pallas_call(kernel, grid_spec=pltpu.PrefetchScalarGridSpec(num_scalar_...  26.6 us
    sort x1, other arithmetic, place_requests(): lax.sort(((owner * entries + place).reshape(-1), slot_index.reshape(-1)),...  18.5 us
    ppermute x4, starting transfers between devices, passed_along(): return lax.ppermute(value, axis, pairs)  13.3 us
  transfers between devices with their start and end apart: 9, of which 1 were waited for; matrix products, arithmetic and copies ran while one was open for 10% of the time, Pallas kernels for 47%

profile of v6, /device:TPU:9, one launch (start us, length us, event | category | flops | bytes accessed | tf_op | source)
XLA Modules:
  0.0 536.2 jit_solution(1894327202895272939)
XLA Ops:
  10.7 3.9 convolution_convert_fusion.3.own_ref
  18.0 18.5 %sort.23 = (s32[32768]{0:T(1024)S(1)}, s32[32768]{0:T(1024)S(1)}, s32[32768]{0:T(1024)}) sort(s32[32768]{0:T(1024)S(1)} %reshape.246, s32[32768]{0:T(1024)} %reshape.247, s32[32768]{0:T(1024)S(1)} %iota.53), dimensions={0}, to_apply=%region_0.0 | sort | flops 491520 | bytes 786432 | tf_op jit(solution)/shard_map/sort | solution.py:61
  38.4 2.8 make_lists.1
  41.3 6.7 %all-to-all-start = ((s32[16,24,128]{2,1,0:T(8,128)}), s32[16,24,128]{2,1,0:T(8,128)S(1)}, u32[]{:S(2)}, u32[]{:S(2)}) async-start(s32[16,24,128]{2,1,0:T(8,128)} %make_lists.1), calls=%async_computation | async-start | bytes 393216 | tf_op jit(solution)/shard_map/all_to_all | solution.py:1241
  48.8 3.1 collective-permute-start.3
  51.9 3.1 collective-permute-start.2
  55.0 4.0 collective-permute-start.1
  59.0 3.1 collective-permute-start
  65.1 2.7 convert_reduce_fusion.1
  70.9 56.0 %gather_rows.1 = (bf16[49152,128]{1,0:T(8,128)(2,1)}, bf16[49152,128]{1,0:T(8,128)(2,1)}) custom-call(s32[49152]{0:T(1024)} %bitcast.56, s32[16]{0:T(128)} %slice_reduce_fusion.counts_ref, bf16[4096,1024]{1,0:T(8,128)(2,1)} %keys.1, bf16[4096,1024]{1,0:T(8,128)(2,1)} %values.1), custom_call_target="tpu_custom_call" | custom-call | bytes 126000000 | tf_op jit(solution)/shard_map/gather_rows/pallas_call | solution.py:146
  128.4 6.7 %local_forward.1 = (f32[128,1024]{1,0:T(8,128)}, f32[128,128]{1,0:T(8,128)}) custom-call(f32[8,768]{1,0:T(8,128)} %pad.17.base_ref, s32[128,128]{1,0:T(8,128)} %broadcast_in_dim.24.column_ref, s32[8,640]{1,0:T(8,128)} %broadcast_in_dim.26.row_ref, bf16[128,3072]{1,0:T(8,128)(2,1)} %copy-done.2, bf16[128,2048]{1,0:T(8,128)(2,1)} %collective-permute-done.refs_0_, ...), custom_call_target="tpu_custom_call" | custom-call | bytes 30000000 | tf_op jit(solution)/shard_map/local_forward/pallas_call | solution.py:940
  135.0 26.6 %memory_forward.1.parts_ref = bf16[2048,1152]{1,0:T(8,128)(2,1)} custom-call(s32[144]{0:T(256)} %reshape.249.bounds_ref, bf16[2048,1024]{1,0:T(8,128)(2,1)} %all-gather.2.cloned.1.call-done.q_ref.refs_0_.refs_1_.refs_2_.refs_3_.refs_4_, bf16[49152,128]{1,0:T(8,128)(2,1)} %get-tuple-element.34.k_ref, bf16[49152,128]{1,0:T(8,128)(2,1)} %get-tuple-element.35.v_ref, ...), custom_call_target="tpu_custom_call" | custom-call | bytes 75000000 | tf_op jit(solution)/shard_map/memory_forward/pallas_call | solution.py:284
  161.6 59.4 %reduce_group.2 = (f32[128,1024]{1,0:T(8,128)}, f32[128,128]{1,0:T(8,128)}) custom-call(bf16[2048,1152]{1,0:T(8,128)(2,1)} %memory_forward.1.parts_ref), custom_call_target="tpu_custom_call" | custom-call | bytes 165000000 | tf_op jit(solution)/shard_map/reduce_group/pallas_call | solution.py:757
  221.1 1.9 constant_dynamic-update-slice_fusion.2
  225.2 4.8 fusion.71
  230.0 6.8 %add_convert_fusion = (bf16[128,4096]{1,0:T(8,128)(2,1)S(1)}, f32[128,4096]{1,0:T(8,128)S(1)}) fusion(f32[128,4096]{1,0:T(8,128)S(1)} %fusion.71, bf16[128,1024]{1,0:T(8,128)(2,1)S(1)} %copy-done.5, bf16[1024,4096]{1,0:T(8,128)(2,1)S(1)} %bitcast.55), kind=kOutput, calls=%fused_computation.7 | convolution fusion | flops 1111490560 | bytes 13893632 | tf_op jit(solution)/shard_map/dot_general | solution.py:1291
  237.1 3.0 multiply_reduce_fusion
  243.9 1.6 fusion.72.mix_ref
  245.5 7.0 %local_queries.1 = (f32[128,1024]{1,0:T(8,128)}, f32[8,768]{1,0:T(8,128)}, f32[8,128]{1,0:T(8,128)}, bf16[128,1152]{1,0:T(8,128)(2,1)}) custom-call(f32[8,768]{1,0:T(8,128)} %pad.17.base_ref, s32[128,128]{1,0:T(8,128)} %broadcast_in_dim.24.column_ref, s32[8,640]{1,0:T(8,128)} %broadcast_in_dim.26.row_ref, bf16[128,3072]{1,0:T(8,128)(2,1)} %copy-done.2, ...), custom_call_target="tpu_custom_call" | custom-call | bytes 45000000 | tf_op jit(solution)/shard_map/local_queries/pallas_call | solution.py:1017
  253.2 1.3 convolution_convert_fusion.2
  255.8 4.7 pad_maximum_fusion
  262.4 7.0 %fusion.6 = bf16[128,1024]{1,0:T(8,128)(2,1)} fusion(f32[128,1024]{1,0:T(8,128)S(1)} %get-tuple-element.92, bf16[128,4096]{1,0:T(8,128)(2,1)S(1)} %copy-done.4, bf16[1024,4096]{1,0:T(8,128)(2,1)} %param.24), kind=kOutput, calls=%fused_computation.27 | convolution fusion | flops 1074003968 | bytes 10223616 | tf_op jit(solution)/shard_map/dot_general | solution.py:1287
  269.4 56.4 %gather_group.1.g_ref.refs_5_.refs_6_.refs_7_.refs_8_.refs_9_ = bf16[2048,1152]{1,0:T(8,128)(2,1)} custom-call(bf16[128,1152]{1,0:T(8,128)(2,1)} %get-tuple-element.43.x_ref), custom_call_target="tpu_custom_call" | custom-call | bytes 150000000 | tf_op jit(solution)/shard_map/gather_group/pallas_call | solution.py:633
  325.8 27.3 %memory_backward.1.parts_ref = bf16[2048,1024]{1,0:T(8,128)(2,1)} custom-call(s32[144]{0:T(256)} %reshape.249.bounds_ref, bf16[2048,1024]{1,0:T(8,128)(2,1)} %all-gather.2.cloned.1.call-done.q_ref.refs_0_.refs_1_.refs_2_.refs_3_.refs_4_, bf16[2048,1152]{1,0:T(8,128)(2,1)} %gather_group.1.g_ref.refs_5_.refs_6_.refs_7_.refs_8_.refs_9_, ...), custom_call_target="tpu_custom_call" | custom-call | bytes 75000000 | tf_op jit(solution)/shard_map/memory_backward/pallas_call | solution.py:434
  353.1 89.4 %reduce_group.3 = f32[128,1024]{1,0:T(8,128)} custom-call(bf16[2048,1024]{1,0:T(8,128)(2,1)} %memory_backward.1.parts_ref), custom_call_target="tpu_custom_call" | custom-call | bytes 165000000 | tf_op jit(solution)/shard_map/reduce_group/pallas_call | solution.py:757
  443.1 6.1 %local_keys.1 = bf16[128,2048]{1,0:T(8,128)(2,1)} custom-call(s32[1]{0:T(128)} %bitcast.7.me_ref, f32[8,768]{1,0:T(8,128)} %pad.18.base_ref, s32[128,128]{1,0:T(8,128)} %broadcast_in_dim.24.column_ref, s32[8,640]{1,0:T(8,128)} %broadcast_in_dim.30.row_ref, bf16[128,3072]{1,0:T(8,128)(2,1)} %copy-done.2, f32[8]{0:T(128)} %get-tuple-element.58.ratio_ref, ...), custom_call_target="tpu_custom_call" | custom-call | bytes 45000000 | tf_op jit(solution)/shard_map/local_keys/pallas_call | solution.py:1081
  449.4 1.3 fusion.38
  451.5 5.1 fusion.20
  458.4 2.7 convolution_convert_fusion.parts_ref
  461.1 12.6 %reduce-scatter.2.cloned.1.call-done.early_ref = bf16[64,4608]{1,0:T(8,128)(2,1)} async-done(((bf16[1024,4608]{1,0:T(8,128)(2,1)}), bf16[64,4608]{1,0:T(8,128)(2,1)}) %reduce-scatter.2.cloned.1.call-update) | async-done | bytes 589840 | tf_op jit(solution)/shard_map/reduce_scatter | solution.py:864
  473.7 44.5 %finish_grads.1 = (bf16[2,64,1536]{2,1,0:T(8,128)(2,1)}, bf16[2,64,4608]{2,1,0:T(8,128)(2,1)}, f32[24,128]{1,0:T(8,128)}) custom-call(bf16[1024,1536]{1,0:T(8,128)(2,1)} %convolution_convert_fusion.parts_ref, bf16[64,4608]{1,0:T(8,128)(2,1)} %reduce-scatter.2.cloned.1.call-done.early_ref, f32[24,128]{1,0:T(8,128)} %fusion.59.small_ref), custom_call_target="tpu_custom_call" | custom-call | bytes 135000000 | tf_op jit(solution)/shard_map/finish_grads/pallas_call | solution.py:1166
  520.1 1.5 convert_element_type.236
  (182 shorter events, 39.5 us)
Async XLA Ops:
  7.2 215.8 %copy-start = (bf16[1024,1024]{1,0:T(8,128)(2,1)S(1)}, bf16[1024,1024]{1,0:T(8,128)(2,1)}, u32[]{:S(2)}) copy-start(bf16[1024,1024]{1,0:T(8,128)(2,1)} %param.19) | copy-start | bytes 6291460
  7.2 127.8 %all-gather.2.cloned.1.call-start = ((), (), s32[]{:S(2)}) async-start(), calls=%async_computation.2 | async-start | bytes 4456448 | tf_op jit(solution)/shard_map/all_gather | solution.py:1252
  10.7 4.0 copy-start.8
  10.7 4.8 copy-start.19
  10.7 4.8 copy-start.20
  14.6 33.3 %copy-start.2 = (bf16[128,3072]{1,0:T(8,128)(2,1)}, bf16[128,3072]{1,0:T(8,128)(2,1)S(1)}, u32[]{:S(2)}) copy-start(bf16[128,3072]{1,0:T(8,128)(2,1)S(1)} %convolution_convert_fusion.3.own_ref) | copy-start | bytes 2359300
  15.9 46.2 %copy-start.39 = (s32[1,3]{1,0:T(1,128)S(1)}, s32[1,3]{1,0:T(1,128)}, u32[]{:S(2)}) copy-start(s32[1,3]{1,0:T(1,128)} %param.27) | copy-start | bytes 40
  16.0 46.4 %copy-start.40 = (f32[8]{0:T(128)S(1)}, f32[8]{0:T(128)}, u32[]{:S(2)}) copy-start(f32[8]{0:T(128)} %param.21) | copy-start | bytes 100
  16.0 47.6 %copy-start.38 = (f32[8,32]{1,0:T(8,128)S(1)}, f32[8,32]{1,0:T(8,128)}, u32[]{:S(2)}) copy-start(f32[8,32]{1,0:T(8,128)} %param.20) | copy-start | bytes 3076
  41.3 23.9 %all-to-all-start = ((s32[16,24,128]{2,1,0:T(8,128)}), s32[16,24,128]{2,1,0:T(8,128)S(1)}, u32[]{:S(2)}, u32[]{:S(2)}) async-start(s32[16,24,128]{2,1,0:T(8,128)} %make_lists.1), calls=%async_computation | async-start | bytes 393216 | tf_op jit(solution)/shard_map/all_to_all | solution.py:1241
  47.9 425.7 %reduce-scatter.2.cloned.1.call-start = ((), (), s32[]{:S(2)}) async-start(), calls=%async_computation.3 | async-start | bytes 10027008 | tf_op jit(solution)/shard_map/reduce_scatter | solution.py:864
  48.8 78.1 %collective-permute-start.3 = (bf16[128,2048]{1,0:T(8,128)(2,1)}, bf16[128,2048]{1,0:T(8,128)(2,1)S(1)}, u32[]{:S(2)}, u32[]{:S(2)}) collective-permute-start(bf16[128,2048]{1,0:T(8,128)(2,1)} %slice.115), channel_id=1, source_target_pairs={{0,1},{1,2},{2,3},{3,4},{4,5},{5,6},{6,7},{7,8},{8,9},{9,10},{10,1... | collective-permute-start | bytes 1572872 | tf_op jit(solution)/shard_map/ppermute | solution.py:25
  51.9 75.0 %collective-permute-start.2 = (bf16[128,2048]{1,0:T(8,128)(2,1)}, bf16[128,2048]{1,0:T(8,128)(2,1)S(1)}, u32[]{:S(2)}, u32[]{:S(2)}) collective-permute-start(bf16[128,2048]{1,0:T(8,128)(2,1)} %slice.115), channel_id=1, source_target_pairs={{0,2},{1,3},{2,4},{3,5},{4,6},{5,7},{6,8},{7,9},{8,10},{9,11},{10,... | collective-permute-start | bytes 1572872 | tf_op jit(solution)/shard_map/ppermute | solution.py:25
  55.0 71.9 %collective-permute-start.1 = (bf16[128,2048]{1,0:T(8,128)(2,1)}, bf16[128,2048]{1,0:T(8,128)(2,1)}, u32[]{:S(2)}, u32[]{:S(2)}) collective-permute-start(bf16[128,2048]{1,0:T(8,128)(2,1)} %slice.115), channel_id=1, source_target_pairs={{0,3},{1,4},{2,5},{3,6},{4,7},{5,8},{6,9},{7,10},{8,11},{9,12},{10... | collective-permute-start | bytes 1572872 | tf_op jit(solution)/shard_map/ppermute | solution.py:25
  59.0 67.9 %collective-permute-start = (bf16[128,2048]{1,0:T(8,128)(2,1)}, bf16[128,2048]{1,0:T(8,128)(2,1)}, u32[]{:S(2)}, u32[]{:S(2)}) collective-permute-start(bf16[128,2048]{1,0:T(8,128)(2,1)} %slice.115), channel_id=1, source_target_pairs={{0,4},{1,5},{2,6},{3,7},{4,8},{5,9},{6,10},{7,11},{8,12},{9,13},{1... | collective-permute-start | bytes 1572872 | tf_op jit(solution)/shard_map/ppermute | solution.py:25
  161.6 59.4 %copy-start.12 = (f32[128,1024]{1,0:T(8,128)S(1)}, f32[128,1024]{1,0:T(8,128)}, u32[]{:S(2)}) copy-start(f32[128,1024]{1,0:T(8,128)} %get-tuple-element.38.loc_ref) | copy-start | bytes 1572868
  161.6 61.3 %copy-start.6 = (bf16[128,1024]{1,0:T(8,128)(2,1)S(1)}, bf16[128,1024]{1,0:T(8,128)(2,1)}, u32[]{:S(2)}) copy-start(bf16[128,1024]{1,0:T(8,128)(2,1)} %param.16) | copy-start | bytes 786436
  221.0 2.5 copy-start.21
  221.0 3.4 copy-start.5
  223.0 7.0 %slice-start.2 = ((s8[8388608]{0:T(1024)(128)(4,1)}), s8[4194304]{0:T(1024)(128)(4,1)S(1)}, s32[]{:S(2)}) async-start(s8[8388608]{0:T(1024)(128)(4,1)} %bitcast.54), calls=%async_computation.6 | async-start | bytes 8388608
  225.1 4.8 slice-start.3
  225.1 11.9 %slice-start = ((s8[8388608]{0:T(1024)(128)(4,1)}), s8[4194304]{0:T(1024)(128)(4,1)S(1)}, s32[]{:S(2)}) async-start(s8[8388608]{0:T(1024)(128)(4,1)} %bitcast.52), calls=%async_computation.4 | async-start | bytes 8388608
  230.0 7.1 %slice-start.1 = ((s8[8388608]{0:T(1024)(128)(4,1)}), s8[4194304]{0:T(1024)(128)(4,1)S(1)}, s32[]{:S(2)}) async-start(s8[8388608]{0:T(1024)(128)(4,1)} %bitcast.52), calls=%async_computation.5 | async-start | bytes 8388608
  237.0 5.4 %copy-start.3 = (bf16[128,4096]{1,0:T(8,128)(2,1)}, bf16[128,4096]{1,0:T(8,128)(2,1)S(1)}, u32[]{:S(2)}) copy-start(bf16[128,4096]{1,0:T(8,128)(2,1)S(1)} %multiply_convert_fusion) | copy-start | bytes 3145732
  243.4 9.1 %collective-permute-start.4 = (bf16[128,7680]{1,0:T(8,128)(2,1)}, bf16[128,7680]{1,0:T(8,128)(2,1)S(1)}, u32[]{:S(2)}, u32[]{:S(2)}) collective-permute-start(bf16[128,7680]{1,0:T(8,128)(2,1)} %get-tuple-element.80), channel_id=1, source_target_pairs={{0,16},{16,0},{1,17},{17,1},{2,18},{18,2},{3,19},{19,3},{4,20},{20... | collective-permute-start | bytes 5898248 | tf_op jit(solution)/shard_map/ppermute | solution.py:29
  443.1 6.1 %copy-start.11 = (f32[128,1024]{1,0:T(8,128)S(1)}, f32[128,1024]{1,0:T(8,128)}, u32[]{:S(2)}) copy-start(f32[128,1024]{1,0:T(8,128)} %reduce_group.3) | copy-start | bytes 1572868
  443.1 6.1 %copy-start.17 = (f32[128,1024]{1,0:T(8,128)S(1)}, f32[128,1024]{1,0:T(8,128)}, u32[]{:S(2)}) copy-start(f32[128,1024]{1,0:T(8,128)} %get-tuple-element.41) | copy-start | bytes 1572868
  450.8 6.5 %copy-start.36 = (f32[128]{0:T(128)S(1)}, f32[128]{0:T(128)}, u32[]{:S(2)}) copy-start(f32[128]{0:T(128)} %copy-done.35) | copy-start | bytes 1540
  450.8 6.5 %copy-start.31 = (f32[128]{0:T(128)S(1)}, f32[128]{0:T(128)}, u32[]{:S(2)}) copy-start(f32[128]{0:T(128)} %copy-done.30) | copy-start | bytes 1540
  450.8 7.6 %collective-permute-start.5 = (bf16[128,2560]{1,0:T(8,128)(2,1)S(1)}, bf16[128,2560]{1,0:T(8,128)(2,1)S(1)}, u32[]{:S(2)}, u32[]{:S(2)}) collective-permute-start(bf16[128,2560]{1,0:T(8,128)(2,1)S(1)} %pad_maximum_fusion.6), channel_id=1, source_target_pairs={{0,16},{16,0},{1,17},{17,1},{2,18},{18,2},{3,19},{19,3},{4,20},{20... | collective-permute-start | bytes 1966088 | tf_op jit(solution)/shard_map/ppermute | solution.py:29
  521.7 3.0 copy-start.18
  525.8 3.2 copy-start.1
  (22 other events, 30.0 us)
Sparse Core Ops, SparseCore 0:
  15.5 90.9 all-gather.1
  260.8 212.8 reduce-scatter.1

commit v7 on v6

--- a/solution.py
+++ b/solution.py
@@ -25,10 +25,6 @@
     return lax.ppermute(value, axis, pairs)
 
 
-def swapped(value):
-    return lax.ppermute(value, "dp", [(0, 1), (1, 0)])
-
-
 def bucket_of(offset):
     past_edges = sum(((offset >= edge_pos).astype(jnp.int32) for edge_pos in bucket_edges))
     return jnp.where(offset < 16, offset, 16 + past_edges)
@@ -38,10 +34,6 @@
     return (
         values * lax.rsqrt(jnp.mean(values * values, axis=-1, keepdims=True) + eps_norm) * gain_vec
     )
-
-
-def gelu_exact(values):
-    return jax.nn.gelu(values, approximate=False)
 
 
 def book_of(positions, lengths):
@@ -833,31 +825,6 @@
         jax.ShapeDtypeStruct((rows, 128), jnp.float32),
     ]
     return reduce_group(parts, sources, collective_id, merge, pack, finish, out_shape)
-
-
-def weight_halves(pairs):
-    core = lax.axis_index("dp")
-    lefts, kept, sent = [], [], []
-    for left, right in pairs:
-        half = right.shape[1] // 2
-        lefts.append(left)
-        kept.append(lax.dynamic_slice_in_dim(right, core * half, half, 1))
-        sent.append(lax.dynamic_slice_in_dim(right, (1 - core) * half, half, 1))
-    other = swapped(jnp.concatenate(lefts + sent, axis=1))
-    partials, left_at, at = [], 0, sum(left.shape[1] for left in lefts)
-    for left, right in zip(lefts, kept):
-        other_left = other[:, left_at : left_at + left.shape[1]]
-        other_right = other[:, at : at + right.shape[1]]
-        left_at, at = left_at + left.shape[1], at + right.shape[1]
-        partials.append(
-            lax.dot_general(
-                jnp.concatenate([left, other_left], axis=0),
-                jnp.concatenate([right, other_right], axis=0),
-                contract_rows,
-                preferred_element_type=jnp.float32,
-            ).astype(jnp.bfloat16)
-        )
-    return jnp.concatenate(partials, axis=1)
 
 
 def scattered(halves):
@@ -1096,15 +1063,167 @@
     )(me, base, book_column, book_row, own, ratio, *([queries] * count), *([sent] * count))
 
 
-def finish_grads(parts, early, small, sources, collective_id):
-    rows, width = parts.shape[0] // sources, parts.shape[1]
+def feed_forward(normed_mid, cotangent, up_weight, down_weight):
+    rows, width = normed_mid.shape
+    hidden = up_weight.shape[1]
+    block = math.gcd(hidden, 1024)
+
+    def kernel(mid_ref, cot_ref, up_ref, down_ref, act_ref, d_up_ref, branch_ref, d_mid_ref):
+        first = pl.program_id(0) == 0
+        up = jnp.dot(mid_ref[...], up_ref[...], preferred_element_type=jnp.float32)
+        d_act = jnp.dot(cot_ref[...], down_ref[...], preferred_element_type=jnp.float32)
+        below = 0.5 * (1.0 + lax.erf(up * math.sqrt(0.5)))
+        density = jnp.exp(-0.5 * up * up) * (1.0 / math.sqrt(2.0 * math.pi))
+        act = (up * below).astype(jnp.bfloat16)
+        d_up = (d_act * (below + up * density)).astype(jnp.bfloat16)
+        act_ref[...] = act
+        d_up_ref[...] = d_up
+        branch = lax.dot_general(act, down_ref[...], contract_cols, preferred_element_type=jnp.float32)
+        d_mid = lax.dot_general(d_up, up_ref[...], contract_cols, preferred_element_type=jnp.float32)
+        branch_ref[...] = jnp.where(first, branch, branch_ref[...] + branch)
+        d_mid_ref[...] = jnp.where(first, d_mid, d_mid_ref[...] + d_mid)
+
+    whole = pl.BlockSpec((rows, width), lambda i: (0, 0))
+    weight = pl.BlockSpec((width, block), lambda i: (0, i))
+    middle = pl.BlockSpec((rows, block), lambda i: (0, i))
+    return pl.pallas_call(
+        kernel,
+        grid=(hidden // block,),
+        in_specs=[whole, whole, weight, weight],
+        out_specs=[middle, middle, whole, whole],
+        out_shape=[
+            jax.ShapeDtypeStruct((rows, hidden), jnp.bfloat16),
+            jax.ShapeDtypeStruct((rows, hidden), jnp.bfloat16),
+            jax.ShapeDtypeStruct((rows, width), jnp.float32),
+            jax.ShapeDtypeStruct((rows, width), jnp.float32),
+        ],
+        compiler_params=pltpu.CompilerParams(vmem_limit_bytes=VMEM_LIMIT),
+        cost_estimate=lasting(15),
+        name="feed_forward",
+    )(normed_mid, cotangent, up_weight, down_weight)
+
+
+def exchange_pairs(lefts, rights, other_lefts, other_right, send, recv):
+    core = lax.axis_index("dp")
+    copies, at = [], 0
+
+    def push(source, target):
+        i = len(copies)
+        copy = pltpu.make_async_remote_copy(
+            src_ref=source,
+            dst_ref=target,
+            send_sem=send.at[i],
+            recv_sem=recv.at[i],
+            device_id={"dp": 1 - core},
+            device_id_type=pl.DeviceIdType.MESH,
+        )
+        copy.start()
+        copies.append(copy)
+
+    for i, (left, right) in enumerate(zip(lefts, rights)):
+        half = right.shape[1] // 2
+        push(left, other_lefts.at[i])
+        there = pl.ds(pl.multiple_of((1 - core) * half, 128), half)
+        push(right.at[:, there], other_right.at[:, pl.ds(at, half)])
+        at += half
+    return copies
+
+
+def pair_products(lefts, rights, other_lefts, other_right, turned, store):
+    core = lax.axis_index("dp")
+    rows = lefts[0].shape[0]
+    at = 0
+    for i, (left, right) in enumerate(zip(lefts, rights)):
+        half = right.shape[1] // 2
+        turned[:, :rows] = left[...].T
+        turned[:, rows:] = other_lefts[i].T
+        block = math.gcd(half, 512)
+        for column in range(0, half, block):
+            kept = right[:, pl.ds(pl.multiple_of(core * half + column, 128), block)]
+            both = jnp.concatenate([kept, other_right[:, at + column : at + column + block]], axis=0)
+            store(
+                at + column,
+                jnp.dot(turned[...], both, preferred_element_type=jnp.float32).astype(jnp.bfloat16),
+            )
+        at += half
+
+
+def pair_scratch(lefts, rights):
+    rows, width = lefts[0].shape
+    count = len(lefts)
+    return [
+        pltpu.VMEM((count, rows, width), jnp.bfloat16),
+        pltpu.VMEM((rows, sum(right.shape[1] for right in rights) // 2), jnp.bfloat16),
+        pltpu.VMEM((width, 2 * rows), jnp.bfloat16),
+        pltpu.SemaphoreType.DMA((2 * count,)),
+        pltpu.SemaphoreType.DMA((2 * count,)),
+    ]
+
+
+def pair_grads(lefts, rights, collective_id):
+    count, width = len(lefts), lefts[0].shape[1]
+    total = sum(right.shape[1] for right in rights) // 2
+    block = math.gcd(*[right.shape[1] // 2 for right in rights], 512)
+
+    def kernel(*refs):
+        left_refs, right_refs, out_ref = refs[:count], refs[count : 2 * count], refs[2 * count]
+        other_lefts, other_right, turned, send, recv, staged, out_sem = refs[2 * count + 1 :]
+        barrier = pltpu.get_barrier_semaphore()
+        partner = {"dp": 1 - lax.axis_index("dp")}
+        pl.semaphore_signal(barrier, inc=1, device_id=partner, device_id_type=pl.DeviceIdType.MESH)
+        pl.semaphore_wait(barrier, 1)
+        copies = exchange_pairs(left_refs, right_refs, other_lefts, other_right, send, recv)
+        for copy in copies:
+            copy.wait_recv()
+        written = []
+
+        def store(column, value):
+            slot = len(written) % 2
+            if len(written) >= 2:
+                written[-2].wait()
+            staged[slot] = value
+            copy = pltpu.make_async_copy(
+                staged.at[slot], out_ref.at[:, pl.ds(column, block)], out_sem.at[slot]
+            )
+            copy.start()
+            written.append(copy)
+
+        pair_products(left_refs, right_refs, other_lefts, other_right, turned, store)
+        for copy in written[-2:]:
+            copy.wait()
+        for copy in copies:
+            copy.wait_send()
+
+    vmem = pl.BlockSpec(memory_space=pltpu.VMEM)
+    return pl.pallas_call(
+        kernel,
+        in_specs=[vmem] * (2 * count),
+        out_specs=pl.BlockSpec(memory_space=pl.ANY),
+        out_shape=jax.ShapeDtypeStruct((width, total), jnp.bfloat16),
+        scratch_shapes=pair_scratch(lefts, rights)
+        + [pltpu.VMEM((2, width, block), jnp.bfloat16), pltpu.SemaphoreType.DMA((2,))],
+        compiler_params=pltpu.CompilerParams(
+            collective_id=collective_id, has_side_effects=True, vmem_limit_bytes=VMEM_LIMIT
+        ),
+        cost_estimate=lasting(10),
+        name="pair_grads",
+    )(*lefts, *rights)
+
+
+def finish_grads(left, right, early, early_widths, small, sources, collective_id):
+    width, total = left.shape[1], right.shape[1] // 2
+    rows = width // sources
     mesh_type = pl.DeviceIdType.MESH
-    ref_shapes, sem_shapes = reduce_scratch(rows, width, parts.dtype, sources)
-
-    def kernel(parts_ref, early_ref, small_ref, late_out, early_out, small_out, *refs):
+    ref_shapes, sem_shapes = reduce_scratch(rows, total, jnp.bfloat16, sources)
+    pair_shapes = pair_scratch([left], [right])
+    outs = len(early_widths) + 2
+
+    def kernel(left_ref, right_ref, early_ref, small_ref, *refs):
+        (late_out, *early_outs, small_out), refs = refs[:outs], refs[outs:]
         steps_refs, refs = refs[: len(ref_shapes)], refs[len(ref_shapes) :]
         steps_sems, refs = refs[: len(sem_shapes)], refs[len(sem_shapes) :]
-        smalls, core_small, small_send, small_recv, core_send, core_recv = refs
+        (other_left, other_right, turned, pair_send, pair_recv), refs = refs[:5], refs[5:]
+        parts, late, both, smalls, core_small, small_send, small_recv, core_send, core_recv = refs
         me, core = lax.axis_index("mem"), lax.axis_index("dp")
         barrier = pltpu.get_barrier_semaphore()
         peers = [lax.rem(me + k, sources) for k in range(1, sources)]
@@ -1120,7 +1239,7 @@
             return total
 
         def pack(target, total):
-            target[...] = total.astype(parts.dtype)
+            target[...] = total.astype(jnp.bfloat16)
 
         def across_cores(source, target, i):
             copy = pltpu.make_async_remote_copy(
@@ -1134,6 +1253,7 @@
             copy.start()
             return copy
 
+        pair_copies = exchange_pairs([left_ref], [right_ref], other_left, other_right, pair_send, pair_recv)
         smalls[me] = small_ref[...]
         small_copies = [
             remote(small_ref, smalls.at[me], small_send.at[i], small_recv.at[me], peer)
@@ -1141,12 +1261,19 @@
         ]
         for copy in small_copies:
             copy.start()
-        early_copy = across_cores(early_ref, early_out.at[core], 0)
-        early_out[core] = early_ref[...]
-        final, still_open = reduce_steps(parts_ref, sources, steps_refs, steps_sems, merge, pack)
+        for copy in pair_copies:
+            copy.wait_recv()
+
+        def store(column, value):
+            parts[:, column : column + value.shape[1]] = value
+
+        pair_products([left_ref], [right_ref], other_left, other_right, turned, store)
+        early_copy = across_cores(early_ref, both.at[core], 0)
+        both[core] = early_ref[...]
+        final, still_open = reduce_steps(parts, sources, steps_refs, steps_sems, merge, pack)
         for here, blocks in final:
-            late_out[core, here] = merge(blocks).astype(parts.dtype)
-        late_copy = across_cores(late_out.at[core], late_out.at[core], 2)
+            late[core, here] = merge(blocks).astype(jnp.bfloat16)
+        late_copy = across_cores(late.at[core], late.at[core], 2)
         for peer in peers:
             remote(
                 smalls.at[peer], smalls.at[peer], small_send.at[0], small_recv.at[peer], peer
@@ -1156,25 +1283,38 @@
             group_small = group_small + smalls[i]
         core_small[0] = group_small
         small_copy = across_cores(core_small.at[0], core_small.at[1], 1)
-        for copy in (early_copy, late_copy, small_copy):
+        early_copy.wait()
+        at = 0
+        for out, size in zip(early_outs, early_widths):
+            half = size // 2
+            for c in (0, 1):
+                out[:, c * half : (c + 1) * half] = both[c, :, at : at + half].astype(jnp.float32)
+            at += half
+        for copy in (late_copy, small_copy):
             copy.wait()
+        for c in (0, 1):
+            late_out[:, c * total : (c + 1) * total] = late[c].astype(jnp.float32)
         small_out[...] = core_small[0] + core_small[1]
-        for copy in still_open + small_copies:
+        for copy in still_open + small_copies + pair_copies:
             copy.wait_send()
 
     vmem = pl.BlockSpec(memory_space=pltpu.VMEM)
     return pl.pallas_call(
         kernel,
-        in_specs=[vmem] * 3,
-        out_specs=[vmem] * 3,
-        out_shape=[
-            jax.ShapeDtypeStruct((2, rows, width), parts.dtype),
-            jax.ShapeDtypeStruct((2, *early.shape), early.dtype),
-            jax.ShapeDtypeStruct(small.shape, small.dtype),
-        ],
+        in_specs=[vmem] * 4,
+        out_specs=[vmem] * outs,
+        out_shape=[jax.ShapeDtypeStruct((rows, size), jnp.float32) for size in (2 * total, *early_widths)]
+        + [jax.ShapeDtypeStruct(small.shape, small.dtype)],
         scratch_shapes=ref_shapes
         + sem_shapes
-        + [pltpu.VMEM((sources, *small.shape), small.dtype), pltpu.VMEM((2, *small.shape), small.dtype)]
+        + pair_shapes
+        + [
+            pltpu.VMEM((width, total), jnp.bfloat16),
+            pltpu.VMEM((2, rows, total), jnp.bfloat16),
+            pltpu.VMEM((2, *early.shape), early.dtype),
+            pltpu.VMEM((sources, *small.shape), small.dtype),
+            pltpu.VMEM((2, *small.shape), small.dtype),
+        ]
         + [pltpu.SemaphoreType.DMA((sources,))] * 2
         + [pltpu.SemaphoreType.DMA((3,))] * 2,
         compiler_params=pltpu.CompilerParams(
@@ -1182,7 +1322,7 @@
         ),
         cost_estimate=lasting(45),
         name="finish_grads",
-    )(parts, early, small)
+    )(left, right, early, small)
 
 
 def on_device(
@@ -1281,23 +1421,17 @@
     residual = tokens_f + jnp.dot(mixed_heads, out_weight, preferred_element_type=jnp.float32)
     normed_mid_f, norm_mid_back = jax.vjp(normed, residual, ffn_gain)
     normed_mid = normed_mid_f.astype(jnp.bfloat16)
-    up_proj = jnp.dot(normed_mid, up_weight, preferred_element_type=jnp.float32)
-    activated_f, gelu_back = jax.vjp(gelu_exact, up_proj)
-    activated = activated_f.astype(jnp.bfloat16)
-    ffn_branch = lax.dot_general(
-        activated, down_weight, contract_cols, preferred_element_type=jnp.float32
-    )
+    activated, d_up, ffn_branch, d_mid = feed_forward(normed_mid, cotangent, up_weight, down_weight)
     block_out = (residual + ffn_branch).astype(jnp.bfloat16)
-    d_act = jnp.dot(cotangent, down_weight, preferred_element_type=jnp.float32)
-    d_up = gelu_back(d_act)[0].astype(jnp.bfloat16)
-    d_mid = lax.dot_general(d_up, up_weight, contract_cols, preferred_element_type=jnp.float32)
     d_resid_part, ffn_gain_part = norm_mid_back(d_mid)
     d_residual = cotangent.astype(jnp.float32) + d_resid_part
     d_branch = d_residual.astype(jnp.bfloat16)
     d_mixed = lax.dot_general(
         d_branch, out_weight, contract_cols, preferred_element_type=jnp.float32
     )
-    early_halves = weight_halves([(mixed_heads, d_branch), (normed_mid, d_up), (cotangent, activated)])
+    early_halves = pair_grads(
+        [mixed_heads, normed_mid, cotangent], [d_branch, d_up, activated], 5
+    )
     d_queries, diagonals, gate_products, sent_grads = local_queries(
         before_bias,
         own_book,
@@ -1363,21 +1497,24 @@
     )
     d_tokens_part, attn_gain_part = norm_in_back(d_in)
     tokens_grad = d_residual + d_tokens_part
-    late_halves = weight_halves([(normed_in, d_projected)])
-    late_halves, early_sums = lax.optimization_barrier((late_halves, early_sums))
     small = jnp.concatenate(
         [attn_gain_part, ffn_gain_part, bias_part.reshape(-1), gate_part], axis=0
     )
     small = jnp.pad(small, (0, -small.shape[0] % 1024)).reshape(-1, 128)
+    early_widths = [width, hidden, hidden]
     if groups == 16:
-        late_both, early_both, small = finish_grads(late_halves, early_sums, small, groups, 4)
+        qkv_grad, out_grad, up_grad, down_grad, small = finish_grads(
+            normed_in, d_projected, early_sums, early_widths, small, groups, 4
+        )
     else:
+        late_halves = pair_grads([normed_in], [d_projected], 6)
+        late_halves, early_sums = lax.optimization_barrier((late_halves, early_sums))
         late_both = lax.all_gather(scattered(late_halves), "dp", axis=0)
         early_both = lax.all_gather(early_sums, "dp", axis=0)
         small = lax.psum(small, ("dp", "mem"))
+        out_grad, up_grad, down_grad = whole_grads(early_both, early_widths)
+        qkv_grad = whole_grads(late_both, [3 * width])[0]
     small = small.reshape(-1)
-    out_grad, up_grad, down_grad = whole_grads(early_both, [width, hidden, hidden])
-    qkv_grad = whole_grads(late_both, [3 * width])[0]
     at_bias = 2 * width + heads * buckets
     return (
         block_out,

time: 547 us -> 538 us (0.984)
  matrix products: 39.1 us -> 10.2 us
  Pallas kernels: 382 us -> 402 us
  waiting for transfers between devices: 12.6 us -> 24.1 us
  other arithmetic: 44 us -> 36.7 us
    dot_general x8 -> x0, matrix products: 27.3 us -> none  [the longest x1 6.97 us: on_device(): lax.dot_general(activated, down_weight, contract_cols, preferred_element_...]
    pallas_call x1 -> x3, Pallas kernels: 44.5 us -> 71.3 us  [the longest x1 46 us: finish_grads(): pl.pallas_call(kernel, in_specs=[vmem] * 4, out_specs=[vmem] * outs, out_...]
    pallas_call x1, Pallas kernels: 56 us -> 38.3 us  [gather_rows(): pl.pallas_call(kernel, grid_spec=pltpu.PrefetchScalarGridSpec(num_scalar_...]
    pallas_call x2, Pallas kernels: 149 us -> 162 us  [reduce_group(): pl.pallas_call(kernel, in_specs=[pl.BlockSpec(memory_space=pltpu.VMEM)],...]
    reduce_scatter x1, waiting for transfers between devices: 12.6 us -> 24.1 us  [scattered(): return lax.psum_scatter(halves, 'mem', scatter_dimension=0, tiled=True)]
    concatenate x6 -> x0, other arithmetic: 8.52 us -> none  [the longest x1 4.74 us: weight_halves(): return jnp.concatenate(partials, axis=1)]
  transfers between devices with their start and end apart: 9 -> 7, of which waited for: 1 -> 1; matrix products, arithmetic and copies ran while one was open for 10% -> 8% of each run, Pallas kernels for 47% -> 42%
where the time goes in v7:
time: 538 us; the launch traced here: 528 us
  Pallas kernels  402 us (75%)
  other arithmetic  36.7 us (7%)
  waiting for transfers between devices  24.1 us (4%)
  starting transfers between devices  20 us (4%)
  local copies, waits for them, and re-layouts  19.9 us (4%)
  between operations  15 us (3%)
  matrix products  10.2 us (2%)
    pallas_call x2, Pallas kernels, reduce_group(): pl.pallas_call(kernel, in_specs=[pl.BlockSpec(memory_space=pltpu.VMEM)],...  162 us
    pallas_call x1, Pallas kernels, gather_group(): pl.pallas_call(kernel, in_specs=[pl.BlockSpec(memory_space=pl.ANY)], out_...  54.1 us
    pallas_call x1, Pallas kernels, finish_grads(): pl.pallas_call(kernel, in_specs=[vmem] * 4, out_specs=[vmem] * outs, out_...  46 us
    pallas_call x1, Pallas kernels, gather_rows(): pl.pallas_call(kernel, grid_spec=pltpu.PrefetchScalarGridSpec(num_scalar_...  38.3 us
    pallas_call x1, Pallas kernels, memory_backward(): pl.pallas_call(kernel, grid_spec=pltpu.PrefetchScalarGridSpec(num_scalar_...  27.5 us
    pallas_call x1, Pallas kernels, memory_forward(): pl.pallas_call(kernel, grid_spec=pltpu.PrefetchScalarGridSpec(num_scalar_...  26.4 us
    reduce_scatter x1, waiting for transfers between devices, scattered(): return lax.psum_scatter(halves, 'mem', scatter_dimension=0, tiled=True)  24.1 us
    sort x1, other arithmetic, place_requests(): lax.sort(((owner * entries + place).reshape(-1), slot_index.reshape(-1)),...  18.8 us
  transfers between devices with their start and end apart: 7, of which 1 were waited for; matrix products, arithmetic and copies ran while one was open for 8% of the time, Pallas kernels for 42%

profile of v7, /device:TPU:9, one launch (start us, length us, event | category | flops | bytes accessed | tf_op | source)
XLA Modules:
  0.0 527.8 jit_solution(7319829891089318590)
XLA Ops:
  7.2 1.2 fusion.6
  9.6 3.9 convolution_convert_fusion.own_ref
  16.9 18.8 %sort.23 = (s32[32768]{0:T(1024)S(1)}, s32[32768]{0:T(1024)S(1)}, s32[32768]{0:T(1024)}) sort(s32[32768]{0:T(1024)S(1)} %reshape.246, s32[32768]{0:T(1024)} %reshape.247, s32[32768]{0:T(1024)S(1)} %iota.53), dimensions={0}, to_apply=%region_0.0 | sort | flops 491520 | bytes 786432 | tf_op jit(solution)/shard_map/sort | solution.py:53
  37.6 2.8 make_lists.1
  40.4 6.7 %all-to-all-start = ((s32[16,24,128]{2,1,0:T(8,128)}), s32[16,24,128]{2,1,0:T(8,128)S(1)}, u32[]{:S(2)}, u32[]{:S(2)}) async-start(s32[16,24,128]{2,1,0:T(8,128)} %make_lists.1), calls=%async_computation | async-start | bytes 393216 | tf_op jit(solution)/shard_map/all_to_all | solution.py:1381
  47.9 3.1 collective-permute-start.3
  51.0 3.1 collective-permute-start.2
  54.1 4.0 collective-permute-start.1
  58.1 3.1 collective-permute-start
  61.5 1.2 subtract_multiply_fusion
  64.2 2.7 convert_reduce_fusion.1
  70.0 38.3 %gather_rows.1 = (bf16[49152,128]{1,0:T(8,128)(2,1)}, bf16[49152,128]{1,0:T(8,128)(2,1)}) custom-call(s32[49152]{0:T(1024)} %bitcast.30, s32[16]{0:T(128)} %slice_reduce_fusion.counts_ref, bf16[4096,1024]{1,0:T(8,128)(2,1)} %keys.1, bf16[4096,1024]{1,0:T(8,128)(2,1)} %values.1), custom_call_target="tpu_custom_call" | custom-call | bytes 126000000 | tf_op jit(solution)/shard_map/gather_rows/pallas_call | solution.py:138
  109.8 6.7 %local_forward.1 = (f32[128,1024]{1,0:T(8,128)}, f32[128,128]{1,0:T(8,128)}) custom-call(f32[8,768]{1,0:T(8,128)} %pad.17.base_ref, s32[128,128]{1,0:T(8,128)} %broadcast_in_dim.24.column_ref, s32[8,640]{1,0:T(8,128)} %broadcast_in_dim.26.row_ref, bf16[128,3072]{1,0:T(8,128)(2,1)} %copy-done.2, bf16[128,2048]{1,0:T(8,128)(2,1)} %collective-permute-done.refs_0_, ...), custom_call_target="tpu_custom_call" | custom-call | bytes 30000000 | tf_op jit(solution)/shard_map/local_forward/pallas_call | solution.py:907
  116.4 26.4 %memory_forward.1.parts_ref = bf16[2048,1152]{1,0:T(8,128)(2,1)} custom-call(s32[144]{0:T(256)} %reshape.249.bounds_ref, bf16[2048,1024]{1,0:T(8,128)(2,1)} %all-gather.2.cloned.1.call-done.q_ref.refs_0_.refs_1_.refs_2_.refs_3_.refs_4_, bf16[49152,128]{1,0:T(8,128)(2,1)} %get-tuple-element.38.k_ref, bf16[49152,128]{1,0:T(8,128)(2,1)} %get-tuple-element.39.v_ref, ...), custom_call_target="tpu_custom_call" | custom-call | bytes 75000000 | tf_op jit(solution)/shard_map/memory_forward/pallas_call | solution.py:276
  142.8 77.2 %reduce_group.2 = (f32[128,1024]{1,0:T(8,128)}, f32[128,128]{1,0:T(8,128)}) custom-call(bf16[2048,1152]{1,0:T(8,128)(2,1)} %memory_forward.1.parts_ref), custom_call_target="tpu_custom_call" | custom-call | bytes 165000000 | tf_op jit(solution)/shard_map/reduce_group/pallas_call | solution.py:749
  222.7 12.2 %feed_forward.1 = (bf16[128,4096]{1,0:T(8,128)(2,1)}, bf16[128,4096]{1,0:T(8,128)(2,1)}, f32[128,1024]{1,0:T(8,128)}, f32[128,1024]{1,0:T(8,128)}) custom-call(bf16[128,1024]{1,0:T(8,128)(2,1)} %multiply_convert_fusion.mid_ref.refs_1_, bf16[128,1024]{1,0:T(8,128)(2,1)} %refs_2_.1, bf16[1024,4096]{1,0:T(8,128)(2,1)} %up_ref.1, bf16[1024,4096]{1,0:T(8,128)(2,1)} %down_ref.1), custom_call_target="tpu_custom_call" | custom-call | bytes 45000000 | tf_op jit(solution)/shard_map/feed_forward/pallas_call | solution.py:1089
  234.9 1.2 multiply_reduce_fusion
  236.1 1.2 fusion.29.refs_3_
  237.3 1.7 fusion.30.mix_ref
  239.0 13.1 %pair_grads.1 = bf16[1024,4608]{1,0:T(8,128)(2,1)} custom-call(bf16[128,1024]{1,0:T(8,128)(2,1)} %copy-done.8, bf16[128,1024]{1,0:T(8,128)(2,1)} %multiply_convert_fusion.mid_ref.refs_1_, bf16[128,1024]{1,0:T(8,128)(2,1)} %refs_2_.1, bf16[128,1024]{1,0:T(8,128)(2,1)} %copy-done.9, bf16[128,4096]{1,0:T(8,128)(2,1)} %get-tuple-element.49.refs_4_, ...), custom_call_target="tpu_custom_call" | custom-call | bytes 30000000 | tf_op jit(solution)/shard_map/pair_grads/pallas_call | solution.py:1198
  252.1 7.0 %local_queries.1 = (f32[128,1024]{1,0:T(8,128)}, f32[8,768]{1,0:T(8,128)}, f32[8,128]{1,0:T(8,128)}, bf16[128,1152]{1,0:T(8,128)(2,1)}) custom-call(f32[8,768]{1,0:T(8,128)} %pad.17.base_ref, s32[128,128]{1,0:T(8,128)} %broadcast_in_dim.24.column_ref, s32[8,640]{1,0:T(8,128)} %broadcast_in_dim.26.row_ref, bf16[128,3072]{1,0:T(8,128)(2,1)} %copy-done.2, ...), custom_call_target="tpu_custom_call" | custom-call | bytes 45000000 | tf_op jit(solution)/shard_map/local_queries/pallas_call | solution.py:984
  260.2 54.1 %gather_group.1.g_ref.refs_5_.refs_6_.refs_7_.refs_8_.refs_9_ = bf16[2048,1152]{1,0:T(8,128)(2,1)} custom-call(bf16[128,1152]{1,0:T(8,128)(2,1)} %get-tuple-element.51.x_ref), custom_call_target="tpu_custom_call" | custom-call | bytes 150000000 | tf_op jit(solution)/shard_map/gather_group/pallas_call | solution.py:625
  314.3 27.5 %memory_backward.1.parts_ref = bf16[2048,1024]{1,0:T(8,128)(2,1)} custom-call(s32[144]{0:T(256)} %reshape.249.bounds_ref, bf16[2048,1024]{1,0:T(8,128)(2,1)} %all-gather.2.cloned.1.call-done.q_ref.refs_0_.refs_1_.refs_2_.refs_3_.refs_4_, bf16[2048,1152]{1,0:T(8,128)(2,1)} %gather_group.1.g_ref.refs_5_.refs_6_.refs_7_.refs_8_.refs_9_, ...), custom_call_target="tpu_custom_call" | custom-call | bytes 75000000 | tf_op jit(solution)/shard_map/memory_backward/pallas_call | solution.py:426
  341.9 84.3 %reduce_group.3 = f32[128,1024]{1,0:T(8,128)} custom-call(bf16[2048,1024]{1,0:T(8,128)(2,1)} %memory_backward.1.parts_ref), custom_call_target="tpu_custom_call" | custom-call | bytes 165000000 | tf_op jit(solution)/shard_map/reduce_group/pallas_call | solution.py:749
  426.9 6.3 %local_keys.1 = bf16[128,2048]{1,0:T(8,128)(2,1)} custom-call(s32[1]{0:T(128)} %bitcast.7.me_ref, f32[8,768]{1,0:T(8,128)} %pad.18.base_ref, s32[128,128]{1,0:T(8,128)} %broadcast_in_dim.24.column_ref, s32[8,640]{1,0:T(8,128)} %broadcast_in_dim.30.row_ref, bf16[128,3072]{1,0:T(8,128)(2,1)} %copy-done.2, f32[8]{0:T(128)} %get-tuple-element.66.ratio_ref, ...), custom_call_target="tpu_custom_call" | custom-call | bytes 45000000 | tf_op jit(solution)/shard_map/local_keys/pallas_call | solution.py:1048
  434.4 3.5 fusion.3
  440.6 24.1 %reduce-scatter.2.cloned.1.call-done.early_ref = bf16[64,4608]{1,0:T(8,128)(2,1)} async-done(((bf16[1024,4608]{1,0:T(8,128)(2,1)}), bf16[64,4608]{1,0:T(8,128)(2,1)}) %reduce-scatter.2.cloned.1.call-update) | async-done | bytes 589840 | tf_op jit(solution)/shard_map/reduce_scatter | solution.py:831
  464.7 46.0 %finish_grads.1 = (f32[64,3072]{1,0:T(8,128)}, f32[64,1024]{1,0:T(8,128)}, f32[64,4096]{1,0:T(8,128)}, f32[64,4096]{1,0:T(8,128)}, f32[24,128]{1,0:T(8,128)}) custom-call(bf16[128,1024]{1,0:T(8,128)(2,1)} %copy-done.7, bf16[128,3072]{1,0:T(8,128)(2,1)} %pad_maximum_fusion.right_ref, bf16[64,4608]{1,0:T(8,128)(2,1)} %reduce-scatter.2.cloned.1.call-done.early_ref, ...), custom_call_target="tpu_custom_call" | custom-call | bytes 135000000 | tf_op jit(solution)/shard_map/finish_grads/pallas_call | solution.py:1302
  511.5 1.3 slice_bitcast_fusion
  512.8 1.2 slice.52
  514.6 2.2 copy.37
  516.8 1.8 copy.38
  (127 shorter events, 25.0 us)
Async XLA Ops:
  7.2 214.1 %copy-start = (bf16[1024,1024]{1,0:T(8,128)(2,1)S(1)}, bf16[1024,1024]{1,0:T(8,128)(2,1)}, u32[]{:S(2)}) copy-start(bf16[1024,1024]{1,0:T(8,128)(2,1)} %param.19) | copy-start | bytes 6291460
  7.2 109.2 %all-gather.2.cloned.1.call-start = ((), (), s32[]{:S(2)}) async-start(), calls=%async_computation.2 | async-start | bytes 4456448 | tf_op jit(solution)/shard_map/all_gather | solution.py:1392
  9.6 3.9 copy-start.7
  9.6 4.8 copy-start.18
  9.6 4.8 copy-start.19
  13.5 33.6 %copy-start.2 = (bf16[128,3072]{1,0:T(8,128)(2,1)}, bf16[128,3072]{1,0:T(8,128)(2,1)S(1)}, u32[]{:S(2)}) copy-start(bf16[128,3072]{1,0:T(8,128)(2,1)S(1)} %convolution_convert_fusion.own_ref) | copy-start | bytes 2359300
  14.8 46.4 %copy-start.28 = (s32[1,3]{1,0:T(1,128)S(1)}, s32[1,3]{1,0:T(1,128)}, u32[]{:S(2)}) copy-start(s32[1,3]{1,0:T(1,128)} %param.27) | copy-start | bytes 40
  14.9 48.0 %copy-start.27 = (f32[8,32]{1,0:T(8,128)S(1)}, f32[8,32]{1,0:T(8,128)}, u32[]{:S(2)}) copy-start(f32[8,32]{1,0:T(8,128)} %param.20) | copy-start | bytes 3076
  40.4 23.8 %all-to-all-start = ((s32[16,24,128]{2,1,0:T(8,128)}), s32[16,24,128]{2,1,0:T(8,128)S(1)}, u32[]{:S(2)}, u32[]{:S(2)}) async-start(s32[16,24,128]{2,1,0:T(8,128)} %make_lists.1), calls=%async_computation | async-start | bytes 393216 | tf_op jit(solution)/shard_map/all_to_all | solution.py:1381
  47.1 417.6 %reduce-scatter.2.cloned.1.call-start = ((), (), s32[]{:S(2)}) async-start(), calls=%async_computation.3 | async-start | bytes 10027008 | tf_op jit(solution)/shard_map/reduce_scatter | solution.py:831
  47.9 60.4 %collective-permute-start.3 = (bf16[128,2048]{1,0:T(8,128)(2,1)}, bf16[128,2048]{1,0:T(8,128)(2,1)S(1)}, u32[]{:S(2)}, u32[]{:S(2)}) collective-permute-start(bf16[128,2048]{1,0:T(8,128)(2,1)} %slice.51), channel_id=1, source_target_pairs={{0,1},{1,2},{2,3},{3,4},{4,5},{5,6},{6,7},{7,8},{8,9},{9,10},{10,1... | collective-permute-start | bytes 1572872 | tf_op jit(solution)/shard_map/ppermute | solution.py:25
  51.0 57.3 %collective-permute-start.2 = (bf16[128,2048]{1,0:T(8,128)(2,1)}, bf16[128,2048]{1,0:T(8,128)(2,1)S(1)}, u32[]{:S(2)}, u32[]{:S(2)}) collective-permute-start(bf16[128,2048]{1,0:T(8,128)(2,1)} %slice.51), channel_id=1, source_target_pairs={{0,2},{1,3},{2,4},{3,5},{4,6},{5,7},{6,8},{7,9},{8,10},{9,11},{10,... | collective-permute-start | bytes 1572872 | tf_op jit(solution)/shard_map/ppermute | solution.py:25
  54.1 54.2 %collective-permute-start.1 = (bf16[128,2048]{1,0:T(8,128)(2,1)}, bf16[128,2048]{1,0:T(8,128)(2,1)}, u32[]{:S(2)}, u32[]{:S(2)}) collective-permute-start(bf16[128,2048]{1,0:T(8,128)(2,1)} %slice.51), channel_id=1, source_target_pairs={{0,3},{1,4},{2,5},{3,6},{4,7},{5,8},{6,9},{7,10},{8,11},{9,12},{10... | collective-permute-start | bytes 1572872 | tf_op jit(solution)/shard_map/ppermute | solution.py:25
  58.1 50.2 %collective-permute-start = (bf16[128,2048]{1,0:T(8,128)(2,1)}, bf16[128,2048]{1,0:T(8,128)(2,1)}, u32[]{:S(2)}, u32[]{:S(2)}) collective-permute-start(bf16[128,2048]{1,0:T(8,128)(2,1)} %slice.51), channel_id=1, source_target_pairs={{0,4},{1,5},{2,6},{3,7},{4,8},{5,9},{6,10},{7,11},{8,12},{9,13},{1... | collective-permute-start | bytes 1572872 | tf_op jit(solution)/shard_map/ppermute | solution.py:25
  62.7 45.6 %copy-start.22 = (f32[8]{0:T(128)}, f32[8]{0:T(128)S(1)}, u32[]{:S(2)}) copy-start(f32[8]{0:T(128)S(1)} %get-tuple-element.67.share_ref) | copy-start | bytes 100
  142.8 77.3 %copy-start.12 = (f32[128,1024]{1,0:T(8,128)S(1)}, f32[128,1024]{1,0:T(8,128)}, u32[]{:S(2)}) copy-start(f32[128,1024]{1,0:T(8,128)} %get-tuple-element.42.loc_ref) | copy-start | bytes 1572868
  142.8 78.4 %copy-start.6 = (bf16[128,1024]{1,0:T(8,128)(2,1)S(1)}, bf16[128,1024]{1,0:T(8,128)(2,1)}, u32[]{:S(2)}) copy-start(bf16[128,1024]{1,0:T(8,128)(2,1)} %param.16) | copy-start | bytes 786436
  221.3 13.6 %copy-start.8 = (bf16[128,1024]{1,0:T(8,128)(2,1)}, bf16[128,1024]{1,0:T(8,128)(2,1)S(1)}, u32[]{:S(2)}) copy-start(bf16[128,1024]{1,0:T(8,128)(2,1)S(1)} %add_convert_fusion.2.refs_0_) | copy-start | bytes 786436
  222.7 13.4 %copy-start.4 = (bf16[128,1024]{1,0:T(8,128)(2,1)S(1)}, bf16[128,1024]{1,0:T(8,128)(2,1)}, u32[]{:S(2)}) copy-start(bf16[128,1024]{1,0:T(8,128)(2,1)} %refs_2_.1) | copy-start | bytes 786436
  341.9 84.3 %copy-start.24 = (f32[8,128]{1,0:T(8,128)S(1)}, f32[8,128]{1,0:T(8,128)}, u32[]{:S(2)}) copy-start(f32[8,128]{1,0:T(8,128)} %get-tuple-element.54) | copy-start | bytes 12292
  341.9 92.4 %slice-start = ((s8[6291456]{0:T(1024)(128)(4,1)}), s8[2097152]{0:T(1024)(128)(4,1)S(1)}, s32[]{:S(2)}) async-start(s8[6291456]{0:T(1024)(128)(4,1)} %bitcast.28), calls=%async_computation.4 | async-start | bytes 4194304
  426.9 6.3 %copy-start.23 = (f32[8]{0:T(128)S(1)}, f32[8]{0:T(128)}, u32[]{:S(2)}) copy-start(f32[8]{0:T(128)} %copy-done.22) | copy-start | bytes 100
  426.9 6.3 %copy-start.11 = (f32[128,1024]{1,0:T(8,128)S(1)}, f32[128,1024]{1,0:T(8,128)}, u32[]{:S(2)}) copy-start(f32[128,1024]{1,0:T(8,128)} %reduce_group.3) | copy-start | bytes 1572868
  426.9 7.4 %slice-start.1 = ((s8[6291456]{0:T(1024)(128)(4,1)}), s8[4194304]{0:T(1024)(128)(4,1)S(1)}, s32[]{:S(2)}) async-start(s8[6291456]{0:T(1024)(128)(4,1)} %bitcast.28), calls=%async_computation.5 | async-start | bytes 8388608
  426.9 7.4 %copy-start.21 = (f32[1024]{0:T(1024)S(1)}, f32[1024]{0:T(1024)}, u32[]{:S(2)}) copy-start(f32[1024]{0:T(1024)} %param.17) | copy-start | bytes 12292
  434.4 4.2 copy-start.3
  434.4 4.1 copy-start.5
  434.4 4.1 copy-start.17
  437.9 1.8 copy-start.10
  510.7 7.9 %copy-start.16 = (f32[64,4096]{1,0:T(8,128)S(1)}, f32[64,4096]{1,0:T(8,128)}, u32[]{:S(2)}) copy-start(f32[64,4096]{1,0:T(8,128)} %get-tuple-element.93) | copy-start | bytes 3145732
  514.6 5.0 copy-start.15
  516.8 3.8 copy-start.1
  (6 other events, 8.4 us)
Sparse Core Ops, SparseCore 0:
  14.4 91.2 all-gather.1
  259.3 205.3 reduce-scatter.1
